TPU v7x, 32 devices: a whole 2x2x4 slice. The times are simulated.
32 devices in a mesh: dp: 16 (over z, y, core), mp: 2 (over x).
Axes of the slice: x: 2, y: 2, z: 4, core: 2. Of those that a mesh axis runs over, the one named last changes fastest.
Arguments:
- tokens: bfloat16 [16384, 768], P('dp'), may hold values from -6 to 6
- lengths: int32 [32], P('dp'), may hold values from 64 to 512, as said below
- weights: float32 [768, 13, 768], P('dp', None, 'mp')
- weight_m1: float32 [768, 13, 768], P('dp', None, 'mp')
- weight_m2: float32 [768, 13, 768], P('dp', None, 'mp')
- head_vecs: float32 [6, 768], P(None, 'mp')
- head_m1: float32 [6, 768], P(None, 'mp')
- head_m2: float32 [6, 768], P(None, 'mp')
- norm_vecs: float32 [6, 768], replicated
- norm_m1: float32 [6, 768], replicated
- norm_m2: float32 [6, 768], replicated
- cotangent: bfloat16 [16384, 768], P(('dp', 'mp')), may hold values from -6 to 6
Outputs:
- out_tokens: bfloat16 [16384, 768], P(('dp', 'mp'))
- grad_tokens: float32 [16384, 768], P(('dp', 'mp'))
- new_weights: float32 [768, 13, 768], P('dp', None, 'mp')
- new_weight_m1: float32 [768, 13, 768], P('dp', None, 'mp')
- new_weight_m2: float32 [768, 13, 768], P('dp', None, 'mp')
- new_head_vecs: float32 [6, 768], P(None, 'mp')
- new_head_m1: float32 [6, 768], P(None, 'mp')
- new_head_m2: float32 [6, 768], P(None, 'mp')
- new_norm_vecs: float32 [6, 768], replicated
- new_norm_m1: float32 [6, 768], replicated
- new_norm_m2: float32 [6, 768], replicated
Inputs may be any that keep to these rules, and one draw needn't show every extreme that they name: `lengths`: some sequence has 512 tokens in use in every draw.
All inputs are finite; a program needn't handle non-finite values.
Results may differ from a plain program's by a relative error of at most 0.015.
The roundings to bfloat16 on the way count: a program that leaves them out, or rounds other values in their place, can miss the bound.
Values may be sent and summed in bfloat16 or wider, within the bound.
No kernel may reach another device: no remote copies, remote signals or barrier semaphores. Data moves between devices by JAX's collectives and lax.ppermute only.
A program may use at most 192 MiB of HBM per device.

v0:
```python
import functools

import jax
import jax.numpy as jnp
from jax import lax
from jax.experimental import pallas as pl
from jax.experimental.pallas import tpu as pltpu
from jax.sharding import PartitionSpec as P

HEAD_FEATURES = 64
STEP = 5
EPS_NORM = 1e-05
EPS_ADAM = 1e-08
BETA_ONE = 0.5
BETA_TWO = 0.5
RATE_BIG = 0.03
RATE_SMALL = 0.2
DECAY = 0.01
MASKED = -1e30
SCALE = HEAD_FEATURES ** (-0.5)
ROW_BLOCK = 256
VMEM_MB = 56
UNROLL = 1
BF = jnp.bfloat16
F32 = jnp.float32

NN = (((1,), (0,)), ((), ()))
NT = (((1,), (1,)), ((), ()))
TN = (((0,), (0,)), ((), ()))


def mm(a, b, dims=NN):
    return lax.dot_general(a, b, dims, preferred_element_type=F32)


def whole(shape):
    return pl.BlockSpec(shape, lambda *_: (0,) * len(shape))


def held(shape):
    return pl.BlockSpec(shape, lambda *_: (0,) * len(shape), pipeline_mode=pl.Buffered(1))


def params(mebibytes):
    return pltpu.CompilerParams(vmem_limit_bytes=mebibytes * 1024 * 1024)


def cost(micros):
    return pl.CostEstimate(flops=int(micros * 1e9), bytes_accessed=0, transcendentals=0)


def relative_embedding(length, model_width):
    distance = (length - 1 - jnp.arange(2 * length)).astype(F32)
    freq_index = jnp.arange(model_width // 2).astype(F32)
    inverse = 1.0 / 10000.0 ** (2.0 * freq_index / model_width)
    angles = distance[:, None] * inverse[None, :]
    return jnp.concatenate([jnp.sin(angles), jnp.cos(angles)], axis=1)


def adam_update(param, grad_sum, moment_one, moment_two, rate):
    new_one = BETA_ONE * moment_one + (1.0 - BETA_ONE) * grad_sum
    new_two = BETA_TWO * moment_two + (1.0 - BETA_TWO) * grad_sum * grad_sum
    corrected_one = new_one / (1.0 - BETA_ONE**STEP)
    corrected_two = new_two / (1.0 - BETA_TWO**STEP)
    new_param = param - rate * (
        corrected_one / (jnp.sqrt(corrected_two) + EPS_ADAM) + DECAY * param
    )
    return (new_param, new_one, new_two)


def weight_spec(shape, which, each=None):
    if shape[1] != 2:
        return pl.BlockSpec((shape[0], each) + shape[2:], lambda b: (0, which(b), 0, 0))
    return pl.BlockSpec((each,) + shape[1:], lambda b: (which(b), 0, 0, 0))


def one_block(ref, index):
    if len(ref.shape) == 5:
        return ref.at[:, :, index]
    return ref.at[:, index] if ref.shape[0] > 8 else ref.at[index]


def ring_order(lines):
    order = []
    for turn, (mp, y) in enumerate(((0, 0), (0, 1), (1, 1), (1, 0))):
        for line in range(lines) if turn % 2 == 0 else reversed(range(lines)):
            order += [(mp, line * 4 + y * 2), (mp, line * 4 + y * 2 + 1)]
    return order


def full_matrix(w_ref):
    if len(w_ref.shape) == 3 and w_ref.shape[0] > 2:
        places = w_ref.shape[0]
        order = ring_order(places // 8)
        sides = [
            jnp.concatenate([w_ref[order.index((mp, dp))] for dp in range(places // 2)], axis=0)
            for mp in range(2)
        ]
        return jnp.concatenate(sides, axis=1)
    return jnp.concatenate([w_ref[0], w_ref[1]], axis=1)


RING = ((0, 0, 0), (0, 0, 1), (0, 1, 1), (0, 1, 0), (1, 1, 0), (1, 1, 1), (1, 0, 1), (1, 0, 0))


SQUARE = ((0, 0), (0, 1), (1, 1), (1, 0))


def layered(lines, rows):
    return rows % 16 == 0


def grad_shape(blocks, lines, rows, columns):
    if layered(lines, rows):
        return (len(RING), lines, blocks, rows, columns)
    return (blocks, 2, lines * 4 * rows, columns)


def grad_spec(shape):
    if len(shape) == 5:
        return pl.BlockSpec(shape[:2] + (None,) + shape[3:], lambda b: (0, 0, b, 0, 0))
    return pl.BlockSpec((None,) + shape[1:], lambda b: (b, 0, 0, 0))


def store_matrix(out_ref, value):
    half = value.shape[1] // 2
    low = value.astype(BF)
    if len(out_ref.shape) == 3:
        out_ref[0] = low[:, :half]
        out_ref[1] = low[:, half:]
        return
    places, lines, rows, _ = out_ref.shape
    for place, (mp, y, core) in enumerate(RING):
        for line in range(lines):
            top = (line * 4 + y * 2 + core) * rows
            out_ref[place, line] = low[top : top + rows, mp * half : (mp + 1) * half]


def store_split(keep_ref, send_ref, core, value):
    half = value.shape[1] // 2
    low = value.astype(BF)
    places, lines, rows, _ = keep_ref.shape
    for place, (mp, y) in enumerate(SQUARE):
        for line in range(lines):
            top = (line * 4 + y * 2) * rows
            columns = slice(mp * half, (mp + 1) * half)
            lower, upper = low[top : top + rows, columns], low[top + rows : top + 2 * rows, columns]
            keep_ref[place, line] = jnp.where(core == 0, lower, upper)
            send_ref[place, line] = jnp.where(core == 0, upper, lower)


def project_kernel(x_ref, w_ref, vec_ref, sine_ref, qc_ref, qp_ref, k_ref, v_ref, rel_ref):
    step = pl.program_id(0)

    @pl.when(step == 0)
    def _():
        q = mm(x_ref[...], full_matrix(w_ref))
        qc_ref[...] = (q + vec_ref[0:1]).astype(BF) * BF(SCALE)
        qp_ref[...] = (q + vec_ref[1:2]).astype(BF) * BF(SCALE)

    @pl.when(step == 1)
    def _():
        k_ref[...] = mm(x_ref[...], full_matrix(w_ref)).astype(BF)

    @pl.when(step == 2)
    def _():
        v_ref[...] = mm(x_ref[...], full_matrix(w_ref)).astype(BF)

    @pl.when(step == 3)
    def _():
        rel_ref[...] = mm(sine_ref[...], full_matrix(w_ref)).astype(BF)


def project(x, w, vecs, sine):
    length, width = x.shape
    rows = sine.shape[0]
    shapes = [(length, width)] * 4 + [(rows, width)]
    return pl.pallas_call(
        project_kernel,
        grid=(4,),
        in_specs=[
            whole(x.shape),
            weight_spec(w.shape, lambda b: b),
            whole(vecs.shape),
            whole(sine.shape),
        ],
        out_specs=[whole(s) for s in shapes],
        out_shape=[jax.ShapeDtypeStruct(s, BF) for s in shapes],
        compiler_params=params(VMEM_MB),
        cost_estimate=cost(9),
        name="project",
    )(x, w, vecs, sine)


PARTS = [
    (half, dx, dy, dc)
    for dc in (0, 1)
    for half, dx, dy in (
        (0, 0, 0), (1, 0, 0), (0, 1, 0), (1, 0, 1), (0, 0, 1), (1, 1, 0), (0, 1, 1), (1, 1, 1),
    )
]


def project_parts_kernel(
    cut, place_ref, x_ref, vec_ref, sine_ref, *refs,
):
    parts = refs[: len(PARTS)]
    outs = refs[len(PARTS) : len(PARTS) + 6]
    buffers = refs[len(PARTS) + 6 : len(PARTS) + 12]
    in_sem, out_sem = refs[-2:]
    w_ref = buffers[5]
    mp, line, y, core = (place_ref[i] for i in range(4))
    lines, _, rows, _ = parts[0].shape
    arriving = ([], [])
    for index, (half, dx, dy, dc) in enumerate(PARTS):
        for step in range(lines):
            at = lax.rem(line + lines - step, lines) * 4 + (y ^ dy) * 2 + (core ^ dc)
            start = pl.multiple_of(at * rows, rows)
            arriving[half].append(
                pltpu.make_async_copy(
                    parts[index].at[step],
                    w_ref.at[pl.ds(half * cut, cut), mp ^ dx, pl.ds(start, rows)],
                    in_sem.at[index * lines + step],
                )
            )
    for copy in arriving[0] + arriving[1]:
        copy.start()
    leaving = []

    def leave(source, target):
        copy = pltpu.make_async_copy(source, target, out_sem.at[len(leaving)])
        copy.start()
        leaving.append(copy)

    for copy in arriving[0]:
        copy.wait()
    leave(w_ref.at[0:2], outs[5].at[0:2])
    q = mm(x_ref[...], full_matrix(w_ref.at[0]))
    buffers[0][...] = (q + vec_ref[0:1]).astype(BF) * BF(SCALE)
    leave(buffers[0], outs[0])
    buffers[1][...] = (q + vec_ref[1:2]).astype(BF) * BF(SCALE)
    leave(buffers[1], outs[1])
    buffers[2][...] = mm(x_ref[...], full_matrix(w_ref.at[1])).astype(BF)
    leave(buffers[2], outs[2])
    for copy in arriving[1]:
        copy.wait()
    leave(w_ref.at[2:3], outs[5].at[2:3])
    buffers[4][...] = mm(sine_ref[...], full_matrix(w_ref.at[3])).astype(BF)
    leave(buffers[4], outs[4])
    buffers[3][...] = mm(x_ref[...], full_matrix(w_ref.at[2])).astype(BF)
    leave(buffers[3], outs[3])
    for copy in leaving:
        copy.wait()


def project_parts(x, parts, vecs, sine, place):
    if len(parts) == 1:
        return [*project(x, parts[0], vecs, sine), parts[0]]
    length, width = x.shape
    lines, cut, rows, columns = parts[0].shape
    shapes = [(length, width)] * 4 + [sine.shape]
    matrix = (2, lines * 4 * rows, columns)
    anywhere = pl.BlockSpec(memory_space=pl.ANY)
    return pl.pallas_call(
        functools.partial(project_parts_kernel, cut),
        grid=(1,),
        in_specs=[
            pl.BlockSpec(memory_space=pltpu.SMEM), held(x.shape), held(vecs.shape), held(sine.shape),
        ]
        + [anywhere] * len(parts),
        out_specs=[anywhere] * 6,
        out_shape=[jax.ShapeDtypeStruct(shape, BF) for shape in shapes + [(3,) + matrix]],
        scratch_shapes=[pltpu.VMEM(shape, BF) for shape in shapes + [(4,) + matrix]]
        + [pltpu.SemaphoreType.DMA((len(parts) * lines,)), pltpu.SemaphoreType.DMA((7,))],
        compiler_params=params(VMEM_MB),
        cost_estimate=cost(9),
        name="project",
    )(place, x, vecs, sine, *parts)


def lane_mask(which, shape):
    lanes = lax.broadcasted_iota(jnp.int32, shape, 1)
    return (lanes >= HEAD_FEATURES) if which else (lanes < HEAD_FEATURES)


def attend_kernel(len_ref, qc_ref, qp_ref, k_ref, v_ref, rel_ref, probs_ref, mixed_ref):
    length = qc_ref.shape[0]
    block = ROW_BLOCK
    pair = qc_ref.shape[1]
    valid = lax.broadcasted_iota(jnp.int32, (1, length), 1) < len_ref[0]
    k = k_ref[...]
    v = v_ref[...]
    zero = jnp.zeros((), BF)
    span = length + block
    jobs = [(top, head) for top in range(0, length, block) for head in range(2)]
    raw = []
    for top, head in jobs:
        rows = pl.ds(top, block)
        first = length - block - top
        mask = lane_mask(head, (block, pair))
        content = mm(jnp.where(mask, qc_ref[rows, :], zero), k, NT)
        place = mm(jnp.where(mask, qp_ref[rows, :], zero), rel_ref[first : first + span, :], NT)
        raw.append((content, place))
    for (top, head), (content, place) in zip(jobs, raw):
        place = pltpu.roll(place, span - (block - 1), 1, stride=1, stride_axis=0)
        scores = jnp.where(valid, content + place[:, :length], MASKED)
        top_score = jnp.max(scores, axis=1, keepdims=True)
        grown = jnp.exp(scores - top_score)
        probs = grown * (1.0 / jnp.sum(grown, axis=1, keepdims=True))
        probs_ref[head, pl.ds(top, block), :] = probs.astype(BF)
    for top in range(0, length, block):
        rows = pl.ds(top, block)
        lower, upper = mm(probs_ref[0, rows, :], v), mm(probs_ref[1, rows, :], v)
        mixed_ref[rows, :] = jnp.where(lane_mask(1, (block, pair)), upper, lower).astype(BF)


def attend(length_used, qc, qp, k, v, rel):
    length, width = qc.shape
    pair = 2 * HEAD_FEATURES
    heads = width // HEAD_FEATURES
    column = pl.BlockSpec((length, pair), lambda p: (0, p))
    return pl.pallas_call(
        attend_kernel,
        grid=(heads // 2,),
        in_specs=[pl.BlockSpec(memory_space=pltpu.SMEM)]
        + [column] * 4
        + [pl.BlockSpec((rel.shape[0], pair), lambda p: (0, p))],
        out_specs=[pl.BlockSpec((2, length, length), lambda p: (p, 0, 0)), column],
        out_shape=[
            jax.ShapeDtypeStruct((heads, length, length), BF),
            jax.ShapeDtypeStruct((length, width), BF),
        ],
        compiler_params=params(VMEM_MB),
        cost_estimate=cost(19),
        name="attend",
    )(length_used, qc, qp, k, v, rel)


def norm_parts(rows):
    mean = jnp.mean(rows, axis=1, keepdims=True)
    centred = rows - mean
    spread = jnp.mean(centred * centred, axis=1, keepdims=True)
    inverse = lax.rsqrt(spread + EPS_NORM)
    return centred * inverse, inverse


def norm_back(unit, inverse, scaled):
    return (
        scaled
        - jnp.mean(scaled, axis=1, keepdims=True)
        - unit * jnp.mean(scaled * unit, axis=1, keepdims=True)
    ) * inverse


def mlp_kernel(
    blocks, nv_ref, hb_ref, mixed_hbm, x_hbm, cot_hbm, w_hbm,
    out_hbm, unit_hbm, inv_ref, gh2_hbm, gw_hbm, ghid_hbm, sums_ref,
    mixed_ref, x_ref, cot_ref, w_ref, out_ref, unit_ref, gh2_ref, gw_ref,
    low_ref, turned_ref, act_ref, slope_ref, gffn_ref, gturned_ref, ghid_ref, total_ref, hsum_ref,
    in_sem, out_sem,
):
    copy_in = lambda source, target, at: pltpu.make_async_copy(source, target, in_sem.at[at])
    copy_w = lambda at: copy_in(stacked_block(w_hbm, at), w_ref.at[at], at)
    copy_mixed = copy_in(mixed_hbm, mixed_ref, 2 * blocks + 1)
    copy_x = copy_in(x_hbm, x_ref, 2 * blocks + 2)
    copy_cot = copy_in(cot_hbm, cot_ref, 2 * blocks + 3)
    copy_mixed.start()
    copy_w(2 * blocks).start()
    copy_x.start()
    for i in range(blocks):
        copy_w(i).start()
        copy_w(blocks + i).start()
    copy_cot.start()

    copy_out = lambda source, target, at: pltpu.make_async_copy(source, target, out_sem.at[at])
    copy_g = lambda at: copy_out(gw_ref.at[at], one_block(gw_hbm, at), at)
    copy_h = lambda at: copy_out(ghid_ref.at[at], ghid_hbm.at[at], 2 * blocks + at)
    copy_unit = copy_out(unit_ref, unit_hbm, 3 * blocks)
    copy_result = copy_out(out_ref, out_hbm, 3 * blocks + 1)
    copy_gh2 = copy_out(gh2_ref, gh2_hbm, 3 * blocks + 2)

    copy_mixed.wait()
    copy_w(2 * blocks).wait()
    attn = mm(mixed_ref[...], full_matrix(w_ref.at[2 * blocks]), NT)
    copy_x.wait()
    unit, inverse = norm_parts(x_ref[...].astype(F32) + attn + nv_ref[4:5])
    unit_ref[...] = unit
    copy_unit.start()
    inv_ref[...] = jnp.broadcast_to(inverse, inv_ref.shape)
    first = unit * nv_ref[0:1] + nv_ref[1:2]
    low_ref[...] = first.astype(BF)
    total_ref[...] = first + nv_ref[5:6]
    turned_ref[...] = low_ref[...].T

    def forward(i, carry):
        copy_w(i).wait()
        hidden = mm(low_ref[...], full_matrix(w_ref.at[i])) + hb_ref[i]
        bell = 0.5 * (1.0 + lax.erf(hidden * 0.7071067811865476))
        act_ref[i] = (hidden * bell).astype(BF)
        slope_ref[i] = (
            bell + hidden * (jnp.exp(hidden * hidden * -0.5) * 0.3989422804014327)
        ).astype(BF)
        copy_w(blocks + i).wait()
        total_ref[...] += mm(act_ref[i], full_matrix(w_ref.at[blocks + i]), NT)
        return carry

    lax.fori_loop(0, blocks, forward, 0, unroll=UNROLL)
    copy_cot.wait()
    unit, inverse = norm_parts(total_ref[...])
    out_ref[...] = (unit * nv_ref[2:3] + nv_ref[3:4]).astype(BF)
    copy_result.start()
    cot = cot_ref[...].astype(F32)
    gh2 = norm_back(unit, inverse, cot * nv_ref[2:3])
    gh2_ref[...] = gh2
    copy_gh2.start()
    gffn_ref[...] = gh2.astype(BF)
    for i, value in enumerate((cot * unit, cot, gh2)):
        sums_ref[i : i + 1] = jnp.sum(value, axis=0, keepdims=True)
    gturned_ref[...] = gffn_ref[...].T

    def backward(i, carry):
        gact = mm(gffn_ref[...], full_matrix(w_ref.at[blocks + i]))
        store_matrix(gw_ref.at[2 * i + 1], mm(gturned_ref[...], act_ref[i]))
        copy_g(2 * i + 1).start()
        ghid = (gact * slope_ref[i].astype(F32)).astype(BF)
        ghid_ref[i] = ghid
        copy_h(i).start()
        hsum_ref[i] = jnp.sum(ghid.astype(F32), axis=0, keepdims=True)
        store_matrix(gw_ref.at[2 * i], mm(turned_ref[...], ghid_ref[i]))
        copy_g(2 * i).start()
        return carry

    lax.fori_loop(0, blocks, backward, 0, unroll=UNROLL)
    for i in range(blocks):
        sums_ref[3 + i : 4 + i] = hsum_ref[i]
    copy_unit.wait()
    copy_result.wait()
    copy_gh2.wait()
    for i in range(blocks):
        copy_h(i).wait()
        copy_g(2 * i).wait()
        copy_g(2 * i + 1).wait()


def stacked_block(ref, at):
    return ref.at[at] if ref.shape[1] == 2 else ref.at[:, at]


def one_matrix(shape):
    return shape[1:] if shape[1] == 2 else shape[:1] + shape[2:]


def mlp(mixed, w_feed, x, nv, hb, cot, lines, rows):
    length, width = x.shape
    blocks = hb.shape[0]
    token = lambda d, *lead: jax.ShapeDtypeStruct((*lead, length, width), d)
    full = grad_shape(2 * blocks, lines, rows, width // 2)
    one_g = full[:2] + full[3:] if len(full) == 5 else full[1:]
    buffer = lambda d, *lead: pltpu.VMEM((*lead, length, width), d)
    anywhere = pl.BlockSpec(memory_space=pl.ANY)
    side = pltpu.VMEM((width, length), BF)
    return pl.pallas_call(
        functools.partial(mlp_kernel, blocks),
        grid=(1,),
        in_specs=[held(nv.shape), held(hb.shape)] + [anywhere] * 4,
        out_specs=[
            anywhere, anywhere, whole((length, 128)), anywhere, anywhere, anywhere,
            whole((3 + blocks, width)),
        ],
        out_shape=[
            token(BF), token(F32), jax.ShapeDtypeStruct((length, 128), F32), token(F32),
            jax.ShapeDtypeStruct(full, BF), token(BF, blocks),
            jax.ShapeDtypeStruct((3 + blocks, width), F32),
        ],
        scratch_shapes=[
            buffer(BF), buffer(BF), buffer(BF),
            pltpu.VMEM((2 * blocks + 1, *one_matrix(w_feed.shape)), BF),
            buffer(BF), buffer(F32), buffer(F32), pltpu.VMEM((2 * blocks, *one_g), BF),
            buffer(BF), side, buffer(BF, blocks), buffer(BF, blocks), buffer(BF), side,
            buffer(BF, blocks), buffer(F32), pltpu.VMEM((blocks, 1, width), F32),
            pltpu.SemaphoreType.DMA((2 * blocks + 4,)), pltpu.SemaphoreType.DMA((3 * blocks + 3,)),
        ],
        compiler_params=params(VMEM_MB),
        cost_estimate=cost(23),
        name="mlp",
    )(nv, hb, mixed, x, cot, w_feed)


def norm_down_kernel(
    blocks, nv_ref, inv_ref, unit_hbm, gh2_hbm, ghid_hbm, w_hbm,
    gh1_ref, gattn_ref, gmixed_ref, sums_ref,
    unit_ref, total_ref, ghid_ref, w_ref, sem,
):
    copy_in = lambda source, target, at: pltpu.make_async_copy(source, target, sem.at[at])
    copy_h = lambda i: copy_in(ghid_hbm.at[i], ghid_ref.at[i], i)
    copy_w = lambda i: copy_in(stacked_block(w_hbm, i), w_ref.at[i], blocks + i)
    copy_gh2 = copy_in(gh2_hbm, total_ref, 2 * blocks)
    copy_unit = copy_in(unit_hbm, unit_ref, 2 * blocks + 1)
    copy_last = copy_in(stacked_block(w_hbm, 2 * blocks), w_ref.at[blocks], 2 * blocks + 2)
    copy_gh2.start()
    for i in range(blocks):
        copy_h(i).start()
        copy_w(i).start()
    copy_unit.start()
    copy_last.start()
    copy_gh2.wait()

    def add(i, carry):
        copy_h(i).wait()
        copy_w(i).wait()
        total_ref[...] += mm(ghid_ref[i], full_matrix(w_ref.at[i]), NT)
        return carry

    lax.fori_loop(0, blocks, add, 0)
    copy_unit.wait()
    gfirst = total_ref[...]
    unit = unit_ref[...]
    gh1 = norm_back(unit, inv_ref[:, 0:1], gfirst * nv_ref[0:1])
    gh1_ref[...] = gh1
    gattn_ref[...] = gh1.astype(BF)
    copy_last.wait()
    gmixed_ref[...] = mm(gattn_ref[...], full_matrix(w_ref.at[blocks])).astype(BF)
    for i, value in enumerate((gfirst * unit, gfirst, gh1)):
        sums_ref[i : i + 1] = jnp.sum(value, axis=0, keepdims=True)


def norm_down(gh2, ghid, unit, inv, nv, w_feed):
    length, width = gh2.shape
    blocks = ghid.shape[0]
    one = whole((length, width))
    token = lambda d: jax.ShapeDtypeStruct((length, width), d)
    buffer = lambda d, *lead: pltpu.VMEM((*lead, length, width), d)
    return pl.pallas_call(
        functools.partial(norm_down_kernel, blocks),
        grid=(1,),
        in_specs=[held(nv.shape), held(inv.shape)] + [pl.BlockSpec(memory_space=pl.ANY)] * 4,
        out_specs=[one, one, one, whole((3, width))],
        out_shape=[token(F32), token(BF), token(BF), jax.ShapeDtypeStruct((3, width), F32)],
        scratch_shapes=[
            buffer(F32), buffer(F32), buffer(BF, blocks),
            pltpu.VMEM((blocks + 1, *one_matrix(w_feed.shape)), BF),
            pltpu.SemaphoreType.DMA((2 * blocks + 3,)),
        ],
        compiler_params=params(VMEM_MB),
        cost_estimate=cost(8),
        name="norm_down",
    )(nv, inv, unit, gh2, ghid, w_feed)


def attend_back_kernel(
    probs_ref, gm_ref, qc_ref, qp_ref, k_ref, v_ref, rel_ref,
    gq_ref, gk_ref, gv_ref, grel_ref, sums_ref,
    rel_acc,
):
    length, pair = gm_ref.shape
    block = ROW_BLOCK
    span = length + block
    zero = jnp.zeros((), BF)
    flip = (
        lax.broadcasted_iota(jnp.int32, (block, block), 0)
        + lax.broadcasted_iota(jnp.int32, (block, block), 1)
        == block - 1
    ).astype(F32).astype(BF)
    k = k_ref[...]
    v = v_ref[...]
    tops = range(0, length, block)
    jobs = [(top, head) for top in tops for head in range(2)]
    pick = lambda ref, top, head: jnp.where(
        lane_mask(head, (block, pair)), ref[pl.ds(top, block), :], zero
    )
    band = lambda top: pl.ds(length - block - top, span)
    gprobs = [mm(pick(gm_ref, top, head), v, NT) for top, head in jobs]
    turned_qp = {top: mm(flip, qp_ref[pl.ds(top, block), :]).astype(BF) for top in tops}
    gsums = []
    for (top, head), gprob in zip(jobs, gprobs):
        probs = probs_ref[head, pl.ds(top, block), :].astype(F32)
        product = probs * gprob
        inner = jnp.sum(product, axis=1, keepdims=True)
        gsums.append((product - probs * inner).astype(BF))
    wides = []
    for gsum in gsums:
        wide = jnp.concatenate([mm(flip, gsum), jnp.zeros((block, block), F32)], axis=1)
        wides.append(pltpu.roll(wide, 0, 1, stride=1, stride_axis=0).astype(BF))
    gk = gv = None
    gqc, gqp = {}, {}
    for (top, head), gsum in zip(jobs, gsums):
        tall = lane_mask(head, (length, pair))
        a = mm(gsum, jnp.where(tall, k, zero))
        gqc[top] = a if head == 0 else gqc[top] + a
        b = mm(gsum, pick(qc_ref, top, head), TN)
        c = mm(probs_ref[head, pl.ds(top, block), :], pick(gm_ref, top, head), TN)
        gk = b if gk is None else gk + b
        gv = c if gv is None else gv + c
    rel_acc[...] = jnp.zeros_like(rel_acc)
    for (top, head), wide in zip(jobs, wides):
        rel = jnp.where(lane_mask(head, (span, pair)), rel_ref[band(top), :], zero)
        d = mm(wide, rel)
        gqp[top] = d if head == 0 else gqp[top] + d
        mask = lane_mask(head, (block, pair))
        rel_acc[band(top), :] += mm(wide, jnp.where(mask, turned_qp[top], zero), TN)
    sum_c = sum_p = None
    for top in tops:
        c, p = gqc[top] * SCALE, gqp[top] * SCALE
        high = p.astype(BF)
        rest = (p - high.astype(F32)).astype(BF)
        straight = mm(flip, high) + mm(flip, rest)
        gq_ref[pl.ds(top, block), :] = (c + straight).astype(BF)
        e = jnp.sum(c, axis=0, keepdims=True)
        f = jnp.sum(p, axis=0, keepdims=True)
        sum_c = e if sum_c is None else sum_c + e
        sum_p = f if sum_p is None else sum_p + f
    gk_ref[...] = gk.astype(BF)
    gv_ref[...] = gv.astype(BF)
    grel_ref[...] = rel_acc[...].astype(BF)
    sums_ref[0:1] = sum_c
    sums_ref[1:2] = sum_p


def attend_back(probs, gm, qc, qp, k, v, rel):
    length, width = qc.shape
    pair = 2 * HEAD_FEATURES
    heads = width // HEAD_FEATURES
    column = pl.BlockSpec((length, pair), lambda p: (0, p))
    tall = pl.BlockSpec((rel.shape[0], pair), lambda p: (0, p))
    token = jax.ShapeDtypeStruct((length, width), BF)
    return pl.pallas_call(
        attend_back_kernel,
        grid=(heads // 2,),
        in_specs=[pl.BlockSpec((2, length, length), lambda p: (p, 0, 0))] + [column] * 5 + [tall],
        out_specs=[column, column, column, tall, pl.BlockSpec((2, pair), lambda p: (0, p))],
        out_shape=[
            token, token, token,
            jax.ShapeDtypeStruct(rel.shape, BF),
            jax.ShapeDtypeStruct((2, width), F32),
        ],
        scratch_shapes=[pltpu.VMEM((rel.shape[0], pair), F32)],
        compiler_params=params(VMEM_MB),
        cost_estimate=cost(28),
        name="attend_back",
    )(probs, gm, qc, qp, k, v, rel)


def project_back_kernel(
    core_ref, x_ref, gq_ref, gk_ref, gv_ref, grel_ref, sine_ref, gattn_ref, mixed_ref, *refs,
):
    *gw_refs, turned_ref = refs
    step = pl.program_id(0)

    def store(value):
        if len(gw_refs) == 2:
            store_split(*gw_refs, core_ref[0], value)
        else:
            store_matrix(gw_refs[0], value)

    @pl.when(step == 0)
    def _():
        turned_ref[...] = x_ref[...].T

    for which, g_ref in enumerate((gq_ref, gk_ref, gv_ref)):

        @pl.when(step == which)
        def _():
            store(mm(turned_ref[...], g_ref[...]))

    @pl.when(step == 3)
    def _():
        store(mm(sine_ref[...], grel_ref[...], TN))

    @pl.when(step == 4)
    def _():
        store(mm(gattn_ref[...], mixed_ref[...], TN))


def project_back(core, x, gq, gk, gv, grel, sine, gattn, mixed, lines, rows):
    length, width = x.shape
    one = held((length, width))
    if layered(lines, rows):
        shapes = [(len(SQUARE), lines, 5, rows, width // 2)] * 2
    else:
        shapes = [grad_shape(5, lines, rows, width // 2)]
    return pl.pallas_call(
        project_back_kernel,
        grid=(5,),
        in_specs=[
            pl.BlockSpec(memory_space=pltpu.SMEM),
            one, one, one, one, held(grel.shape), held(sine.shape), one, one,
        ],
        out_specs=[grad_spec(shape) for shape in shapes],
        out_shape=[jax.ShapeDtypeStruct(shape, BF) for shape in shapes],
        scratch_shapes=[pltpu.VMEM((width, length), BF)],
        compiler_params=params(VMEM_MB),
        cost_estimate=cost(9),
        name="project_back",
    )(core, x, gq, gk, gv, grel, sine, gattn, mixed)


def token_grad_kernel(gq_ref, gk_ref, gv_ref, w_ref, gh1_ref, gtok_ref):
    total = gh1_ref[...]
    for i, g_ref in enumerate((gq_ref, gk_ref, gv_ref)):
        total += mm(g_ref[...], full_matrix(w_ref.at[i]), NT)
    gtok_ref[...] = total


def token_grad(gq, gk, gv, w, gh1):
    one = whole(gq.shape)
    return pl.pallas_call(
        token_grad_kernel,
        grid=(1,),
        in_specs=[one, one, one, whole((3,) + w.shape[1:]), one],
        out_specs=one,
        out_shape=jax.ShapeDtypeStruct(gq.shape, F32),
        compiler_params=params(VMEM_MB),
        cost_estimate=cost(6),
        name="token_grad",
    )(gq, gk, gv, w, gh1)


def swap_x(value):
    return lax.ppermute(value, "mp", [(0, 1), (1, 0)])


def swap_dp(value, bit):
    return lax.ppermute(value, "dp", [(d, d ^ bit) for d in range(lax.axis_size("dp"))])


def shift_line(value, step):
    dp = lax.axis_size("dp")
    return lax.ppermute(value, "dp", [(d, (d + 4 * step) % dp) for d in range(dp)])


def gather_matrices(shard):
    dp = lax.axis_size("dp")
    if shard.shape[1] % 16 == 0:
        order = [mp * dp + index for mp, index in ring_order(dp // 4)]
        return lax.all_gather(
            shard, ("mp", "dp"), axis=0, axis_index_groups=[order], tiled=False
        )
    pieces = lax.all_gather(shard, ("mp", "dp"), axis=0, tiled=False)
    return whole_matrices(pieces.reshape((2, dp) + shard.shape))


def whole_matrices(pieces):
    mp, dp, blocks, rows, columns = pieces.shape
    return pieces.transpose(2, 0, 1, 3, 4).reshape(blocks, mp, dp * rows, columns)


def gather_lines(shard, others):
    lines = lax.axis_size("dp") // 4
    if lines != 4 or shard.shape[1] % 16 != 0:
        return shard, others
    near = [shard] + [shift_line(shard, step) for step in range(1, lines)]
    near, others = lax.optimization_barrier((near, others))
    return jnp.stack(near), others


def gather_stepwise(near, shard):
    dp = lax.axis_size("dp")
    blocks, rows, columns = shard.shape
    lines = dp // 4
    if lines != 4 or rows % 16 != 0:
        pieces = lax.all_gather(shard, ("mp", "dp"), axis=0, tiled=False)
        return (whole_matrices(pieces.reshape((2, dp) + shard.shape)),)
    cut = blocks // 2
    one, two = near[:, :cut], near[:, cut:]
    one_x = swap_x(one)
    two_y = swap_dp(two, 2)
    one_y = swap_dp(one, 2)
    two_x = swap_x(two)
    one_xy = swap_dp(one_x, 2)
    two_xy = swap_x(two_y)
    lane = [one, two, one_x, two_y, one_y, two_x, one_xy, two_xy]
    return tuple(lane + [swap_dp(part, 1) for part in lane])


def own_place():
    index = lax.axis_index("dp")
    place = jnp.stack([lax.axis_index("mp"), index // 4, (index // 2) % 2, index % 2])
    return place.astype(jnp.int32)


def plane_groups(dp):
    return [
        [mp * dp + line * 4 + y * 2 + core for mp, y, core in RING] for line in range(dp // 4)
    ]


def line_groups(dp):
    return [
        [mp * dp + line * 4 + low for line in range(dp // 4)] for mp in range(2) for low in range(4)
    ]


def scatter_plane(grads):
    dp = lax.axis_size("dp")
    if grads.ndim == 4:
        blocks, _, all_rows, columns = grads.shape
        grads = grads.reshape(blocks, 2, dp // 4, 2, 2, all_rows // dp, columns)
        grads = jnp.stack([grads[:, mp, :, y, core] for mp, y, core in RING])
        grads = grads.transpose(0, 2, 1, 3, 4)
    return lax.psum_scatter(
        grads, ("mp", "dp"), scatter_dimension=0, axis_index_groups=plane_groups(dp), tiled=False
    )


def scatter_square(keep, send, before):
    dp = lax.axis_size("dp")
    grads = (keep.astype(F32) + swap_dp(send, 1).astype(F32)).astype(BF)
    grads, before = lax.optimization_barrier((grads, before))
    groups = [
        [mp * dp + line * 4 + y * 2 + core for mp, y in SQUARE]
        for line in range(dp // 4)
        for core in range(2)
    ]
    part = lax.psum_scatter(
        grads, ("mp", "dp"), scatter_dimension=0, axis_index_groups=groups, tiled=False
    )
    return part, before


def line_pieces(part):
    dp = lax.axis_size("dp")
    lines = dp // 4
    if lines != 4:
        return [part]
    line = lax.axis_index("dp") // 4
    return [
        lax.dynamic_index_in_dim(part, (line + step) % lines, 0, keepdims=False)
        for step in range(lines)
    ]


def trade_pieces(pieces):
    dp = lax.axis_size("dp")
    if len(pieces) == 1:
        return [
            lax.psum_scatter(
                pieces[0], ("mp", "dp"), scatter_dimension=0, axis_index_groups=line_groups(dp),
                tiled=False,
            )
        ]
    return [pieces[0]] + [shift_line(pieces[step], step) for step in range(1, len(pieces))]


def sum_plane(value, meanwhile):
    value = value + swap_dp(value, 1)
    value = value + swap_x(value)
    value, *meanwhile = lax.optimization_barrier((value, *meanwhile))
    return value + swap_dp(value, 2), meanwhile


def sum_line(value):
    lines = lax.axis_size("dp") // 4
    if lines != 4:
        return lax.psum(value, ("dp",), axis_index_groups=line_only(lines))
    total = value
    for piece in [shift_line(value, step) for step in range(1, lines)]:
        total = total + piece
    return total


def line_only(lines):
    return [[line * 4 + low for line in range(lines)] for low in range(4)]


def adam_kernel(order, count, *refs):
    pieces = refs[:count]
    p_ref, one_ref, two_ref = refs[count : count + 3]
    outs = refs[-3:]
    for block, at in enumerate(order):
        grad = pieces[0][block].astype(F32)
        for piece in pieces[1:]:
            grad = grad + piece[block].astype(F32)
        results = adam_update(p_ref[at], grad, one_ref[at], two_ref[at], RATE_BIG)
        for out, result in zip(outs, results):
            out[at] = result


def adam_blocks(pieces, order, param, one, two, done):
    blocks, rows, columns = pieces[0].shape
    part = whole((blocks, rows, columns) if done else param.shape)
    shape = jax.ShapeDtypeStruct(param.shape, F32)
    count = len(pieces)
    return pl.pallas_call(
        functools.partial(adam_kernel, order, count),
        grid=(1,),
        in_specs=[whole(pieces[0].shape)] * count
        + [part] * 3
        + [pl.BlockSpec(memory_space=pl.ANY)] * len(done),
        out_specs=[part] * 3,
        out_shape=[shape] * 3,
        input_output_aliases={count + 3 + i: i for i in range(len(done))},
        compiler_params=params(VMEM_MB),
        cost_estimate=cost(blocks // 2),
        name="adam",
    )(*pieces, param, one, two, *done)


def per_device(
    tokens,
    lengths,
    weights,
    weight_m1,
    weight_m2,
    head_vecs,
    head_m1,
    head_m2,
    norm_vecs,
    norm_m1,
    norm_m2,
    cotangent,
):
    mp_index = lax.axis_index("mp")
    seq_len = cotangent.shape[0]
    weight_rows = weights.shape[0]
    local_width = weights.shape[2]
    model_width = tokens.shape[1]
    lines = lax.axis_size("dp") // 4
    x = lax.dynamic_slice_in_dim(tokens, mp_index * seq_len, seq_len, 0)
    used = lax.dynamic_slice_in_dim(lengths, mp_index, 1, 0)
    sine = relative_embedding(seq_len, model_width).astype(BF)
    shard = weights.transpose(1, 0, 2)
    shard_low = shard.astype(BF)
    heads_all = lax.all_gather(head_vecs, "mp", axis=1, tiled=True)
    w_feed = gather_matrices(jnp.concatenate([shard_low[5:13], shard_low[4:5]]))
    near, (x, sine, heads_all) = gather_lines(shard_low[0:4], (x, sine, heads_all))
    parts = gather_stepwise(near, shard_low[0:4])

    qc, qp, k, v, rel, w = project_parts(x, parts, heads_all[0:2], sine, own_place())
    probs, mixed = attend(used, qc, qp, k, v, rel)
    hb = heads_all[2:6].reshape(4, 1, model_width)
    out, unit, inv, gh2, gw_feed, ghid, sums2 = mlp(
        mixed, w_feed, x, norm_vecs, hb, cotangent, lines, weight_rows
    )
    part_feed = scatter_plane(gw_feed)
    gh1, gattn, gmixed, sums1 = norm_down(gh2, ghid, unit, inv, norm_vecs, w_feed)
    gq, gk, gv, grel, sums_q = attend_back(probs, gmixed, qc, qp, k, v, rel)
    small = sum_line(jnp.concatenate([sums2, sums1, sums_q], axis=0))
    place = own_place()
    gproj = project_back(
        place[3:4], x, gq, gk, gv, grel, sine, gattn, mixed, lines, weight_rows
    )
    *gproj, small = lax.optimization_barrier((*gproj, small))
    if len(gproj) == 2:
        part_proj, part_feed = scatter_square(*gproj, part_feed)
    else:
        gproj, part_feed = lax.optimization_barrier((gproj[0], part_feed))
        part_proj = scatter_plane(gproj)

    pieces_feed = line_pieces(part_feed)
    *pieces_feed, gq = lax.optimization_barrier((*pieces_feed, gq))
    grad_tokens = token_grad(gq, gk, gv, w, gh1)
    pieces_feed = trade_pieces(pieces_feed)
    small, grad_tokens = lax.optimization_barrier((small, grad_tokens))
    small, pieces_feed = sum_plane(small, pieces_feed)
    norm_grad = jnp.concatenate([small[7:9], small[0:2], small[9:10], small[2:3]], axis=0)
    head_grad = jnp.concatenate([small[10:12], small[3:7]], axis=0)
    head_grad = lax.dynamic_slice_in_dim(head_grad, mp_index * local_width, local_width, 1)
    state = (shard, weight_m1.transpose(1, 0, 2), weight_m2.transpose(1, 0, 2))
    done = adam_blocks(pieces_feed, (5, 9, 6, 10, 7, 11, 8, 12), *state, ())
    small, norm_grad, done, part_proj = lax.optimization_barrier((small, norm_grad, done, part_proj))
    pieces_proj = trade_pieces(line_pieces(part_proj))
    new_big = adam_blocks(pieces_proj, tuple(range(5)), *state, done)
    new_weights, new_weight_m1, new_weight_m2 = [a.transpose(1, 0, 2) for a in new_big]
    new_head, new_head_m1, new_head_m2 = adam_update(
        head_vecs, head_grad, head_m1, head_m2, RATE_SMALL
    )
    new_norm, new_norm_m1, new_norm_m2 = adam_update(
        norm_vecs, norm_grad, norm_m1, norm_m2, RATE_SMALL
    )
    return (
        out,
        grad_tokens,
        new_weights,
        new_weight_m1,
        new_weight_m2,
        new_head,
        new_head_m1,
        new_head_m2,
        new_norm,
        new_norm_m1,
        new_norm_m2,
    )


def solution(mesh):
    shard = P("dp", None, "mp")
    return jax.shard_map(
        per_device,
        mesh=mesh,
        in_specs=(P("dp", None), P("dp"), shard, shard, shard)
        + (P(None, "mp"),) * 3
        + (P(),) * 3
        + (P(("dp", "mp"), None),),
        out_specs=(P(("dp", "mp"), None),) * 2
        + (shard,) * 3
        + (P(None, "mp"),) * 3
        + (P(),) * 3,
        check_vma=False,
    )
```

profile of v0, /device:TPU:0, one launch (start us, length us, event | category | flops | bytes accessed | tf_op | source)
XLA Modules:
  0.0 244.8 jit_solution(9000532307840986522)
XLA Ops:
  7.2 1.4 bitcast_convert_fusion
  8.7 0.8 pad_maximum_fusion.2
  9.5 3.1 %collective-permute-start = (bf16[4,48,384]{2,1,0:T(8,128)(2,1)S(1)}, bf16[4,48,384]{2,1,0:T(8,128)(2,1)S(1)}, u32[]{:S(2)}, u32[]{:S(2)}) collective-permute-start(bf16[4,48,384]{2,1,0:T(8,128)(2,1)S(1)} %slice.52), channel_id=1, source_target_pairs={{0,8},{2,10},{4,12},{6,14},{8,16},{10,18},{12,20},{14,22},{16,24},... | collective-permute-start | bytes 442376 | tf_op jit(solution)/shard_map/ppermute | solution.py:728
  12.6 2.6 %collective-permute-start.1 = (bf16[4,48,384]{2,1,0:T(8,128)(2,1)S(1)}, bf16[4,48,384]{2,1,0:T(8,128)(2,1)S(1)}, u32[]{:S(2)}, u32[]{:S(2)}) collective-permute-start(bf16[4,48,384]{2,1,0:T(8,128)(2,1)S(1)} %slice.52), channel_id=1, source_target_pairs={{0,16},{2,18},{4,20},{6,22},{8,24},{10,26},{12,28},{14,30},{16,0},... | collective-permute-start | bytes 442376 | tf_op jit(solution)/shard_map/ppermute | solution.py:728
  15.2 1.3 collective-permute-start.2
  16.5 4.4 %all_gather.9 = f32[6,768]{1,0:T(8,128)S(1)} all-gather(f32[6,384]{1,0:T(8,128)S(1)} %copy-done.6), channel_id=1, replica_groups=mesh['dp'=16,'mp'=2] {'mp'}, dimensions={1}, use_global_device_ids=true | all-gather | bytes 27648 | tf_op jit(solution)/shard_map/all_gather | solution.py:923
  21.0 0.9 constant_dynamic-slice_fusion.x_ref.x_hbm
  21.9 6.3 %fusion = (bf16[1024,384]{1,0:T(8,128)(2,1)S(1)}, bf16[1024,384]{1,0:T(8,128)(2,1)S(1)}) fusion(f32[384]{0:T(512)S(1)} %negate_power_fusion, f32[1024]{0:T(1024)S(1)} %subtract_convert_fusion), kind=kLoop, calls=%fused_computation.3 | loop fusion | flops 1179648 | bytes 1578496 | tf_op jit(solution)/shard_map/convert
  28.2 1.3 pad_maximum_fusion.sine_ref
  29.7 1.6 collective-permute-start.3
  31.3 1.5 collective-permute-start.4
  33.8 11.6 %collective-permute-done.3.refs_2_ = bf16[4,2,48,384]{3,2,1,0:T(8,128)(2,1)S(1)} collective-permute-done((bf16[4,2,48,384]{3,2,1,0:T(8,128)(2,1)S(1)}, bf16[4,2,48,384]{3,2,1,0:T(8,128)(2,1)S(1)}, u32[]{:S(2)}, u32[]{:S(2)}) %collective-permute-start.3) | collective-permute-done | bytes 294944 | tf_op jit(solution)/shard_map/ppermute | solution.py:719
  45.5 1.9 collective-permute-start.7
  47.4 12.9 %collective-permute-start.8 = (bf16[4,2,48,384]{3,2,1,0:T(8,128)(2,1)S(1)}, bf16[4,2,48,384]{3,2,1,0:T(8,128)(2,1)S(1)}, u32[]{:S(2)}, u32[]{:S(2)}) collective-permute-start(bf16[4,2,48,384]{3,2,1,0:T(8,128)(2,1)S(1)} %collective-permute-done.4.refs_3_), channel_id=1, source_target_pairs={{0,1},{1,0},{2,3},{3,2},{4,5},{5,4},{6,7},{7,6},{8,9},{9,8},{10,11... | collective-permute-start | bytes 884744 | tf_op jit(solution)/shard_map/ppermute | solution.py:719
  61.3 10.9 %collective-permute-done.8.refs_7_ = bf16[4,2,48,384]{3,2,1,0:T(8,128)(2,1)S(1)} collective-permute-done((bf16[4,2,48,384]{3,2,1,0:T(8,128)(2,1)S(1)}, bf16[4,2,48,384]{3,2,1,0:T(8,128)(2,1)S(1)}, u32[]{:S(2)}, u32[]{:S(2)}) %collective-permute-start.8) | collective-permute-done | bytes 294944 | tf_op jit(solution)/shard_map/ppermute | solution.py:719
  72.2 0.8 copy-done.22
  76.0 8.6 %project.1 = (bf16[512,768]{1,0:T(8,128)(2,1)}, bf16[512,768]{1,0:T(8,128)(2,1)}, bf16[512,768]{1,0:T(8,128)(2,1)}, bf16[512,768]{1,0:T(8,128)(2,1)}, bf16[1024,...) custom-call(s32[4]{0:T(128)} %pad_add_fusion.place_ref, bf16[512,768]{1,0:T(8,128)(2,1)} %constant_dynamic-slice_fusion.x_ref.x_hbm, ...), custom_call_target="tpu_custom_call" | custom-call | flops 8999999488 | tf_op jit(solution)/shard_map/project/pallas_call | solution.py:264
  84.6 15.8 %attend.1 = (bf16[12,512,512]{2,1,0:T(8,128)(2,1)}, bf16[512,768]{1,0:T(8,128)(2,1)}) custom-call(s32[1]{0:T(128)} %dynamic_slice.36.len_ref, bf16[512,768]{1,0:T(8,128)(2,1)} %get-tuple-element.79.qc_ref, bf16[512,768]{1,0:T(8,128)(2,1)} %get-tuple-element.80.qp_ref, bf16[512,768]{1,0:T(8,128)(2,1)} %get-tuple-element.81.k_ref, ...), custom_call_target="tpu_custom_call" | custom-call | flops 19000000512 | tf_op jit(solution)/shard_map/attend/pallas_call | solution.py:322
  100.4 1.6 all-gather.3.cloned.1.call-done
  102.0 24.8 %mlp.1 = (bf16[512,768]{1,0:T(8,128)(2,1)}, f32[512,768]{1,0:T(8,128)}, f32[512,128]{1,0:T(8,128)}, f32[512,768]{1,0:T(8,128)}, bf16[8,4,8,48,384]{4,3,2,1,0:T(8...) custom-call(f32[6,768]{1,0:T(8,128)} %nv_ref.3, f32[4,1,768]{2,1,0:T(1,128)} %reshape.37.hb_ref, ...), custom_call_target="tpu_custom_call" | custom-call | flops 23000000512 | tf_op jit(solution)/shard_map/mlp/pallas_call | solution.py:462
  126.9 8.9 %norm_down.1 = (f32[512,768]{1,0:T(8,128)}, bf16[512,768]{1,0:T(8,128)(2,1)}, bf16[512,768]{1,0:T(8,128)(2,1)}, f32[3,768]{1,0:T(4,128)}) custom-call(f32[6,768]{1,0:T(8,128)} %nv_ref.3, f32[512,128]{1,0:T(8,128)} %get-tuple-element.87.inv_ref, f32[512,768]{1,0:T(8,128)} %get-tuple-element.88.unit_hbm, f32[512,768]{1,0:T(8,128)} %get-tuple-element.89.gh2_hbm, ...), custom_call_target="tpu_custom_call" | custom-call | flops 8000000000 | tf_op jit(solution)/shard_map/norm_down/pallas_call | solution.py:533
  135.8 19.9 %attend_back.1 = (bf16[512,768]{1,0:T(8,128)(2,1)}, bf16[512,768]{1,0:T(8,128)(2,1)}, bf16[512,768]{1,0:T(8,128)(2,1)}, bf16[1024,768]{1,0:T(8,128)(2,1)}, f32[2,768]{1,0:T(2,128)}) custom-call(bf16[12,512,512]{2,1,0:T(8,128)(2,1)} %get-tuple-element.86.probs_ref, bf16[512,768]{1,0:T(8,128)(2,1)} %get-tuple-element.91.gm_ref, ...), custom_call_target="tpu_custom_call" | custom-call | flops 28000000000 | tf_op jit(solution)/shard_map/attend_back/pallas_call | solution.py:626
  155.7 0.7 pad_maximum_fusion.3
  156.5 2.0 collective-permute-start.19
  159.1 0.9 collective-permute-start.17
  160.1 9.6 %project_back.1 = (bf16[4,4,5,48,384]{4,3,2,1,0:T(8,128)(2,1)}, bf16[4,4,5,48,384]{4,3,2,1,0:T(8,128)(2,1)}) custom-call(s32[1]{0:T(128)} %bitcast.4.core_ref, bf16[512,768]{1,0:T(8,128)(2,1)} %constant_dynamic-slice_fusion.x_ref.x_hbm, bf16[512,768]{1,0:T(8,128)(2,1)} %get-tuple-element.107.gq_ref, bf16[512,768]{1,0:T(8,128)(2,1)} %get-tuple-element.93.gk_ref, ...), custom_call_target="tpu_custom_call" | custom-call | flops 8999999488 | tf_op jit(solution)/shard_map/project_back/pallas_call | solution.py:681
  169.8 5.6 %collective-permute-done.20 = bf16[4,4,5,48,384]{4,3,2,1,0:T(8,128)(2,1)S(1)} collective-permute-done((bf16[4,4,5,48,384]{4,3,2,1,0:T(8,128)(2,1)}, bf16[4,4,5,48,384]{4,3,2,1,0:T(8,128)(2,1)S(1)}, u32[]{:S(2)}, u32[]{:S(2)}) %collective-permute-start.20) | collective-permute-done | bytes 2949152 | tf_op jit(solution)/shard_map/ppermute | solution.py:723
  175.4 4.3 %add_convert_fusion = bf16[4,4,5,48,384]{4,3,2,1,0:T(8,128)(2,1)} fusion(bf16[4,4,5,48,384]{4,3,2,1,0:T(8,128)(2,1)S(1)} %collective-permute-done.20, bf16[4,4,5,48,384]{4,3,2,1,0:T(8,128)(2,1)} %get-tuple-element.103), kind=kLoop, calls=%fused_computation | loop fusion | flops 5898240 | bytes 8847360 | tf_op jit(solution)/shard_map/convert_element_type | solution.py:807
  180.1 1.2 copy-done.2
  181.3 0.9 dynamic-slice_bitcast_fusion
  182.1 2.0 collective-permute-start.23
  184.1 1.9 collective-permute-start.24
  186.0 1.4 collective-permute-start.25
  187.5 6.8 %token_grad.1 = f32[512,768]{1,0:T(8,128)} custom-call(bf16[512,768]{1,0:T(8,128)(2,1)} %get-tuple-element.107.gq_ref, bf16[512,768]{1,0:T(8,128)(2,1)} %get-tuple-element.93.gk_ref, bf16[512,768]{1,0:T(8,128)(2,1)} %get-tuple-element.94.gv_ref, bf16[3,2,768,384]{3,2,1,0:T(8,128)(2,1)} %get-tuple-element.108.w_ref, f32[512,768]{1,0:T(8,128)} %get-tuple-element.109.gh1_ref), custom_call_target="tpu_custom_call" | custom-call | flops 6000000000 | tf_op jit(solution)/shard_map/token_grad/pallas_call | solution.py:706
  194.3 1.2 collective-permute-done.21
  196.2 4.7 %collective-permute-done.22 = f32[12,768]{1,0:T(8,128)S(1)} collective-permute-done((f32[12,768]{1,0:T(8,128)S(1)}, f32[12,768]{1,0:T(8,128)S(1)}, u32[]{:S(2)}, u32[]{:S(2)}) %collective-permute-start.22) | collective-permute-done | bytes 36896 | tf_op jit(solution)/shard_map/ppermute | solution.py:719
  201.0 4.5 %collective-permute-done.24.refs_2_ = bf16[8,48,384]{2,1,0:T(8,128)(2,1)S(1)} collective-permute-done((bf16[8,48,384]{2,1,0:T(8,128)(2,1)S(1)}, bf16[8,48,384]{2,1,0:T(8,128)(2,1)S(1)}, u32[]{:S(2)}, u32[]{:S(2)}) %collective-permute-start.24) | collective-permute-done | bytes 294944 | tf_op jit(solution)/shard_map/ppermute | solution.py:728
  205.5 1.6 collective-permute-start.26
  207.2 4.2 %adam.2 = (f32[13,48,384]{2,1,0:T(8,128)}, f32[13,48,384]{2,1,0:T(8,128)}, f32[13,48,384]{2,1,0:T(8,128)}) custom-call(bf16[8,48,384]{2,1,0:T(8,128)(2,1)} %get-tuple-element.117.refs_0_, bf16[8,48,384]{2,1,0:T(8,128)(2,1)} %copy-done.23, bf16[8,48,384]{2,1,0:T(8,128)(2,1)} %copy-done.24, bf16[8,48,384]{2,1,0:T(8,128)(2,1)} %copy-done.25, ...), custom_call_target="tpu_custom_call" | custom-call | flops 4000000000 | tf_op jit(solution)/shard_map/adam/pallas_call | solution.py:883
  211.5 0.7 multiply_subtract_fusion.1
  212.2 4.2 %reduce-scatter.5.cloned.1.call-done = bf16[1,4,5,48,384]{4,3,2,1,0:T(8,128)(2,1)} async-done(((bf16[4,4,5,48,384]{4,3,2,1,0:T(8,128)(2,1)}), bf16[1,4,5,48,384]{4,3,2,1,0:T(8,128)(2,1)}) %reduce-scatter.5.cloned.1.call-update) | async-done | bytes 737296 | tf_op jit(solution)/shard_map/reduce_scatter | solution.py:814
  216.4 1.9 dynamic-slice_bitcast_fusion.4
  218.4 2.5 %collective-permute-start.27 = (bf16[5,48,384]{2,1,0:T(8,128)(2,1)S(1)}, bf16[5,48,384]{2,1,0:T(8,128)(2,1)S(1)}, u32[]{:S(2)}, u32[]{:S(2)}) collective-permute-start(bf16[5,48,384]{2,1,0:T(8,128)(2,1)S(1)} %get-tuple-element.145), channel_id=1, source_target_pairs={{0,8},{2,10},{4,12},{6,14},{8,16},{10,18},{12,20},{14,22},{16,24},... | collective-permute-start | bytes 552968 | tf_op jit(solution)/shard_map/ppermute | solution.py:728
  220.9 1.4 collective-permute-start.28
  222.3 1.4 collective-permute-start.29
  224.4 3.5 %collective-permute-done.27.refs_1_ = bf16[5,48,384]{2,1,0:T(8,128)(2,1)S(1)} collective-permute-done((bf16[5,48,384]{2,1,0:T(8,128)(2,1)S(1)}, bf16[5,48,384]{2,1,0:T(8,128)(2,1)S(1)}, u32[]{:S(2)}, u32[]{:S(2)}) %collective-permute-start.27) | collective-permute-done | bytes 184352 | tf_op jit(solution)/shard_map/ppermute | solution.py:728
  227.8 6.8 %collective-permute-done.28.refs_2_ = bf16[5,48,384]{2,1,0:T(8,128)(2,1)S(1)} collective-permute-done((bf16[5,48,384]{2,1,0:T(8,128)(2,1)S(1)}, bf16[5,48,384]{2,1,0:T(8,128)(2,1)S(1)}, u32[]{:S(2)}, u32[]{:S(2)}) %collective-permute-start.28) | collective-permute-done | bytes 184352 | tf_op jit(solution)/shard_map/ppermute | solution.py:728
  235.4 2.9 %adam.3 = (f32[13,48,384]{2,1,0:T(8,128)}, f32[13,48,384]{2,1,0:T(8,128)}, f32[13,48,384]{2,1,0:T(8,128)}) custom-call(bf16[5,48,384]{2,1,0:T(8,128)(2,1)} %get-tuple-element.146.refs_0_, bf16[5,48,384]{2,1,0:T(8,128)(2,1)} %copy-done.26, bf16[5,48,384]{2,1,0:T(8,128)(2,1)} %copy-done.27, ...), custom_call_target="tpu_custom_call", output_to_operand_aliasing={{0}: (7, {}), {1}: (8, {}), {2}: (9, {})} | custom-call | flops 2000000000 | tf_op jit(solution)/shard_map/adam/pallas_call | solution.py:883
  (122 shorter events, 8.7 us)
Async XLA Ops:
  7.2 13.8 %copy-start = (bf16[1024,768]{1,0:T(8,128)(2,1)S(1)}, bf16[1024,768]{1,0:T(8,128)(2,1)}, u32[]{:S(2)}) copy-start(bf16[1024,768]{1,0:T(8,128)(2,1)} %param.12) | copy-start | bytes 4718596
  7.2 94.8 %all-gather.3.cloned.1.call-start = ((), (), s32[]{:S(2)}) async-start(), calls=%async_computation.4 | async-start | bytes 10948608 | tf_op jit(solution)/shard_map/all_gather | solution.py:735
  9.5 170.5 %reduce-scatter.3.cloned.1.call-start = ((), (), s32[]{:S(2)}) async-start(), calls=%async_computation.2 | async-start | bytes 10616832 | tf_op jit(solution)/shard_map/reduce_scatter | solution.py:800
  9.5 20.0 %collective-permute-start = (bf16[4,48,384]{2,1,0:T(8,128)(2,1)S(1)}, bf16[4,48,384]{2,1,0:T(8,128)(2,1)S(1)}, u32[]{:S(2)}, u32[]{:S(2)}) collective-permute-start(bf16[4,48,384]{2,1,0:T(8,128)(2,1)S(1)} %slice.52), channel_id=1, source_target_pairs={{0,8},{2,10},{4,12},{6,14},{8,16},{10,18},{12,20},{14,22},{16,24},... | collective-permute-start | bytes 442376 | tf_op jit(solution)/shard_map/ppermute | solution.py:728
  12.6 16.9 %collective-permute-start.1 = (bf16[4,48,384]{2,1,0:T(8,128)(2,1)S(1)}, bf16[4,48,384]{2,1,0:T(8,128)(2,1)S(1)}, u32[]{:S(2)}, u32[]{:S(2)}) collective-permute-start(bf16[4,48,384]{2,1,0:T(8,128)(2,1)S(1)} %slice.52), channel_id=1, source_target_pairs={{0,16},{2,18},{4,20},{6,22},{8,24},{10,26},{12,28},{14,30},{16,0},... | collective-permute-start | bytes 442376 | tf_op jit(solution)/shard_map/ppermute | solution.py:728
  15.2 14.3 %collective-permute-start.2 = (bf16[4,48,384]{2,1,0:T(8,128)(2,1)S(1)}, bf16[4,48,384]{2,1,0:T(8,128)(2,1)S(1)}, u32[]{:S(2)}, u32[]{:S(2)}) collective-permute-start(bf16[4,48,384]{2,1,0:T(8,128)(2,1)S(1)} %slice.52), channel_id=1, source_target_pairs={{0,24},{2,26},{4,28},{6,30},{8,0},{10,2},{12,4},{14,6},{16,8},{18,... | collective-permute-start | bytes 442376 | tf_op jit(solution)/shard_map/ppermute | solution.py:728
  29.5 43.9 %copy-start.29 = (s32[2]{0:T(128)S(1)}, s32[2]{0:T(128)}, u32[]{:S(2)}) copy-start(s32[2]{0:T(128)} %param.13) | copy-start | bytes 28
  29.7 46.2 %copy-start.3 = (bf16[4,2,48,384]{3,2,1,0:T(8,128)(2,1)}, bf16[4,2,48,384]{3,2,1,0:T(8,128)(2,1)S(1)}, u32[]{:S(2)}) copy-start(bf16[4,2,48,384]{3,2,1,0:T(8,128)(2,1)S(1)} %get-tuple-element.147.refs_1_) | copy-start | bytes 884740
  29.7 46.2 %copy-start.4 = (bf16[4,2,48,384]{3,2,1,0:T(8,128)(2,1)}, bf16[4,2,48,384]{3,2,1,0:T(8,128)(2,1)S(1)}, u32[]{:S(2)}) copy-start(bf16[4,2,48,384]{3,2,1,0:T(8,128)(2,1)S(1)} %get-tuple-element.148.refs_0_) | copy-start | bytes 884740
  29.7 15.8 %collective-permute-start.3 = (bf16[4,2,48,384]{3,2,1,0:T(8,128)(2,1)S(1)}, bf16[4,2,48,384]{3,2,1,0:T(8,128)(2,1)S(1)}, u32[]{:S(2)}, u32[]{:S(2)}) collective-permute-start(bf16[4,2,48,384]{3,2,1,0:T(8,128)(2,1)S(1)} %get-tuple-element.148.refs_0_), channel_id=1, source_target_pairs={{0,1},{1,0},{2,3},{3,2},{4,5},{5,4},{6,7},{7,6},{8,9},{9,8},{10,11... | collective-permute-start | bytes 884744 | tf_op jit(solution)/shard_map/ppermute | solution.py:719
  31.3 14.2 %collective-permute-start.4 = (bf16[4,2,48,384]{3,2,1,0:T(8,128)(2,1)S(1)}, bf16[4,2,48,384]{3,2,1,0:T(8,128)(2,1)S(1)}, u32[]{:S(2)}, u32[]{:S(2)}) collective-permute-start(bf16[4,2,48,384]{3,2,1,0:T(8,128)(2,1)S(1)} %get-tuple-element.147.refs_1_), channel_id=1, source_target_pairs={{0,4},{2,6},{4,0},{6,2},{8,12},{10,14},{12,8},{14,10},{16,20},{18,... | collective-permute-start | bytes 884744 | tf_op jit(solution)/shard_map/ppermute | solution.py:723
  32.8 14.6 %collective-permute-start.5 = (bf16[4,2,48,384]{3,2,1,0:T(8,128)(2,1)S(1)}, bf16[4,2,48,384]{3,2,1,0:T(8,128)(2,1)S(1)}, u32[]{:S(2)}, u32[]{:S(2)}) collective-permute-start(bf16[4,2,48,384]{3,2,1,0:T(8,128)(2,1)S(1)} %get-tuple-element.148.refs_0_), channel_id=1, source_target_pairs={{0,4},{2,6},{4,0},{6,2},{8,12},{10,14},{12,8},{14,10},{16,20},{18,... | collective-permute-start | bytes 884744 | tf_op jit(solution)/shard_map/ppermute | solution.py:723
  33.3 27.0 %collective-permute-start.6 = (bf16[4,2,48,384]{3,2,1,0:T(8,128)(2,1)S(1)}, bf16[4,2,48,384]{3,2,1,0:T(8,128)(2,1)S(1)}, u32[]{:S(2)}, u32[]{:S(2)}) collective-permute-start(bf16[4,2,48,384]{3,2,1,0:T(8,128)(2,1)S(1)} %get-tuple-element.147.refs_1_), channel_id=1, source_target_pairs={{0,1},{1,0},{2,3},{3,2},{4,5},{5,4},{6,7},{7,6},{8,9},{9,8},{10,11... | collective-permute-start | bytes 884744 | tf_op jit(solution)/shard_map/ppermute | solution.py:719
  33.8 26.5 %collective-permute-start.9 = (bf16[4,2,48,384]{3,2,1,0:T(8,128)(2,1)S(1)}, bf16[4,2,48,384]{3,2,1,0:T(8,128)(2,1)S(1)}, u32[]{:S(2)}, u32[]{:S(2)}) collective-permute-start(bf16[4,2,48,384]{3,2,1,0:T(8,128)(2,1)S(1)} %get-tuple-element.148.refs_0_), channel_id=1, source_target_pairs={{0,2},{2,0},{4,6},{6,4},{8,10},{10,8},{12,14},{14,12},{16,18},{18,... | collective-permute-start | bytes 884744 | tf_op jit(solution)/shard_map/ppermute | solution.py:723
  45.5 30.5 %copy-start.14 = (bf16[4,2,48,384]{3,2,1,0:T(8,128)(2,1)}, bf16[4,2,48,384]{3,2,1,0:T(8,128)(2,1)S(1)}, u32[]{:S(2)}) copy-start(bf16[4,2,48,384]{3,2,1,0:T(8,128)(2,1)S(1)} %collective-permute-done.3.refs_2_) | copy-start | bytes 884740
  45.5 15.3 %collective-permute-start.10 = (bf16[4,2,48,384]{3,2,1,0:T(8,128)(2,1)S(1)}, bf16[4,2,48,384]{3,2,1,0:T(8,128)(2,1)S(1)}, u32[]{:S(2)}, u32[]{:S(2)}) collective-permute-start(bf16[4,2,48,384]{3,2,1,0:T(8,128)(2,1)S(1)} %get-tuple-element.147.refs_1_), channel_id=1, source_target_pairs={{0,2},{2,0},{4,6},{6,4},{8,10},{10,8},{12,14},{14,12},{16,18},{18,... | collective-permute-start | bytes 884744 | tf_op jit(solution)/shard_map/ppermute | solution.py:723
  45.5 30.5 %copy-start.15 = (bf16[4,2,48,384]{3,2,1,0:T(8,128)(2,1)}, bf16[4,2,48,384]{3,2,1,0:T(8,128)(2,1)S(1)}, u32[]{:S(2)}) copy-start(bf16[4,2,48,384]{3,2,1,0:T(8,128)(2,1)S(1)} %collective-permute-done.4.refs_3_) | copy-start | bytes 884740
  45.5 15.4 %collective-permute-start.7 = (bf16[4,2,48,384]{3,2,1,0:T(8,128)(2,1)S(1)}, bf16[4,2,48,384]{3,2,1,0:T(8,128)(2,1)S(1)}, u32[]{:S(2)}, u32[]{:S(2)}) collective-permute-start(bf16[4,2,48,384]{3,2,1,0:T(8,128)(2,1)S(1)} %collective-permute-done.3.refs_2_), channel_id=1, source_target_pairs={{0,4},{2,6},{4,0},{6,2},{8,12},{10,14},{12,8},{14,10},{16,20},{18,... | collective-permute-start | bytes 884744 | tf_op jit(solution)/shard_map/ppermute | solution.py:723
  47.4 28.6 %copy-start.16 = (bf16[4,2,48,384]{3,2,1,0:T(8,128)(2,1)}, bf16[4,2,48,384]{3,2,1,0:T(8,128)(2,1)S(1)}, u32[]{:S(2)}) copy-start(bf16[4,2,48,384]{3,2,1,0:T(8,128)(2,1)S(1)} %collective-permute-done.5.refs_4_) | copy-start | bytes 884740
  47.4 24.8 %collective-permute-start.8 = (bf16[4,2,48,384]{3,2,1,0:T(8,128)(2,1)S(1)}, bf16[4,2,48,384]{3,2,1,0:T(8,128)(2,1)S(1)}, u32[]{:S(2)}, u32[]{:S(2)}) collective-permute-start(bf16[4,2,48,384]{3,2,1,0:T(8,128)(2,1)S(1)} %collective-permute-done.4.refs_3_), channel_id=1, source_target_pairs={{0,1},{1,0},{2,3},{3,2},{4,5},{5,4},{6,7},{7,6},{8,9},{9,8},{10,11... | collective-permute-start | bytes 884744 | tf_op jit(solution)/shard_map/ppermute | solution.py:719
  60.3 15.7 %copy-start.17 = (bf16[4,2,48,384]{3,2,1,0:T(8,128)(2,1)}, bf16[4,2,48,384]{3,2,1,0:T(8,128)(2,1)S(1)}, u32[]{:S(2)}) copy-start(bf16[4,2,48,384]{3,2,1,0:T(8,128)(2,1)S(1)} %collective-permute-done.6.refs_5_) | copy-start | bytes 884740
  60.3 11.9 %collective-permute-start.11 = (bf16[4,2,48,384]{3,2,1,0:T(8,128)(2,1)S(1)}, bf16[4,2,48,384]{3,2,1,0:T(8,128)(2,1)S(1)}, u32[]{:S(2)}, u32[]{:S(2)}) collective-permute-start(bf16[4,2,48,384]{3,2,1,0:T(8,128)(2,1)S(1)} %collective-permute-done.3.refs_2_), channel_id=1, source_target_pairs={{0,2},{2,0},{4,6},{6,4},{8,10},{10,8},{12,14},{14,12},{16,18},{18,... | collective-permute-start | bytes 884744 | tf_op jit(solution)/shard_map/ppermute | solution.py:723
  60.3 15.7 %copy-start.18 = (bf16[4,2,48,384]{3,2,1,0:T(8,128)(2,1)}, bf16[4,2,48,384]{3,2,1,0:T(8,128)(2,1)S(1)}, u32[]{:S(2)}) copy-start(bf16[4,2,48,384]{3,2,1,0:T(8,128)(2,1)S(1)} %collective-permute-done.9.refs_8_) | copy-start | bytes 884740
  60.3 15.6 %collective-permute-start.12 = (bf16[4,2,48,384]{3,2,1,0:T(8,128)(2,1)S(1)}, bf16[4,2,48,384]{3,2,1,0:T(8,128)(2,1)}, u32[]{:S(2)}, u32[]{:S(2)}) collective-permute-start(bf16[4,2,48,384]{3,2,1,0:T(8,128)(2,1)S(1)} %collective-permute-done.4.refs_3_), channel_id=1, source_target_pairs={{0,2},{2,0},{4,6},{6,4},{8,10},{10,8},{12,14},{14,12},{16,18},{18,... | collective-permute-start | bytes 884744 | tf_op jit(solution)/shard_map/ppermute | solution.py:723
  60.8 15.2 %copy-start.19 = (bf16[4,2,48,384]{3,2,1,0:T(8,128)(2,1)}, bf16[4,2,48,384]{3,2,1,0:T(8,128)(2,1)S(1)}, u32[]{:S(2)}) copy-start(bf16[4,2,48,384]{3,2,1,0:T(8,128)(2,1)S(1)} %collective-permute-done.10.refs_9_) | copy-start | bytes 884740
  60.8 15.1 %collective-permute-start.13 = (bf16[4,2,48,384]{3,2,1,0:T(8,128)(2,1)S(1)}, bf16[4,2,48,384]{3,2,1,0:T(8,128)(2,1)}, u32[]{:S(2)}, u32[]{:S(2)}) collective-permute-start(bf16[4,2,48,384]{3,2,1,0:T(8,128)(2,1)S(1)} %collective-permute-done.5.refs_4_), channel_id=1, source_target_pairs={{0,2},{2,0},{4,6},{6,4},{8,10},{10,8},{12,14},{14,12},{16,18},{18,... | collective-permute-start | bytes 884744 | tf_op jit(solution)/shard_map/ppermute | solution.py:723
  60.9 15.1 %copy-start.20 = (bf16[4,2,48,384]{3,2,1,0:T(8,128)(2,1)}, bf16[4,2,48,384]{3,2,1,0:T(8,128)(2,1)S(1)}, u32[]{:S(2)}) copy-start(bf16[4,2,48,384]{3,2,1,0:T(8,128)(2,1)S(1)} %collective-permute-done.7.refs_6_) | copy-start | bytes 884740
  60.9 15.0 %collective-permute-start.14 = (bf16[4,2,48,384]{3,2,1,0:T(8,128)(2,1)S(1)}, bf16[4,2,48,384]{3,2,1,0:T(8,128)(2,1)}, u32[]{:S(2)}, u32[]{:S(2)}) collective-permute-start(bf16[4,2,48,384]{3,2,1,0:T(8,128)(2,1)S(1)} %collective-permute-done.6.refs_5_), channel_id=1, source_target_pairs={{0,2},{2,0},{4,6},{6,4},{8,10},{10,8},{12,14},{14,12},{16,18},{18,... | collective-permute-start | bytes 884744 | tf_op jit(solution)/shard_map/ppermute | solution.py:723
  72.2 3.7 %collective-permute-start.15 = (bf16[4,2,48,384]{3,2,1,0:T(8,128)(2,1)S(1)}, bf16[4,2,48,384]{3,2,1,0:T(8,128)(2,1)}, u32[]{:S(2)}, u32[]{:S(2)}) collective-permute-start(bf16[4,2,48,384]{3,2,1,0:T(8,128)(2,1)S(1)} %collective-permute-done.7.refs_6_), channel_id=1, source_target_pairs={{0,2},{2,0},{4,6},{6,4},{8,10},{10,8},{12,14},{14,12},{16,18},{18,... | collective-permute-start | bytes 884744 | tf_op jit(solution)/shard_map/ppermute | solution.py:723
  73.0 2.9 %collective-permute-start.16 = (bf16[4,2,48,384]{3,2,1,0:T(8,128)(2,1)S(1)}, bf16[4,2,48,384]{3,2,1,0:T(8,128)(2,1)}, u32[]{:S(2)}, u32[]{:S(2)}) collective-permute-start(bf16[4,2,48,384]{3,2,1,0:T(8,128)(2,1)S(1)} %collective-permute-done.8.refs_7_), channel_id=1, source_target_pairs={{0,2},{2,0},{4,6},{6,4},{8,10},{10,8},{12,14},{14,12},{16,18},{18,... | collective-permute-start | bytes 884744 | tf_op jit(solution)/shard_map/ppermute | solution.py:723
  126.8 89.6 %reduce-scatter.5.cloned.1.call-start = ((), (), s32[]{:S(2)}) async-start(), calls=%async_computation.3 | async-start | bytes 3686400 | tf_op jit(solution)/shard_map/reduce_scatter | solution.py:814
  135.7 20.0 %copy-start.5 = (f32[7,768]{1,0:T(8,128)S(1)}, f32[7,768]{1,0:T(8,128)}, u32[]{:S(2)}) copy-start(f32[7,768]{1,0:T(8,128)} %get-tuple-element.99) | copy-start | bytes 64516
  135.8 20.0 %copy-start.7 = (f32[3,768]{1,0:T(4,128)S(1)}, f32[3,768]{1,0:T(4,128)}, u32[]{:S(2)}) copy-start(f32[3,768]{1,0:T(4,128)} %get-tuple-element.100) | copy-start | bytes 27652
  156.5 13.2 %collective-permute-start.19 = (f32[12,768]{1,0:T(8,128)S(1)}, f32[12,768]{1,0:T(8,128)S(1)}, u32[]{:S(2)}, u32[]{:S(2)}) collective-permute-start(f32[12,768]{1,0:T(8,128)S(1)} %pad_maximum_fusion.3), channel_id=1, source_target_pairs={{0,24},{2,26},{4,28},{6,30},{8,0},{10,2},{12,4},{14,6},{16,8},{18,... | collective-permute-start | bytes 110600 | tf_op jit(solution)/shard_map/ppermute | solution.py:728
  158.5 11.2 %collective-permute-start.18 = (f32[12,768]{1,0:T(8,128)S(1)}, f32[12,768]{1,0:T(8,128)S(1)}, u32[]{:S(2)}, u32[]{:S(2)}) collective-permute-start(f32[12,768]{1,0:T(8,128)S(1)} %pad_maximum_fusion.3), channel_id=1, source_target_pairs={{0,16},{2,18},{4,20},{6,22},{8,24},{10,26},{12,28},{14,30},{16,0},... | collective-permute-start | bytes 110600 | tf_op jit(solution)/shard_map/ppermute | solution.py:728
  159.1 10.5 %collective-permute-start.17 = (f32[12,768]{1,0:T(8,128)S(1)}, f32[12,768]{1,0:T(8,128)S(1)}, u32[]{:S(2)}, u32[]{:S(2)}) collective-permute-start(f32[12,768]{1,0:T(8,128)S(1)} %pad_maximum_fusion.3), channel_id=1, source_target_pairs={{0,8},{2,10},{4,12},{6,14},{8,16},{10,18},{12,20},{14,22},{16,24},... | collective-permute-start | bytes 110600 | tf_op jit(solution)/shard_map/ppermute | solution.py:728
  169.7 5.7 %collective-permute-start.20 = (bf16[4,4,5,48,384]{4,3,2,1,0:T(8,128)(2,1)}, bf16[4,4,5,48,384]{4,3,2,1,0:T(8,128)(2,1)S(1)}, u32[]{:S(2)}, u32[]{:S(2)}) collective-permute-start(bf16[4,4,5,48,384]{4,3,2,1,0:T(8,128)(2,1)} %get-tuple-element.104), channel_id=1, source_target_pairs={{0,2},{2,0},{4,6},{6,4},{8,10},{10,8},{12,14},{14,12},{16,18},{18,... | collective-permute-start | bytes 8847368 | tf_op jit(solution)/shard_map/ppermute | solution.py:723
  182.1 18.9 %collective-permute-start.23 = (bf16[8,48,384]{2,1,0:T(8,128)(2,1)S(1)}, bf16[8,48,384]{2,1,0:T(8,128)(2,1)S(1)}, u32[]{:S(2)}, u32[]{:S(2)}) collective-permute-start(bf16[8,48,384]{2,1,0:T(8,128)(2,1)S(1)} %get-tuple-element.113), channel_id=1, source_target_pairs={{0,8},{2,10},{4,12},{6,14},{8,16},{10,18},{12,20},{14,22},{16,24},... | collective-permute-start | bytes 884744 | tf_op jit(solution)/shard_map/ppermute | solution.py:728
  184.1 21.4 %collective-permute-start.24 = (bf16[8,48,384]{2,1,0:T(8,128)(2,1)S(1)}, bf16[8,48,384]{2,1,0:T(8,128)(2,1)S(1)}, u32[]{:S(2)}, u32[]{:S(2)}) collective-permute-start(bf16[8,48,384]{2,1,0:T(8,128)(2,1)S(1)} %get-tuple-element.114), channel_id=1, source_target_pairs={{0,16},{2,18},{4,20},{6,22},{8,24},{10,26},{12,28},{14,30},{16,0},... | collective-permute-start | bytes 884744 | tf_op jit(solution)/shard_map/ppermute | solution.py:728
  186.0 19.5 %collective-permute-start.25 = (bf16[8,48,384]{2,1,0:T(8,128)(2,1)S(1)}, bf16[8,48,384]{2,1,0:T(8,128)(2,1)S(1)}, u32[]{:S(2)}, u32[]{:S(2)}) collective-permute-start(bf16[8,48,384]{2,1,0:T(8,128)(2,1)S(1)} %get-tuple-element.115), channel_id=1, source_target_pairs={{0,24},{2,26},{4,28},{6,30},{8,0},{10,2},{12,4},{14,6},{16,8},{18,... | collective-permute-start | bytes 884744 | tf_op jit(solution)/shard_map/ppermute | solution.py:728
  194.3 1.2 collective-permute-start.21
  195.6 5.4 %collective-permute-start.22 = (f32[12,768]{1,0:T(8,128)S(1)}, f32[12,768]{1,0:T(8,128)S(1)}, u32[]{:S(2)}, u32[]{:S(2)}) collective-permute-start(f32[12,768]{1,0:T(8,128)S(1)} %add.139), channel_id=1, source_target_pairs={{0,1},{1,0},{2,3},{3,2},{4,5},{5,4},{6,7},{7,6},{8,9},{9,8},{10,11... | collective-permute-start | bytes 110600 | tf_op jit(solution)/shard_map/ppermute | solution.py:719
  205.5 5.9 %collective-permute-start.26 = (f32[12,768]{1,0:T(8,128)S(1)}, f32[12,768]{1,0:T(8,128)S(1)}, u32[]{:S(2)}, u32[]{:S(2)}) collective-permute-start(f32[12,768]{1,0:T(8,128)S(1)} %add.140), channel_id=1, source_target_pairs={{0,4},{2,6},{4,0},{6,2},{8,12},{10,14},{12,8},{14,10},{16,20},{18,... | collective-permute-start | bytes 110600 | tf_op jit(solution)/shard_map/ppermute | solution.py:723
  211.4 12.3 %copy-start.9 = (f32[6,768]{1,0:T(8,128)S(1)}, f32[6,768]{1,0:T(8,128)}, u32[]{:S(2)}) copy-start(f32[6,768]{1,0:T(8,128)} %param.21) | copy-start | bytes 55300
  211.4 12.3 %copy-start.10 = (f32[6,768]{1,0:T(8,128)S(1)}, f32[6,768]{1,0:T(8,128)}, u32[]{:S(2)}) copy-start(f32[6,768]{1,0:T(8,128)} %param.22) | copy-start | bytes 55300
  218.4 9.4 %collective-permute-start.27 = (bf16[5,48,384]{2,1,0:T(8,128)(2,1)S(1)}, bf16[5,48,384]{2,1,0:T(8,128)(2,1)S(1)}, u32[]{:S(2)}, u32[]{:S(2)}) collective-permute-start(bf16[5,48,384]{2,1,0:T(8,128)(2,1)S(1)} %get-tuple-element.145), channel_id=1, source_target_pairs={{0,8},{2,10},{4,12},{6,14},{8,16},{10,18},{12,20},{14,22},{16,24},... | collective-permute-start | bytes 552968 | tf_op jit(solution)/shard_map/ppermute | solution.py:728
  220.9 13.7 %collective-permute-start.28 = (bf16[5,48,384]{2,1,0:T(8,128)(2,1)S(1)}, bf16[5,48,384]{2,1,0:T(8,128)(2,1)S(1)}, u32[]{:S(2)}, u32[]{:S(2)}) collective-permute-start(bf16[5,48,384]{2,1,0:T(8,128)(2,1)S(1)} %get-tuple-element.144), channel_id=1, source_target_pairs={{0,16},{2,18},{4,20},{6,22},{8,24},{10,26},{12,28},{14,30},{16,0},... | collective-permute-start | bytes 552968 | tf_op jit(solution)/shard_map/ppermute | solution.py:728
  222.3 12.3 %collective-permute-start.29 = (bf16[5,48,384]{2,1,0:T(8,128)(2,1)S(1)}, bf16[5,48,384]{2,1,0:T(8,128)(2,1)S(1)}, u32[]{:S(2)}, u32[]{:S(2)}) collective-permute-start(bf16[5,48,384]{2,1,0:T(8,128)(2,1)S(1)} %get-tuple-element.143), channel_id=1, source_target_pairs={{0,24},{2,26},{4,28},{6,30},{8,0},{10,2},{12,4},{14,6},{16,8},{18,... | collective-permute-start | bytes 552968 | tf_op jit(solution)/shard_map/ppermute | solution.py:728
  (15 other events, 66.4 us)
Sparse Core Ops, SparseCore 0:
  10.2 91.7 all-gather.2
  127.0 52.9 reduce-scatter.2
  182.3 34.0 reduce-scatter.4
where the time goes:
time: 247 us; the launch traced here: 245 us
  Pallas kernels  102 us (41%)
  waiting for transfers between devices  55 us (22%)
  starting transfers between devices  44.2 us (18%)
  other arithmetic  16.9 us (7%)
  between operations  14.3 us (6%)
  local copies, waits for them, and re-layouts  8.46 us (3%)
  blocking collectives  4.39 us (2%)
    ppermute x4, waiting for transfers between devices, swap_x(): return lax.ppermute(value, 'mp', [(0, 1), (1, 0)])  27.2 us
    pallas_call x1, Pallas kernels, mlp(): pl.pallas_call(functools.partial(mlp_kernel, blocks), grid=(1,), in_specs...  24.8 us
    ppermute x12, starting transfers between devices, shift_line(): lax.ppermute(value, 'dp', [(d, (d + 4 * step) % dp) for d in range(dp)])  21.3 us
    pallas_call x1, Pallas kernels, attend_back(): pl.pallas_call(attend_back_kernel, grid=(heads // 2,), in_specs=[pl.Block...  19.9 us
    pallas_call x1, Pallas kernels, attend(): pl.pallas_call(attend_kernel, grid=(heads // 2,), in_specs=[pl.BlockSpec(...  15.8 us
    ppermute x4, starting transfers between devices, swap_x(): return lax.ppermute(value, 'mp', [(0, 1), (1, 0)])  15.7 us
    ppermute x12, waiting for transfers between devices, shift_line(): lax.ppermute(value, 'dp', [(d, (d + 4 * step) % dp) for d in range(dp)])  14.7 us
    pallas_call x1, Pallas kernels, project_back(): pl.pallas_call(project_back_kernel, grid=(5,), in_specs=[pl.BlockSpec(mem...  9.6 us
  transfers between devices with their start and end apart: 33, of which 11 were waited for; matrix products, arithmetic and copies ran while one was open for 8% of the time, Pallas kernels for 30%

commit v1 on v0

--- a/solution.py
+++ b/solution.py
@@ -20,6 +20,7 @@
 SCALE = HEAD_FEATURES ** (-0.5)
 ROW_BLOCK = 256
 VMEM_MB = 56
+ADAM_MB = 16
 UNROLL = 1
 BF = jnp.bfloat16
 F32 = jnp.float32
@@ -877,8 +878,10 @@
 
 def adam_blocks(pieces, order, param, one, two, done):
     blocks, rows, columns = pieces[0].shape
+    shape = jax.ShapeDtypeStruct(param.shape, F32)
     part = whole((blocks, rows, columns) if done else param.shape)
-    shape = jax.ShapeDtypeStruct(param.shape, F32)
+    if done:
+        param, one, two = param[:blocks], one[:blocks], two[:blocks]
     count = len(pieces)
     return pl.pallas_call(
         functools.partial(adam_kernel, order, count),
@@ -889,7 +892,7 @@
         out_specs=[part] * 3,
         out_shape=[shape] * 3,
         input_output_aliases={count + 3 + i: i for i in range(len(done))},
-        compiler_params=params(VMEM_MB),
+        compiler_params=params(ADAM_MB),
         cost_estimate=cost(blocks // 2),
         name="adam",
     )(*pieces, param, one, two, *done)

time: 247 us -> 245 us (level)
  Pallas kernels: 102 us -> 97.6 us
  local copies, waits for them, and re-layouts: 8.46 us -> 12.2 us
    pallas_call x2, Pallas kernels: 7.12 us -> 3.05 us  [adam_blocks(): pl.pallas_call(functools.partial(adam_kernel, order, count), grid=(1,), i...]
    unnamed x60 -> x54, local copies, waits for them, and re-layouts: 2.79 us -> 5.03 us
where the time goes in v1:
time: 245 us; the launch traced here: 242 us
  Pallas kernels  97.6 us (40%)
  waiting for transfers between devices  53 us (22%)
  starting transfers between devices  44.1 us (18%)
  other arithmetic  16.9 us (7%)
  between operations  14.3 us (6%)
  local copies, waits for them, and re-layouts  12.2 us (5%)
  blocking collectives  4.39 us (2%)
    ppermute x4, waiting for transfers between devices, swap_x(): return lax.ppermute(value, 'mp', [(0, 1), (1, 0)])  25.1 us
    pallas_call x1, Pallas kernels, mlp(): pl.pallas_call(functools.partial(mlp_kernel, blocks), grid=(1,), in_specs...  24.9 us
    ppermute x12, starting transfers between devices, shift_line(): lax.ppermute(value, 'dp', [(d, (d + 4 * step) % dp) for d in range(dp)])  21.2 us
    pallas_call x1, Pallas kernels, attend_back(): pl.pallas_call(attend_back_kernel, grid=(heads // 2,), in_specs=[pl.Block...  20 us
    pallas_call x1, Pallas kernels, attend(): pl.pallas_call(attend_kernel, grid=(heads // 2,), in_specs=[pl.BlockSpec(...  15.8 us
    ppermute x4, starting transfers between devices, swap_x(): return lax.ppermute(value, 'mp', [(0, 1), (1, 0)])  15.7 us
    ppermute x12, waiting for transfers between devices, shift_line(): lax.ppermute(value, 'dp', [(d, (d + 4 * step) % dp) for d in range(dp)])  15 us
    pallas_call x1, Pallas kernels, project_back(): pl.pallas_call(project_back_kernel, grid=(5,), in_specs=[pl.BlockSpec(mem...  9.59 us
  transfers between devices with their start and end apart: 33, of which 11 were waited for; matrix products, arithmetic and copies ran while one was open for 8% of the time, Pallas kernels for 30%

profile of v1, /device:TPU:0, one launch (start us, length us, event | category | flops | bytes accessed | tf_op | source)
XLA Modules:
  0.0 242.4 jit_solution(746841109920672043)
XLA Ops:
  7.2 1.4 bitcast_convert_fusion
  9.5 3.1 %collective-permute-start = (bf16[4,48,384]{2,1,0:T(8,128)(2,1)S(1)}, bf16[4,48,384]{2,1,0:T(8,128)(2,1)S(1)}, u32[]{:S(2)}, u32[]{:S(2)}) collective-permute-start(bf16[4,48,384]{2,1,0:T(8,128)(2,1)S(1)} %slice.64), channel_id=1, source_target_pairs={{0,8},{2,10},{4,12},{6,14},{8,16},{10,18},{12,20},{14,22},{16,24},... | collective-permute-start | bytes 442376 | tf_op jit(solution)/shard_map/ppermute | solution.py:729
  12.6 2.6 %collective-permute-start.1 = (bf16[4,48,384]{2,1,0:T(8,128)(2,1)S(1)}, bf16[4,48,384]{2,1,0:T(8,128)(2,1)S(1)}, u32[]{:S(2)}, u32[]{:S(2)}) collective-permute-start(bf16[4,48,384]{2,1,0:T(8,128)(2,1)S(1)} %slice.64), channel_id=1, source_target_pairs={{0,16},{2,18},{4,20},{6,22},{8,24},{10,26},{12,28},{14,30},{16,0},... | collective-permute-start | bytes 442376 | tf_op jit(solution)/shard_map/ppermute | solution.py:729
  15.2 1.3 collective-permute-start.2
  16.5 4.4 %all_gather.9 = f32[6,768]{1,0:T(8,128)S(1)} all-gather(f32[6,384]{1,0:T(8,128)S(1)} %copy-done.9), channel_id=1, replica_groups=mesh['dp'=16,'mp'=2] {'mp'}, dimensions={1}, use_global_device_ids=true | all-gather | bytes 27648 | tf_op jit(solution)/shard_map/all_gather | solution.py:926
  21.0 0.9 constant_dynamic-slice_fusion.x_ref.x_hbm
  21.9 6.3 %fusion = (bf16[1024,384]{1,0:T(8,128)(2,1)S(1)}, bf16[1024,384]{1,0:T(8,128)(2,1)S(1)}) fusion(f32[384]{0:T(512)S(1)} %negate_power_fusion, f32[1024]{0:T(1024)S(1)} %subtract_convert_fusion), kind=kLoop, calls=%fused_computation.3 | loop fusion | flops 1179648 | bytes 1578496 | tf_op jit(solution)/shard_map/convert
  28.2 1.3 pad_maximum_fusion.sine_ref
  29.7 1.6 collective-permute-start.3
  31.3 1.5 collective-permute-start.4
  33.8 11.6 %collective-permute-done.3.refs_2_ = bf16[4,2,48,384]{3,2,1,0:T(8,128)(2,1)S(1)} collective-permute-done((bf16[4,2,48,384]{3,2,1,0:T(8,128)(2,1)S(1)}, bf16[4,2,48,384]{3,2,1,0:T(8,128)(2,1)S(1)}, u32[]{:S(2)}, u32[]{:S(2)}) %collective-permute-start.3) | collective-permute-done | bytes 294944 | tf_op jit(solution)/shard_map/ppermute | solution.py:720
  45.5 1.9 collective-permute-start.7
  47.4 12.9 %collective-permute-start.8 = (bf16[4,2,48,384]{3,2,1,0:T(8,128)(2,1)S(1)}, bf16[4,2,48,384]{3,2,1,0:T(8,128)(2,1)S(1)}, u32[]{:S(2)}, u32[]{:S(2)}) collective-permute-start(bf16[4,2,48,384]{3,2,1,0:T(8,128)(2,1)S(1)} %collective-permute-done.4.refs_3_), channel_id=1, source_target_pairs={{0,1},{1,0},{2,3},{3,2},{4,5},{5,4},{6,7},{7,6},{8,9},{9,8},{10,11... | collective-permute-start | bytes 884744 | tf_op jit(solution)/shard_map/ppermute | solution.py:720
  61.3 10.9 %collective-permute-done.8.refs_7_ = bf16[4,2,48,384]{3,2,1,0:T(8,128)(2,1)S(1)} collective-permute-done((bf16[4,2,48,384]{3,2,1,0:T(8,128)(2,1)S(1)}, bf16[4,2,48,384]{3,2,1,0:T(8,128)(2,1)S(1)}, u32[]{:S(2)}, u32[]{:S(2)}) %collective-permute-start.8) | collective-permute-done | bytes 294944 | tf_op jit(solution)/shard_map/ppermute | solution.py:720
  75.9 8.6 %project.1 = (bf16[512,768]{1,0:T(8,128)(2,1)}, bf16[512,768]{1,0:T(8,128)(2,1)}, bf16[512,768]{1,0:T(8,128)(2,1)}, bf16[512,768]{1,0:T(8,128)(2,1)}, bf16[1024,...) custom-call(s32[4]{0:T(128)} %pad_add_fusion.place_ref, bf16[512,768]{1,0:T(8,128)(2,1)} %constant_dynamic-slice_fusion.x_ref.x_hbm, ...), custom_call_target="tpu_custom_call" | custom-call | flops 8999999488 | tf_op jit(solution)/shard_map/project/pallas_call | solution.py:265
  84.5 15.8 %attend.1 = (bf16[12,512,512]{2,1,0:T(8,128)(2,1)}, bf16[512,768]{1,0:T(8,128)(2,1)}) custom-call(s32[1]{0:T(128)} %dynamic_slice.36.len_ref, bf16[512,768]{1,0:T(8,128)(2,1)} %get-tuple-element.79.qc_ref, bf16[512,768]{1,0:T(8,128)(2,1)} %get-tuple-element.80.qp_ref, bf16[512,768]{1,0:T(8,128)(2,1)} %get-tuple-element.81.k_ref, ...), custom_call_target="tpu_custom_call" | custom-call | flops 19000000512 | tf_op jit(solution)/shard_map/attend/pallas_call | solution.py:323
  100.4 1.7 all-gather.3.cloned.1.call-done
  102.1 24.9 %mlp.1 = (bf16[512,768]{1,0:T(8,128)(2,1)}, f32[512,768]{1,0:T(8,128)}, f32[512,128]{1,0:T(8,128)}, f32[512,768]{1,0:T(8,128)}, bf16[8,4,8,48,384]{4,3,2,1,0:T(8...) custom-call(f32[6,768]{1,0:T(8,128)} %nv_ref.3, f32[4,1,768]{2,1,0:T(1,128)} %reshape.37.hb_ref, ...), custom_call_target="tpu_custom_call" | custom-call | flops 23000000512 | tf_op jit(solution)/shard_map/mlp/pallas_call | solution.py:463
  127.0 8.8 %norm_down.1 = (f32[512,768]{1,0:T(8,128)}, bf16[512,768]{1,0:T(8,128)(2,1)}, bf16[512,768]{1,0:T(8,128)(2,1)}, f32[3,768]{1,0:T(4,128)}) custom-call(f32[6,768]{1,0:T(8,128)} %nv_ref.3, f32[512,128]{1,0:T(8,128)} %get-tuple-element.87.inv_ref, f32[512,768]{1,0:T(8,128)} %get-tuple-element.88.unit_hbm, f32[512,768]{1,0:T(8,128)} %get-tuple-element.89.gh2_hbm, ...), custom_call_target="tpu_custom_call" | custom-call | flops 8000000000 | tf_op jit(solution)/shard_map/norm_down/pallas_call | solution.py:534
  135.9 20.0 %attend_back.1 = (bf16[512,768]{1,0:T(8,128)(2,1)}, bf16[512,768]{1,0:T(8,128)(2,1)}, bf16[512,768]{1,0:T(8,128)(2,1)}, bf16[1024,768]{1,0:T(8,128)(2,1)}, f32[2,768]{1,0:T(2,128)}) custom-call(bf16[12,512,512]{2,1,0:T(8,128)(2,1)} %get-tuple-element.86.probs_ref, bf16[512,768]{1,0:T(8,128)(2,1)} %get-tuple-element.91.gm_ref, ...), custom_call_target="tpu_custom_call" | custom-call | flops 28000000000 | tf_op jit(solution)/shard_map/attend_back/pallas_call | solution.py:627
  156.6 1.9 collective-permute-start.19
  159.3 0.9 collective-permute-start.17
  160.2 9.6 %project_back.1 = (bf16[4,4,5,48,384]{4,3,2,1,0:T(8,128)(2,1)}, bf16[4,4,5,48,384]{4,3,2,1,0:T(8,128)(2,1)}) custom-call(s32[1]{0:T(128)} %bitcast.4.core_ref, bf16[512,768]{1,0:T(8,128)(2,1)} %constant_dynamic-slice_fusion.x_ref.x_hbm, bf16[512,768]{1,0:T(8,128)(2,1)} %get-tuple-element.107.gq_ref, bf16[512,768]{1,0:T(8,128)(2,1)} %get-tuple-element.93.gk_ref, ...), custom_call_target="tpu_custom_call" | custom-call | flops 8999999488 | tf_op jit(solution)/shard_map/project_back/pallas_call | solution.py:682
  169.9 5.6 %collective-permute-done.20 = bf16[4,4,5,48,384]{4,3,2,1,0:T(8,128)(2,1)S(1)} collective-permute-done((bf16[4,4,5,48,384]{4,3,2,1,0:T(8,128)(2,1)}, bf16[4,4,5,48,384]{4,3,2,1,0:T(8,128)(2,1)S(1)}, u32[]{:S(2)}, u32[]{:S(2)}) %collective-permute-start.20) | collective-permute-done | bytes 2949152 | tf_op jit(solution)/shard_map/ppermute | solution.py:724
  175.5 4.3 %add_convert_fusion = bf16[4,4,5,48,384]{4,3,2,1,0:T(8,128)(2,1)} fusion(bf16[4,4,5,48,384]{4,3,2,1,0:T(8,128)(2,1)S(1)} %collective-permute-done.20, bf16[4,4,5,48,384]{4,3,2,1,0:T(8,128)(2,1)} %get-tuple-element.103), kind=kLoop, calls=%fused_computation | loop fusion | flops 5898240 | bytes 8847360 | tf_op jit(solution)/shard_map/convert_element_type | solution.py:808
  180.2 1.2 copy-done.5
  181.3 0.9 dynamic-slice_bitcast_fusion
  182.3 1.8 collective-permute-start.23
  184.1 2.0 collective-permute-start.24
  186.1 1.5 collective-permute-start.25
  187.6 6.9 %token_grad.1 = f32[512,768]{1,0:T(8,128)} custom-call(bf16[512,768]{1,0:T(8,128)(2,1)} %get-tuple-element.107.gq_ref, bf16[512,768]{1,0:T(8,128)(2,1)} %get-tuple-element.93.gk_ref, bf16[512,768]{1,0:T(8,128)(2,1)} %get-tuple-element.94.gv_ref, bf16[3,2,768,384]{3,2,1,0:T(8,128)(2,1)} %get-tuple-element.108.w_ref, f32[512,768]{1,0:T(8,128)} %get-tuple-element.109.gh1_ref), custom_call_target="tpu_custom_call" | custom-call | flops 6000000000 | tf_op jit(solution)/shard_map/token_grad/pallas_call | solution.py:707
  194.5 1.2 collective-permute-done.21
  196.4 1.0 slice.74.refs_5_
  197.5 1.0 slice.75.refs_6_
  198.5 2.6 %collective-permute-done.22 = f32[12,768]{1,0:T(8,128)S(1)} collective-permute-done((f32[12,768]{1,0:T(8,128)S(1)}, f32[12,768]{1,0:T(8,128)S(1)}, u32[]{:S(2)}, u32[]{:S(2)}) %collective-permute-start.22) | collective-permute-done | bytes 36896 | tf_op jit(solution)/shard_map/ppermute | solution.py:720
  201.1 4.7 %collective-permute-done.24.refs_2_ = bf16[8,48,384]{2,1,0:T(8,128)(2,1)S(1)} collective-permute-done((bf16[8,48,384]{2,1,0:T(8,128)(2,1)}, bf16[8,48,384]{2,1,0:T(8,128)(2,1)S(1)}, u32[]{:S(2)}, u32[]{:S(2)}) %collective-permute-start.24) | collective-permute-done | bytes 294944 | tf_op jit(solution)/shard_map/ppermute | solution.py:729
  205.9 1.5 collective-permute-start.26
  207.4 1.2 copy-done.3
  208.6 1.2 copy-done.4
  209.8 1.9 adam.2
  212.5 4.0 %reduce-scatter.5.cloned.1.call-done = bf16[1,4,5,48,384]{4,3,2,1,0:T(8,128)(2,1)} async-done(((bf16[4,4,5,48,384]{4,3,2,1,0:T(8,128)(2,1)}), bf16[1,4,5,48,384]{4,3,2,1,0:T(8,128)(2,1)}) %reduce-scatter.5.cloned.1.call-update) | async-done | bytes 737296 | tf_op jit(solution)/shard_map/reduce_scatter | solution.py:815
  216.5 1.3 dynamic-slice_bitcast_fusion.4
  217.7 2.9 %collective-permute-start.27 = (bf16[5,48,384]{2,1,0:T(8,128)(2,1)S(1)}, bf16[5,48,384]{2,1,0:T(8,128)(2,1)S(1)}, u32[]{:S(2)}, u32[]{:S(2)}) collective-permute-start(bf16[5,48,384]{2,1,0:T(8,128)(2,1)S(1)} %get-tuple-element.145), channel_id=1, source_target_pairs={{0,8},{2,10},{4,12},{6,14},{8,16},{10,18},{12,20},{14,22},{16,24},... | collective-permute-start | bytes 552968 | tf_op jit(solution)/shard_map/ppermute | solution.py:729
  220.6 1.0 collective-permute-start.28
  221.7 1.4 collective-permute-start.29
  223.8 3.5 %collective-permute-done.27.refs_1_ = bf16[5,48,384]{2,1,0:T(8,128)(2,1)S(1)} collective-permute-done((bf16[5,48,384]{2,1,0:T(8,128)(2,1)S(1)}, bf16[5,48,384]{2,1,0:T(8,128)(2,1)S(1)}, u32[]{:S(2)}, u32[]{:S(2)}) %collective-permute-start.27) | collective-permute-done | bytes 184352 | tf_op jit(solution)/shard_map/ppermute | solution.py:729
  227.2 6.8 %collective-permute-done.28.refs_2_ = bf16[5,48,384]{2,1,0:T(8,128)(2,1)S(1)} collective-permute-done((bf16[5,48,384]{2,1,0:T(8,128)(2,1)S(1)}, bf16[5,48,384]{2,1,0:T(8,128)(2,1)S(1)}, u32[]{:S(2)}, u32[]{:S(2)}) %collective-permute-start.28) | collective-permute-done | bytes 184352 | tf_op jit(solution)/shard_map/ppermute | solution.py:729
  234.0 1.2 adam.3
  (119 shorter events, 11.5 us)
Async XLA Ops:
  7.2 13.8 %copy-start = (bf16[1024,768]{1,0:T(8,128)(2,1)S(1)}, bf16[1024,768]{1,0:T(8,128)(2,1)}, u32[]{:S(2)}) copy-start(bf16[1024,768]{1,0:T(8,128)(2,1)} %param.12) | copy-start | bytes 4718596
  7.2 94.9 %all-gather.3.cloned.1.call-start = ((), (), s32[]{:S(2)}) async-start(), calls=%async_computation.4 | async-start | bytes 10948608 | tf_op jit(solution)/shard_map/all_gather | solution.py:736
  9.5 170.6 %reduce-scatter.3.cloned.1.call-start = ((), (), s32[]{:S(2)}) async-start(), calls=%async_computation.2 | async-start | bytes 10616832 | tf_op jit(solution)/shard_map/reduce_scatter | solution.py:801
  9.5 20.0 %collective-permute-start = (bf16[4,48,384]{2,1,0:T(8,128)(2,1)S(1)}, bf16[4,48,384]{2,1,0:T(8,128)(2,1)S(1)}, u32[]{:S(2)}, u32[]{:S(2)}) collective-permute-start(bf16[4,48,384]{2,1,0:T(8,128)(2,1)S(1)} %slice.64), channel_id=1, source_target_pairs={{0,8},{2,10},{4,12},{6,14},{8,16},{10,18},{12,20},{14,22},{16,24},... | collective-permute-start | bytes 442376 | tf_op jit(solution)/shard_map/ppermute | solution.py:729
  12.6 16.9 %collective-permute-start.1 = (bf16[4,48,384]{2,1,0:T(8,128)(2,1)S(1)}, bf16[4,48,384]{2,1,0:T(8,128)(2,1)S(1)}, u32[]{:S(2)}, u32[]{:S(2)}) collective-permute-start(bf16[4,48,384]{2,1,0:T(8,128)(2,1)S(1)} %slice.64), channel_id=1, source_target_pairs={{0,16},{2,18},{4,20},{6,22},{8,24},{10,26},{12,28},{14,30},{16,0},... | collective-permute-start | bytes 442376 | tf_op jit(solution)/shard_map/ppermute | solution.py:729
  15.2 14.3 %collective-permute-start.2 = (bf16[4,48,384]{2,1,0:T(8,128)(2,1)S(1)}, bf16[4,48,384]{2,1,0:T(8,128)(2,1)S(1)}, u32[]{:S(2)}, u32[]{:S(2)}) collective-permute-start(bf16[4,48,384]{2,1,0:T(8,128)(2,1)S(1)} %slice.64), channel_id=1, source_target_pairs={{0,24},{2,26},{4,28},{6,30},{8,0},{10,2},{12,4},{14,6},{16,8},{18,... | collective-permute-start | bytes 442376 | tf_op jit(solution)/shard_map/ppermute | solution.py:729
  29.5 43.9 %copy-start.26 = (s32[2]{0:T(128)S(1)}, s32[2]{0:T(128)}, u32[]{:S(2)}) copy-start(s32[2]{0:T(128)} %param.13) | copy-start | bytes 28
  29.7 46.1 %copy-start.6 = (bf16[4,2,48,384]{3,2,1,0:T(8,128)(2,1)}, bf16[4,2,48,384]{3,2,1,0:T(8,128)(2,1)S(1)}, u32[]{:S(2)}) copy-start(bf16[4,2,48,384]{3,2,1,0:T(8,128)(2,1)S(1)} %get-tuple-element.147.refs_1_) | copy-start | bytes 884740
  29.7 46.1 %copy-start.7 = (bf16[4,2,48,384]{3,2,1,0:T(8,128)(2,1)}, bf16[4,2,48,384]{3,2,1,0:T(8,128)(2,1)S(1)}, u32[]{:S(2)}) copy-start(bf16[4,2,48,384]{3,2,1,0:T(8,128)(2,1)S(1)} %get-tuple-element.148.refs_0_) | copy-start | bytes 884740
  29.7 15.8 %collective-permute-start.3 = (bf16[4,2,48,384]{3,2,1,0:T(8,128)(2,1)S(1)}, bf16[4,2,48,384]{3,2,1,0:T(8,128)(2,1)S(1)}, u32[]{:S(2)}, u32[]{:S(2)}) collective-permute-start(bf16[4,2,48,384]{3,2,1,0:T(8,128)(2,1)S(1)} %get-tuple-element.148.refs_0_), channel_id=1, source_target_pairs={{0,1},{1,0},{2,3},{3,2},{4,5},{5,4},{6,7},{7,6},{8,9},{9,8},{10,11... | collective-permute-start | bytes 884744 | tf_op jit(solution)/shard_map/ppermute | solution.py:720
  31.3 14.2 %collective-permute-start.4 = (bf16[4,2,48,384]{3,2,1,0:T(8,128)(2,1)S(1)}, bf16[4,2,48,384]{3,2,1,0:T(8,128)(2,1)S(1)}, u32[]{:S(2)}, u32[]{:S(2)}) collective-permute-start(bf16[4,2,48,384]{3,2,1,0:T(8,128)(2,1)S(1)} %get-tuple-element.147.refs_1_), channel_id=1, source_target_pairs={{0,4},{2,6},{4,0},{6,2},{8,12},{10,14},{12,8},{14,10},{16,20},{18,... | collective-permute-start | bytes 884744 | tf_op jit(solution)/shard_map/ppermute | solution.py:724
  32.8 14.6 %collective-permute-start.5 = (bf16[4,2,48,384]{3,2,1,0:T(8,128)(2,1)S(1)}, bf16[4,2,48,384]{3,2,1,0:T(8,128)(2,1)S(1)}, u32[]{:S(2)}, u32[]{:S(2)}) collective-permute-start(bf16[4,2,48,384]{3,2,1,0:T(8,128)(2,1)S(1)} %get-tuple-element.148.refs_0_), channel_id=1, source_target_pairs={{0,4},{2,6},{4,0},{6,2},{8,12},{10,14},{12,8},{14,10},{16,20},{18,... | collective-permute-start | bytes 884744 | tf_op jit(solution)/shard_map/ppermute | solution.py:724
  33.3 27.0 %collective-permute-start.6 = (bf16[4,2,48,384]{3,2,1,0:T(8,128)(2,1)S(1)}, bf16[4,2,48,384]{3,2,1,0:T(8,128)(2,1)S(1)}, u32[]{:S(2)}, u32[]{:S(2)}) collective-permute-start(bf16[4,2,48,384]{3,2,1,0:T(8,128)(2,1)S(1)} %get-tuple-element.147.refs_1_), channel_id=1, source_target_pairs={{0,1},{1,0},{2,3},{3,2},{4,5},{5,4},{6,7},{7,6},{8,9},{9,8},{10,11... | collective-permute-start | bytes 884744 | tf_op jit(solution)/shard_map/ppermute | solution.py:720
  33.8 26.5 %collective-permute-start.9 = (bf16[4,2,48,384]{3,2,1,0:T(8,128)(2,1)S(1)}, bf16[4,2,48,384]{3,2,1,0:T(8,128)(2,1)S(1)}, u32[]{:S(2)}, u32[]{:S(2)}) collective-permute-start(bf16[4,2,48,384]{3,2,1,0:T(8,128)(2,1)S(1)} %get-tuple-element.148.refs_0_), channel_id=1, source_target_pairs={{0,2},{2,0},{4,6},{6,4},{8,10},{10,8},{12,14},{14,12},{16,18},{18,... | collective-permute-start | bytes 884744 | tf_op jit(solution)/shard_map/ppermute | solution.py:724
  45.5 30.4 %copy-start.17 = (bf16[4,2,48,384]{3,2,1,0:T(8,128)(2,1)}, bf16[4,2,48,384]{3,2,1,0:T(8,128)(2,1)S(1)}, u32[]{:S(2)}) copy-start(bf16[4,2,48,384]{3,2,1,0:T(8,128)(2,1)S(1)} %collective-permute-done.3.refs_2_) | copy-start | bytes 884740
  45.5 15.3 %collective-permute-start.10 = (bf16[4,2,48,384]{3,2,1,0:T(8,128)(2,1)S(1)}, bf16[4,2,48,384]{3,2,1,0:T(8,128)(2,1)S(1)}, u32[]{:S(2)}, u32[]{:S(2)}) collective-permute-start(bf16[4,2,48,384]{3,2,1,0:T(8,128)(2,1)S(1)} %get-tuple-element.147.refs_1_), channel_id=1, source_target_pairs={{0,2},{2,0},{4,6},{6,4},{8,10},{10,8},{12,14},{14,12},{16,18},{18,... | collective-permute-start | bytes 884744 | tf_op jit(solution)/shard_map/ppermute | solution.py:724
  45.5 30.4 %copy-start.18 = (bf16[4,2,48,384]{3,2,1,0:T(8,128)(2,1)}, bf16[4,2,48,384]{3,2,1,0:T(8,128)(2,1)S(1)}, u32[]{:S(2)}) copy-start(bf16[4,2,48,384]{3,2,1,0:T(8,128)(2,1)S(1)} %collective-permute-done.4.refs_3_) | copy-start | bytes 884740
  45.5 15.4 %collective-permute-start.7 = (bf16[4,2,48,384]{3,2,1,0:T(8,128)(2,1)S(1)}, bf16[4,2,48,384]{3,2,1,0:T(8,128)(2,1)S(1)}, u32[]{:S(2)}, u32[]{:S(2)}) collective-permute-start(bf16[4,2,48,384]{3,2,1,0:T(8,128)(2,1)S(1)} %collective-permute-done.3.refs_2_), channel_id=1, source_target_pairs={{0,4},{2,6},{4,0},{6,2},{8,12},{10,14},{12,8},{14,10},{16,20},{18,... | collective-permute-start | bytes 884744 | tf_op jit(solution)/shard_map/ppermute | solution.py:724
  47.4 28.5 %copy-start.19 = (bf16[4,2,48,384]{3,2,1,0:T(8,128)(2,1)}, bf16[4,2,48,384]{3,2,1,0:T(8,128)(2,1)S(1)}, u32[]{:S(2)}) copy-start(bf16[4,2,48,384]{3,2,1,0:T(8,128)(2,1)S(1)} %collective-permute-done.5.refs_4_) | copy-start | bytes 884740
  47.4 24.8 %collective-permute-start.8 = (bf16[4,2,48,384]{3,2,1,0:T(8,128)(2,1)S(1)}, bf16[4,2,48,384]{3,2,1,0:T(8,128)(2,1)S(1)}, u32[]{:S(2)}, u32[]{:S(2)}) collective-permute-start(bf16[4,2,48,384]{3,2,1,0:T(8,128)(2,1)S(1)} %collective-permute-done.4.refs_3_), channel_id=1, source_target_pairs={{0,1},{1,0},{2,3},{3,2},{4,5},{5,4},{6,7},{7,6},{8,9},{9,8},{10,11... | collective-permute-start | bytes 884744 | tf_op jit(solution)/shard_map/ppermute | solution.py:720
  60.3 15.6 %copy-start.20 = (bf16[4,2,48,384]{3,2,1,0:T(8,128)(2,1)}, bf16[4,2,48,384]{3,2,1,0:T(8,128)(2,1)S(1)}, u32[]{:S(2)}) copy-start(bf16[4,2,48,384]{3,2,1,0:T(8,128)(2,1)S(1)} %collective-permute-done.6.refs_5_) | copy-start | bytes 884740
  60.3 11.9 %collective-permute-start.11 = (bf16[4,2,48,384]{3,2,1,0:T(8,128)(2,1)S(1)}, bf16[4,2,48,384]{3,2,1,0:T(8,128)(2,1)S(1)}, u32[]{:S(2)}, u32[]{:S(2)}) collective-permute-start(bf16[4,2,48,384]{3,2,1,0:T(8,128)(2,1)S(1)} %collective-permute-done.3.refs_2_), channel_id=1, source_target_pairs={{0,2},{2,0},{4,6},{6,4},{8,10},{10,8},{12,14},{14,12},{16,18},{18,... | collective-permute-start | bytes 884744 | tf_op jit(solution)/shard_map/ppermute | solution.py:724
  60.3 15.6 %copy-start.21 = (bf16[4,2,48,384]{3,2,1,0:T(8,128)(2,1)}, bf16[4,2,48,384]{3,2,1,0:T(8,128)(2,1)S(1)}, u32[]{:S(2)}) copy-start(bf16[4,2,48,384]{3,2,1,0:T(8,128)(2,1)S(1)} %collective-permute-done.9.refs_8_) | copy-start | bytes 884740
  60.3 15.5 %collective-permute-start.12 = (bf16[4,2,48,384]{3,2,1,0:T(8,128)(2,1)S(1)}, bf16[4,2,48,384]{3,2,1,0:T(8,128)(2,1)}, u32[]{:S(2)}, u32[]{:S(2)}) collective-permute-start(bf16[4,2,48,384]{3,2,1,0:T(8,128)(2,1)S(1)} %collective-permute-done.4.refs_3_), channel_id=1, source_target_pairs={{0,2},{2,0},{4,6},{6,4},{8,10},{10,8},{12,14},{14,12},{16,18},{18,... | collective-permute-start | bytes 884744 | tf_op jit(solution)/shard_map/ppermute | solution.py:724
  60.8 15.1 %copy-start.22 = (bf16[4,2,48,384]{3,2,1,0:T(8,128)(2,1)}, bf16[4,2,48,384]{3,2,1,0:T(8,128)(2,1)S(1)}, u32[]{:S(2)}) copy-start(bf16[4,2,48,384]{3,2,1,0:T(8,128)(2,1)S(1)} %collective-permute-done.10.refs_9_) | copy-start | bytes 884740
  60.8 15.0 %collective-permute-start.13 = (bf16[4,2,48,384]{3,2,1,0:T(8,128)(2,1)S(1)}, bf16[4,2,48,384]{3,2,1,0:T(8,128)(2,1)}, u32[]{:S(2)}, u32[]{:S(2)}) collective-permute-start(bf16[4,2,48,384]{3,2,1,0:T(8,128)(2,1)S(1)} %collective-permute-done.5.refs_4_), channel_id=1, source_target_pairs={{0,2},{2,0},{4,6},{6,4},{8,10},{10,8},{12,14},{14,12},{16,18},{18,... | collective-permute-start | bytes 884744 | tf_op jit(solution)/shard_map/ppermute | solution.py:724
  60.9 15.0 %copy-start.23 = (bf16[4,2,48,384]{3,2,1,0:T(8,128)(2,1)}, bf16[4,2,48,384]{3,2,1,0:T(8,128)(2,1)S(1)}, u32[]{:S(2)}) copy-start(bf16[4,2,48,384]{3,2,1,0:T(8,128)(2,1)S(1)} %collective-permute-done.7.refs_6_) | copy-start | bytes 884740
  60.9 14.9 %collective-permute-start.14 = (bf16[4,2,48,384]{3,2,1,0:T(8,128)(2,1)S(1)}, bf16[4,2,48,384]{3,2,1,0:T(8,128)(2,1)}, u32[]{:S(2)}, u32[]{:S(2)}) collective-permute-start(bf16[4,2,48,384]{3,2,1,0:T(8,128)(2,1)S(1)} %collective-permute-done.6.refs_5_), channel_id=1, source_target_pairs={{0,2},{2,0},{4,6},{6,4},{8,10},{10,8},{12,14},{14,12},{16,18},{18,... | collective-permute-start | bytes 884744 | tf_op jit(solution)/shard_map/ppermute | solution.py:724
  72.2 3.6 %collective-permute-start.15 = (bf16[4,2,48,384]{3,2,1,0:T(8,128)(2,1)S(1)}, bf16[4,2,48,384]{3,2,1,0:T(8,128)(2,1)}, u32[]{:S(2)}, u32[]{:S(2)}) collective-permute-start(bf16[4,2,48,384]{3,2,1,0:T(8,128)(2,1)S(1)} %collective-permute-done.7.refs_6_), channel_id=1, source_target_pairs={{0,2},{2,0},{4,6},{6,4},{8,10},{10,8},{12,14},{14,12},{16,18},{18,... | collective-permute-start | bytes 884744 | tf_op jit(solution)/shard_map/ppermute | solution.py:724
  72.9 2.9 %collective-permute-start.16 = (bf16[4,2,48,384]{3,2,1,0:T(8,128)(2,1)S(1)}, bf16[4,2,48,384]{3,2,1,0:T(8,128)(2,1)}, u32[]{:S(2)}, u32[]{:S(2)}) collective-permute-start(bf16[4,2,48,384]{3,2,1,0:T(8,128)(2,1)S(1)} %collective-permute-done.8.refs_7_), channel_id=1, source_target_pairs={{0,2},{2,0},{4,6},{6,4},{8,10},{10,8},{12,14},{14,12},{16,18},{18,... | collective-permute-start | bytes 884744 | tf_op jit(solution)/shard_map/ppermute | solution.py:724
  127.0 89.5 %reduce-scatter.5.cloned.1.call-start = ((), (), s32[]{:S(2)}) async-start(), calls=%async_computation.3 | async-start | bytes 3686400 | tf_op jit(solution)/shard_map/reduce_scatter | solution.py:815
  135.9 20.0 %copy-start.8 = (f32[7,768]{1,0:T(8,128)S(1)}, f32[7,768]{1,0:T(8,128)}, u32[]{:S(2)}) copy-start(f32[7,768]{1,0:T(8,128)} %get-tuple-element.99) | copy-start | bytes 64516
  135.9 20.0 %copy-start.10 = (f32[3,768]{1,0:T(4,128)S(1)}, f32[3,768]{1,0:T(4,128)}, u32[]{:S(2)}) copy-start(f32[3,768]{1,0:T(4,128)} %get-tuple-element.100) | copy-start | bytes 27652
  156.6 13.1 %collective-permute-start.19 = (f32[12,768]{1,0:T(8,128)S(1)}, f32[12,768]{1,0:T(8,128)S(1)}, u32[]{:S(2)}, u32[]{:S(2)}) collective-permute-start(f32[12,768]{1,0:T(8,128)S(1)} %pad_maximum_fusion.3), channel_id=1, source_target_pairs={{0,24},{2,26},{4,28},{6,30},{8,0},{10,2},{12,4},{14,6},{16,8},{18,... | collective-permute-start | bytes 110600 | tf_op jit(solution)/shard_map/ppermute | solution.py:729
  158.6 11.2 %collective-permute-start.18 = (f32[12,768]{1,0:T(8,128)S(1)}, f32[12,768]{1,0:T(8,128)S(1)}, u32[]{:S(2)}, u32[]{:S(2)}) collective-permute-start(f32[12,768]{1,0:T(8,128)S(1)} %pad_maximum_fusion.3), channel_id=1, source_target_pairs={{0,16},{2,18},{4,20},{6,22},{8,24},{10,26},{12,28},{14,30},{16,0},... | collective-permute-start | bytes 110600 | tf_op jit(solution)/shard_map/ppermute | solution.py:729
  159.3 10.5 %collective-permute-start.17 = (f32[12,768]{1,0:T(8,128)S(1)}, f32[12,768]{1,0:T(8,128)S(1)}, u32[]{:S(2)}, u32[]{:S(2)}) collective-permute-start(f32[12,768]{1,0:T(8,128)S(1)} %pad_maximum_fusion.3), channel_id=1, source_target_pairs={{0,8},{2,10},{4,12},{6,14},{8,16},{10,18},{12,20},{14,22},{16,24},... | collective-permute-start | bytes 110600 | tf_op jit(solution)/shard_map/ppermute | solution.py:729
  169.8 5.7 %collective-permute-start.20 = (bf16[4,4,5,48,384]{4,3,2,1,0:T(8,128)(2,1)}, bf16[4,4,5,48,384]{4,3,2,1,0:T(8,128)(2,1)S(1)}, u32[]{:S(2)}, u32[]{:S(2)}) collective-permute-start(bf16[4,4,5,48,384]{4,3,2,1,0:T(8,128)(2,1)} %get-tuple-element.104), channel_id=1, source_target_pairs={{0,2},{2,0},{4,6},{6,4},{8,10},{10,8},{12,14},{14,12},{16,18},{18,... | collective-permute-start | bytes 8847368 | tf_op jit(solution)/shard_map/ppermute | solution.py:724
  182.3 18.9 %collective-permute-start.23 = (bf16[8,48,384]{2,1,0:T(8,128)(2,1)}, bf16[8,48,384]{2,1,0:T(8,128)(2,1)S(1)}, u32[]{:S(2)}, u32[]{:S(2)}) collective-permute-start(bf16[8,48,384]{2,1,0:T(8,128)(2,1)} %get-tuple-element.113), channel_id=1, source_target_pairs={{0,8},{2,10},{4,12},{6,14},{8,16},{10,18},{12,20},{14,22},{16,24},... | collective-permute-start | bytes 884744 | tf_op jit(solution)/shard_map/ppermute | solution.py:729
  184.1 21.8 %collective-permute-start.24 = (bf16[8,48,384]{2,1,0:T(8,128)(2,1)}, bf16[8,48,384]{2,1,0:T(8,128)(2,1)S(1)}, u32[]{:S(2)}, u32[]{:S(2)}) collective-permute-start(bf16[8,48,384]{2,1,0:T(8,128)(2,1)} %get-tuple-element.114), channel_id=1, source_target_pairs={{0,16},{2,18},{4,20},{6,22},{8,24},{10,26},{12,28},{14,30},{16,0},... | collective-permute-start | bytes 884744 | tf_op jit(solution)/shard_map/ppermute | solution.py:729
  186.1 19.8 %collective-permute-start.25 = (bf16[8,48,384]{2,1,0:T(8,128)(2,1)}, bf16[8,48,384]{2,1,0:T(8,128)(2,1)S(1)}, u32[]{:S(2)}, u32[]{:S(2)}) collective-permute-start(bf16[8,48,384]{2,1,0:T(8,128)(2,1)} %get-tuple-element.115), channel_id=1, source_target_pairs={{0,24},{2,26},{4,28},{6,30},{8,0},{10,2},{12,4},{14,6},{16,8},{18,... | collective-permute-start | bytes 884744 | tf_op jit(solution)/shard_map/ppermute | solution.py:729
  194.4 1.2 collective-permute-start.21
  195.7 5.4 %collective-permute-start.22 = (f32[12,768]{1,0:T(8,128)S(1)}, f32[12,768]{1,0:T(8,128)S(1)}, u32[]{:S(2)}, u32[]{:S(2)}) collective-permute-start(f32[12,768]{1,0:T(8,128)S(1)} %add.139), channel_id=1, source_target_pairs={{0,1},{1,0},{2,3},{3,2},{4,5},{5,4},{6,7},{7,6},{8,9},{9,8},{10,11... | collective-permute-start | bytes 110600 | tf_op jit(solution)/shard_map/ppermute | solution.py:720
  205.9 5.8 %collective-permute-start.26 = (f32[12,768]{1,0:T(8,128)S(1)}, f32[12,768]{1,0:T(8,128)S(1)}, u32[]{:S(2)}, u32[]{:S(2)}) collective-permute-start(f32[12,768]{1,0:T(8,128)S(1)} %add.140), channel_id=1, source_target_pairs={{0,4},{2,6},{4,0},{6,2},{8,12},{10,14},{12,8},{14,10},{16,20},{18,... | collective-permute-start | bytes 110600 | tf_op jit(solution)/shard_map/ppermute | solution.py:724
  211.7 11.5 %copy-start.12 = (f32[6,768]{1,0:T(8,128)S(1)}, f32[6,768]{1,0:T(8,128)}, u32[]{:S(2)}) copy-start(f32[6,768]{1,0:T(8,128)} %param.21) | copy-start | bytes 55300
  211.7 11.5 %copy-start.13 = (f32[6,768]{1,0:T(8,128)S(1)}, f32[6,768]{1,0:T(8,128)}, u32[]{:S(2)}) copy-start(f32[6,768]{1,0:T(8,128)} %param.22) | copy-start | bytes 55300
  217.7 9.5 %collective-permute-start.27 = (bf16[5,48,384]{2,1,0:T(8,128)(2,1)S(1)}, bf16[5,48,384]{2,1,0:T(8,128)(2,1)S(1)}, u32[]{:S(2)}, u32[]{:S(2)}) collective-permute-start(bf16[5,48,384]{2,1,0:T(8,128)(2,1)S(1)} %get-tuple-element.145), channel_id=1, source_target_pairs={{0,8},{2,10},{4,12},{6,14},{8,16},{10,18},{12,20},{14,22},{16,24},... | collective-permute-start | bytes 552968 | tf_op jit(solution)/shard_map/ppermute | solution.py:729
  220.6 13.4 %collective-permute-start.28 = (bf16[5,48,384]{2,1,0:T(8,128)(2,1)S(1)}, bf16[5,48,384]{2,1,0:T(8,128)(2,1)S(1)}, u32[]{:S(2)}, u32[]{:S(2)}) collective-permute-start(bf16[5,48,384]{2,1,0:T(8,128)(2,1)S(1)} %get-tuple-element.144), channel_id=1, source_target_pairs={{0,16},{2,18},{4,20},{6,22},{8,24},{10,26},{12,28},{14,30},{16,0},... | collective-permute-start | bytes 552968 | tf_op jit(solution)/shard_map/ppermute | solution.py:729
  221.7 12.4 %collective-permute-start.29 = (bf16[5,48,384]{2,1,0:T(8,128)(2,1)S(1)}, bf16[5,48,384]{2,1,0:T(8,128)(2,1)S(1)}, u32[]{:S(2)}, u32[]{:S(2)}) collective-permute-start(bf16[5,48,384]{2,1,0:T(8,128)(2,1)S(1)} %get-tuple-element.143), channel_id=1, source_target_pairs={{0,24},{2,26},{4,28},{6,30},{8,0},{10,2},{12,4},{14,6},{16,8},{18,... | collective-permute-start | bytes 552968 | tf_op jit(solution)/shard_map/ppermute | solution.py:729
  (12 other events, 70.5 us)
Sparse Core Ops, SparseCore 0:
  10.2 91.8 all-gather.2
  127.1 52.8 reduce-scatter.2
  182.4 34.0 reduce-scatter.4

commit v2 on v1

--- a/solution.py
+++ b/solution.py
@@ -101,7 +101,7 @@
     return jnp.concatenate([w_ref[0], w_ref[1]], axis=1)
 
 
-RING = ((0, 0, 0), (0, 0, 1), (0, 1, 1), (0, 1, 0), (1, 1, 0), (1, 1, 1), (1, 0, 1), (1, 0, 0))
+RING = ((0, 0, 0), (0, 0, 1), (0, 1, 0), (0, 1, 1), (1, 1, 0), (1, 1, 1), (1, 0, 0), (1, 0, 1))
 
 
 SQUARE = ((0, 0), (0, 1), (1, 1), (1, 0))
@@ -148,6 +148,26 @@
             lower, upper = low[top : top + rows, columns], low[top + rows : top + 2 * rows, columns]
             keep_ref[place, line] = jnp.where(core == 0, lower, upper)
             send_ref[place, line] = jnp.where(core == 0, upper, lower)
+
+
+def round_kernel(shard_ref, low_ref, feed_ref):
+    low_ref[...] = shard_ref[0:4].astype(BF)
+    feed_ref[0:8] = shard_ref[5:13].astype(BF)
+    feed_ref[8] = shard_ref[4].astype(BF)
+
+
+def round_shard(shard):
+    rest = shard.shape[1:]
+    return pl.pallas_call(
+        round_kernel,
+        grid=(1,),
+        in_specs=[whole(shard.shape)],
+        out_specs=[whole((4,) + rest), whole((9,) + rest)],
+        out_shape=[jax.ShapeDtypeStruct((n,) + rest, BF) for n in (4, 9)],
+        compiler_params=params(16),
+        cost_estimate=cost(1),
+        name="round_shard",
+    )(shard)
 
 
 def project_kernel(x_ref, w_ref, vec_ref, sine_ref, qc_ref, qp_ref, k_ref, v_ref, rel_ref):
@@ -550,7 +570,7 @@
 
 def attend_back_kernel(
     probs_ref, gm_ref, qc_ref, qp_ref, k_ref, v_ref, rel_ref,
-    gq_ref, gk_ref, gv_ref, grel_ref, sums_ref,
+    gqkv_ref, grel_ref, sums_ref,
     rel_acc,
 ):
     length, pair = gm_ref.shape
@@ -605,13 +625,13 @@
         high = p.astype(BF)
         rest = (p - high.astype(F32)).astype(BF)
         straight = mm(flip, high) + mm(flip, rest)
-        gq_ref[pl.ds(top, block), :] = (c + straight).astype(BF)
+        gqkv_ref[0, pl.ds(top, block), :] = (c + straight).astype(BF)
         e = jnp.sum(c, axis=0, keepdims=True)
         f = jnp.sum(p, axis=0, keepdims=True)
         sum_c = e if sum_c is None else sum_c + e
         sum_p = f if sum_p is None else sum_p + f
-    gk_ref[...] = gk.astype(BF)
-    gv_ref[...] = gv.astype(BF)
+    gqkv_ref[1] = gk.astype(BF)
+    gqkv_ref[2] = gv.astype(BF)
     grel_ref[...] = rel_acc[...].astype(BF)
     sums_ref[0:1] = sum_c
     sums_ref[1:2] = sum_p
@@ -623,14 +643,17 @@
     heads = width // HEAD_FEATURES
     column = pl.BlockSpec((length, pair), lambda p: (0, p))
     tall = pl.BlockSpec((rel.shape[0], pair), lambda p: (0, p))
-    token = jax.ShapeDtypeStruct((length, width), BF)
     return pl.pallas_call(
         attend_back_kernel,
         grid=(heads // 2,),
         in_specs=[pl.BlockSpec((2, length, length), lambda p: (p, 0, 0))] + [column] * 5 + [tall],
-        out_specs=[column, column, column, tall, pl.BlockSpec((2, pair), lambda p: (0, p))],
+        out_specs=[
+            pl.BlockSpec((3, length, pair), lambda p: (0, 0, p)),
+            tall,
+            pl.BlockSpec((2, pair), lambda p: (0, p)),
+        ],
         out_shape=[
-            token, token, token,
+            jax.ShapeDtypeStruct((3, length, width), BF),
             jax.ShapeDtypeStruct(rel.shape, BF),
             jax.ShapeDtypeStruct((2, width), F32),
         ],
@@ -642,10 +665,12 @@
 
 
 def project_back_kernel(
-    core_ref, x_ref, gq_ref, gk_ref, gv_ref, grel_ref, sine_ref, gattn_ref, mixed_ref, *refs,
+    core_ref, x_ref, gqkv_ref, grel_hbm, sine_hbm, gattn_hbm, mixed_hbm, *refs,
 ):
-    *gw_refs, turned_ref = refs
+    *gw_refs, turned_ref, grel_ref, sine_ref, gattn_ref, mixed_ref, sem = refs
     step = pl.program_id(0)
+    late = (grel_hbm, grel_ref), (sine_hbm, sine_ref), (gattn_hbm, gattn_ref), (mixed_hbm, mixed_ref)
+    late = [pltpu.make_async_copy(*pair, sem.at[i]) for i, pair in enumerate(late)]
 
     def store(value):
         if len(gw_refs) == 2:
@@ -655,16 +680,18 @@
 
     @pl.when(step == 0)
     def _():
+        for copy in late:
+            copy.start()
         turned_ref[...] = x_ref[...].T
 
-    for which, g_ref in enumerate((gq_ref, gk_ref, gv_ref)):
-
-        @pl.when(step == which)
-        def _():
-            store(mm(turned_ref[...], g_ref[...]))
+    @pl.when(step < 3)
+    def _():
+        store(mm(turned_ref[...], gqkv_ref[...]))
 
     @pl.when(step == 3)
     def _():
+        for copy in late:
+            copy.wait()
         store(mm(sine_ref[...], grel_ref[...], TN))
 
     @pl.when(step == 4)
@@ -672,9 +699,8 @@
         store(mm(gattn_ref[...], mixed_ref[...], TN))
 
 
-def project_back(core, x, gq, gk, gv, grel, sine, gattn, mixed, lines, rows):
+def project_back(core, x, gqkv, grel, sine, gattn, mixed, lines, rows):
     length, width = x.shape
-    one = held((length, width))
     if layered(lines, rows):
         shapes = [(len(SQUARE), lines, 5, rows, width // 2)] * 2
     else:
@@ -684,36 +710,40 @@
         grid=(5,),
         in_specs=[
             pl.BlockSpec(memory_space=pltpu.SMEM),
-            one, one, one, one, held(grel.shape), held(sine.shape), one, one,
-        ],
+            held((length, width)),
+            pl.BlockSpec((None, length, width), lambda b: (jnp.minimum(b, 2), 0, 0)),
+        ]
+        + [pl.BlockSpec(memory_space=pl.ANY)] * 4,
         out_specs=[grad_spec(shape) for shape in shapes],
         out_shape=[jax.ShapeDtypeStruct(shape, BF) for shape in shapes],
-        scratch_shapes=[pltpu.VMEM((width, length), BF)],
+        scratch_shapes=[pltpu.VMEM((width, length), BF)]
+        + [pltpu.VMEM(a.shape, BF) for a in (grel, sine, gattn, mixed)]
+        + [pltpu.SemaphoreType.DMA((4,))],
         compiler_params=params(VMEM_MB),
         cost_estimate=cost(9),
         name="project_back",
-    )(core, x, gq, gk, gv, grel, sine, gattn, mixed)
-
-
-def token_grad_kernel(gq_ref, gk_ref, gv_ref, w_ref, gh1_ref, gtok_ref):
+    )(core, x, gqkv, grel, sine, gattn, mixed)
+
+
+def token_grad_kernel(gqkv_ref, w_ref, gh1_ref, gtok_ref):
     total = gh1_ref[...]
-    for i, g_ref in enumerate((gq_ref, gk_ref, gv_ref)):
-        total += mm(g_ref[...], full_matrix(w_ref.at[i]), NT)
+    for i in range(3):
+        total += mm(gqkv_ref[i], full_matrix(w_ref.at[i]), NT)
     gtok_ref[...] = total
 
 
-def token_grad(gq, gk, gv, w, gh1):
-    one = whole(gq.shape)
+def token_grad(gqkv, w, gh1):
+    one = whole(gh1.shape)
     return pl.pallas_call(
         token_grad_kernel,
         grid=(1,),
-        in_specs=[one, one, one, whole((3,) + w.shape[1:]), one],
+        in_specs=[whole(gqkv.shape), whole((3,) + w.shape[1:]), one],
         out_specs=one,
-        out_shape=jax.ShapeDtypeStruct(gq.shape, F32),
+        out_shape=jax.ShapeDtypeStruct(gh1.shape, F32),
         compiler_params=params(VMEM_MB),
         cost_estimate=cost(6),
         name="token_grad",
-    )(gq, gk, gv, w, gh1)
+    )(gqkv, w, gh1)
 
 
 def swap_x(value):
@@ -922,11 +952,11 @@
     used = lax.dynamic_slice_in_dim(lengths, mp_index, 1, 0)
     sine = relative_embedding(seq_len, model_width).astype(BF)
     shard = weights.transpose(1, 0, 2)
-    shard_low = shard.astype(BF)
+    shard_low, shard_feed = round_shard(shard)
     heads_all = lax.all_gather(head_vecs, "mp", axis=1, tiled=True)
-    w_feed = gather_matrices(jnp.concatenate([shard_low[5:13], shard_low[4:5]]))
-    near, (x, sine, heads_all) = gather_lines(shard_low[0:4], (x, sine, heads_all))
-    parts = gather_stepwise(near, shard_low[0:4])
+    w_feed = gather_matrices(shard_feed)
+    near, (x, sine, heads_all) = gather_lines(shard_low, (x, sine, heads_all))
+    parts = gather_stepwise(near, shard_low)
 
     qc, qp, k, v, rel, w = project_parts(x, parts, heads_all[0:2], sine, own_place())
     probs, mixed = attend(used, qc, qp, k, v, rel)
@@ -936,11 +966,11 @@
     )
     part_feed = scatter_plane(gw_feed)
     gh1, gattn, gmixed, sums1 = norm_down(gh2, ghid, unit, inv, norm_vecs, w_feed)
-    gq, gk, gv, grel, sums_q = attend_back(probs, gmixed, qc, qp, k, v, rel)
+    gqkv, grel, sums_q = attend_back(probs, gmixed, qc, qp, k, v, rel)
     small = sum_line(jnp.concatenate([sums2, sums1, sums_q], axis=0))
     place = own_place()
     gproj = project_back(
-        place[3:4], x, gq, gk, gv, grel, sine, gattn, mixed, lines, weight_rows
+        place[3:4], x, gqkv, grel, sine, gattn, mixed, lines, weight_rows
     )
     *gproj, small = lax.optimization_barrier((*gproj, small))
     if len(gproj) == 2:
@@ -950,8 +980,8 @@
         part_proj = scatter_plane(gproj)
 
     pieces_feed = line_pieces(part_feed)
-    *pieces_feed, gq = lax.optimization_barrier((*pieces_feed, gq))
-    grad_tokens = token_grad(gq, gk, gv, w, gh1)
+    *pieces_feed, gqkv = lax.optimization_barrier((*pieces_feed, gqkv))
+    grad_tokens = token_grad(gqkv, w, gh1)
     pieces_feed = trade_pieces(pieces_feed)
     small, grad_tokens = lax.optimization_barrier((small, grad_tokens))
     small, pieces_feed = sum_plane(small, pieces_feed)

time: 245 us -> 244 us (level)
    pallas_call x1 -> x2, Pallas kernels: 6.86 us -> 7.63 us  [the longest x1 6.85 us: token_grad(): pl.pallas_call(token_grad_kernel, grid=(1,), in_specs=[whole(gqkv.shape),...]
    unnamed x54 -> x56, local copies, waits for them, and re-layouts: 5.03 us -> 5.58 us
  transfers between devices with their start and end apart: 33 -> 33, of which waited for: 11 -> 10; matrix products, arithmetic and copies ran while one was open for 8% -> 9% of each run, Pallas kernels for 30% -> 30%
where the time goes in v2:
time: 244 us; the launch traced here: 241 us
  Pallas kernels  98.2 us (40%)
  waiting for transfers between devices  52.3 us (21%)
  starting transfers between devices  44.8 us (18%)
  other arithmetic  14.8 us (6%)
  between operations  14.3 us (6%)
  local copies, waits for them, and re-layouts  12.7 us (5%)
  blocking collectives  4.39 us (2%)
    pallas_call x1, Pallas kernels, mlp(): pl.pallas_call(functools.partial(mlp_kernel, blocks), grid=(1,), in_specs...  24.8 us
    ppermute x4, waiting for transfers between devices, swap_x(): return lax.ppermute(value, 'mp', [(0, 1), (1, 0)])  24.1 us
    ppermute x12, starting transfers between devices, shift_line(): lax.ppermute(value, 'dp', [(d, (d + 4 * step) % dp) for d in range(dp)])  21.1 us
    pallas_call x1, Pallas kernels, attend_back(): pl.pallas_call(attend_back_kernel, grid=(heads // 2,), in_specs=[pl.Block...  20.1 us
    ppermute x4, starting transfers between devices, swap_x(): return lax.ppermute(value, 'mp', [(0, 1), (1, 0)])  17.2 us
    pallas_call x1, Pallas kernels, attend(): pl.pallas_call(attend_kernel, grid=(heads // 2,), in_specs=[pl.BlockSpec(...  15.8 us
    ppermute x12, waiting for transfers between devices, shift_line(): lax.ppermute(value, 'dp', [(d, (d + 4 * step) % dp) for d in range(dp)])  15.4 us
    pallas_call x1, Pallas kernels, project_back(): pl.pallas_call(project_back_kernel, grid=(5,), in_specs=[pl.BlockSpec(mem...  9.41 us
  transfers between devices with their start and end apart: 33, of which 10 were waited for; matrix products, arithmetic and copies ran while one was open for 9% of the time, Pallas kernels for 30%

profile of v2, /device:TPU:0, one launch (start us, length us, event | category | flops | bytes accessed | tf_op | source)
XLA Modules:
  0.0 241.4 jit_solution(12609609601486700814)
XLA Ops:
  7.3 1.3 copy-done.2
  9.4 3.1 %collective-permute-start = (bf16[4,48,384]{2,1,0:T(8,128)(2,1)S(1)}, bf16[4,48,384]{2,1,0:T(8,128)(2,1)S(1)}, u32[]{:S(2)}, u32[]{:S(2)}) collective-permute-start(bf16[4,48,384]{2,1,0:T(8,128)(2,1)S(1)} %get-tuple-element.76), channel_id=1, source_target_pairs={{0,8},{2,10},{4,12},{6,14},{8,16},{10,18},{12,20},{14,22},{16,24},... | collective-permute-start | bytes 442376 | tf_op jit(solution)/shard_map/ppermute | solution.py:759
  12.5 2.6 %collective-permute-start.1 = (bf16[4,48,384]{2,1,0:T(8,128)(2,1)S(1)}, bf16[4,48,384]{2,1,0:T(8,128)(2,1)S(1)}, u32[]{:S(2)}, u32[]{:S(2)}) collective-permute-start(bf16[4,48,384]{2,1,0:T(8,128)(2,1)S(1)} %get-tuple-element.76), channel_id=1, source_target_pairs={{0,16},{2,18},{4,20},{6,22},{8,24},{10,26},{12,28},{14,30},{16,0},... | collective-permute-start | bytes 442376 | tf_op jit(solution)/shard_map/ppermute | solution.py:759
  15.1 1.4 collective-permute-start.2
  16.4 4.4 %all_gather.9 = f32[6,768]{1,0:T(8,128)S(1)} all-gather(f32[6,384]{1,0:T(8,128)S(1)} %copy-done.10), channel_id=1, replica_groups=mesh['dp'=16,'mp'=2] {'mp'}, dimensions={1}, use_global_device_ids=true | all-gather | bytes 27648 | tf_op jit(solution)/shard_map/all_gather | solution.py:956
  20.8 0.9 constant_dynamic-slice_fusion.x_ref.x_hbm
  21.8 6.3 %fusion = (bf16[1024,384]{1,0:T(8,128)(2,1)S(1)}, bf16[1024,384]{1,0:T(8,128)(2,1)S(1)}) fusion(f32[384]{0:T(512)S(1)} %negate_power_fusion, f32[1024]{0:T(1024)S(1)} %subtract_convert_fusion), kind=kLoop, calls=%fused_computation.3 | loop fusion | flops 1179648 | bytes 1578496 | tf_op jit(solution)/shard_map/convert
  28.1 1.3 pad_maximum_fusion.sine_ref.sine_hbm
  29.6 1.6 collective-permute-start.3
  31.2 1.5 collective-permute-start.4
  33.7 11.6 %collective-permute-done.3.refs_2_ = bf16[4,2,48,384]{3,2,1,0:T(8,128)(2,1)S(1)} collective-permute-done((bf16[4,2,48,384]{3,2,1,0:T(8,128)(2,1)S(1)}, bf16[4,2,48,384]{3,2,1,0:T(8,128)(2,1)S(1)}, u32[]{:S(2)}, u32[]{:S(2)}) %collective-permute-start.3) | collective-permute-done | bytes 294944 | tf_op jit(solution)/shard_map/ppermute | solution.py:750
  45.4 1.6 collective-permute-start.7
  47.0 13.4 %collective-permute-start.8 = (bf16[4,2,48,384]{3,2,1,0:T(8,128)(2,1)S(1)}, bf16[4,2,48,384]{3,2,1,0:T(8,128)(2,1)S(1)}, u32[]{:S(2)}, u32[]{:S(2)}) collective-permute-start(bf16[4,2,48,384]{3,2,1,0:T(8,128)(2,1)S(1)} %collective-permute-done.4.refs_3_), channel_id=1, source_target_pairs={{0,1},{1,0},{2,3},{3,2},{4,5},{5,4},{6,7},{7,6},{8,9},{9,8},{10,11... | collective-permute-start | bytes 884744 | tf_op jit(solution)/shard_map/ppermute | solution.py:750
  61.4 10.8 %collective-permute-done.8.refs_7_ = bf16[4,2,48,384]{3,2,1,0:T(8,128)(2,1)S(1)} collective-permute-done((bf16[4,2,48,384]{3,2,1,0:T(8,128)(2,1)S(1)}, bf16[4,2,48,384]{3,2,1,0:T(8,128)(2,1)S(1)}, u32[]{:S(2)}, u32[]{:S(2)}) %collective-permute-start.8) | collective-permute-done | bytes 294944 | tf_op jit(solution)/shard_map/ppermute | solution.py:750
  75.3 8.6 %project.1 = (bf16[512,768]{1,0:T(8,128)(2,1)}, bf16[512,768]{1,0:T(8,128)(2,1)}, bf16[512,768]{1,0:T(8,128)(2,1)}, bf16[512,768]{1,0:T(8,128)(2,1)}, bf16[1024,...) custom-call(s32[4]{0:T(128)} %pad_add_fusion.place_ref, bf16[512,768]{1,0:T(8,128)(2,1)} %constant_dynamic-slice_fusion.x_ref.x_hbm, ...), custom_call_target="tpu_custom_call" | custom-call | flops 8999999488 | tf_op jit(solution)/shard_map/project/pallas_call | solution.py:285
  83.9 15.8 %attend.1 = (bf16[12,512,512]{2,1,0:T(8,128)(2,1)}, bf16[512,768]{1,0:T(8,128)(2,1)}) custom-call(s32[1]{0:T(128)} %dynamic_slice.36.len_ref, bf16[512,768]{1,0:T(8,128)(2,1)} %get-tuple-element.80.qc_ref, bf16[512,768]{1,0:T(8,128)(2,1)} %get-tuple-element.81.qp_ref, bf16[512,768]{1,0:T(8,128)(2,1)} %get-tuple-element.82.k_ref, ...), custom_call_target="tpu_custom_call" | custom-call | flops 19000000512 | tf_op jit(solution)/shard_map/attend/pallas_call | solution.py:343
  99.8 2.2 all-gather.3.cloned.1.call-done
  101.9 24.8 %mlp.1 = (bf16[512,768]{1,0:T(8,128)(2,1)}, f32[512,768]{1,0:T(8,128)}, f32[512,128]{1,0:T(8,128)}, f32[512,768]{1,0:T(8,128)}, bf16[8,4,8,48,384]{4,3,2,1,0:T(8...) custom-call(f32[6,768]{1,0:T(8,128)} %nv_ref.3, f32[4,1,768]{2,1,0:T(1,128)} %reshape.37.hb_ref, ...), custom_call_target="tpu_custom_call" | custom-call | flops 23000000512 | tf_op jit(solution)/shard_map/mlp/pallas_call | solution.py:483
  126.7 8.9 %norm_down.1 = (f32[512,768]{1,0:T(8,128)}, bf16[512,768]{1,0:T(8,128)(2,1)}, bf16[512,768]{1,0:T(8,128)(2,1)}, f32[3,768]{1,0:T(4,128)}) custom-call(f32[6,768]{1,0:T(8,128)} %nv_ref.3, f32[512,128]{1,0:T(8,128)} %get-tuple-element.89.inv_ref, f32[512,768]{1,0:T(8,128)} %get-tuple-element.90.unit_hbm, f32[512,768]{1,0:T(8,128)} %get-tuple-element.91.gh2_hbm, ...), custom_call_target="tpu_custom_call" | custom-call | flops 8000000000 | tf_op jit(solution)/shard_map/norm_down/pallas_call | solution.py:554
  135.6 20.1 %attend_back.1 = (bf16[3,512,768]{2,1,0:T(8,128)(2,1)}, bf16[1024,768]{1,0:T(8,128)(2,1)}, f32[2,768]{1,0:T(2,128)}) custom-call(bf16[12,512,512]{2,1,0:T(8,128)(2,1)} %get-tuple-element.88.probs_ref, bf16[512,768]{1,0:T(8,128)(2,1)} %get-tuple-element.93.gm_ref, bf16[512,768]{1,0:T(8,128)(2,1)} %get-tuple-element.80.qc_ref, ...), custom_call_target="tpu_custom_call" | custom-call | flops 28000000000 | tf_op jit(solution)/shard_map/attend_back/pallas_call | solution.py:646
  156.5 1.9 collective-permute-start.19
  160.0 9.4 %project_back.1 = (bf16[4,4,5,48,384]{4,3,2,1,0:T(8,128)(2,1)}, bf16[4,4,5,48,384]{4,3,2,1,0:T(8,128)(2,1)}) custom-call(s32[1]{0:T(128)} %bitcast.4.core_ref, bf16[512,768]{1,0:T(8,128)(2,1)} %constant_dynamic-slice_fusion.x_ref.x_hbm, bf16[3,512,768]{2,1,0:T(8,128)(2,1)} %get-tuple-element.107.gqkv_ref, bf16[1024,768]{1,0:T(8,128)(2,1)} %get-tuple-element.95.grel_hbm, ...), custom_call_target="tpu_custom_call" | custom-call | flops 8999999488 | tf_op jit(solution)/shard_map/project_back/pallas_call | solution.py:708
  169.5 5.6 %collective-permute-done.20 = bf16[4,4,5,48,384]{4,3,2,1,0:T(8,128)(2,1)S(1)} collective-permute-done((bf16[4,4,5,48,384]{4,3,2,1,0:T(8,128)(2,1)}, bf16[4,4,5,48,384]{4,3,2,1,0:T(8,128)(2,1)S(1)}, u32[]{:S(2)}, u32[]{:S(2)}) %collective-permute-start.20) | collective-permute-done | bytes 2949152 | tf_op jit(solution)/shard_map/ppermute | solution.py:754
  175.1 4.3 %add_convert_fusion = bf16[4,4,5,48,384]{4,3,2,1,0:T(8,128)(2,1)} fusion(bf16[4,4,5,48,384]{4,3,2,1,0:T(8,128)(2,1)S(1)} %collective-permute-done.20, bf16[4,4,5,48,384]{4,3,2,1,0:T(8,128)(2,1)} %get-tuple-element.103), kind=kLoop, calls=%fused_computation | loop fusion | flops 5898240 | bytes 8847360 | tf_op jit(solution)/shard_map/convert_element_type | solution.py:838
  179.6 1.2 copy-done.6
  180.7 0.9 dynamic-slice_bitcast_fusion
  181.7 1.8 collective-permute-start.23
  183.4 1.8 collective-permute-start.24
  185.3 1.3 collective-permute-start.25
  186.6 6.9 %token_grad.1 = f32[512,768]{1,0:T(8,128)} custom-call(bf16[3,512,768]{2,1,0:T(8,128)(2,1)} %get-tuple-element.107.gqkv_ref, bf16[3,2,768,384]{3,2,1,0:T(8,128)(2,1)} %get-tuple-element.108.w_ref, f32[512,768]{1,0:T(8,128)} %get-tuple-element.109.gh1_ref), custom_call_target="tpu_custom_call" | custom-call | flops 6000000000 | tf_op jit(solution)/shard_map/token_grad/pallas_call | solution.py:737
  193.5 1.2 collective-permute-done.21
  194.7 1.7 collective-permute-start.22
  196.4 1.0 slice.59.refs_5_
  197.4 1.0 slice.60.refs_6_
  198.4 1.7 collective-permute-done.22
  200.2 5.3 %collective-permute-done.24.refs_2_ = bf16[8,48,384]{2,1,0:T(8,128)(2,1)S(1)} collective-permute-done((bf16[8,48,384]{2,1,0:T(8,128)(2,1)}, bf16[8,48,384]{2,1,0:T(8,128)(2,1)S(1)}, u32[]{:S(2)}, u32[]{:S(2)}) %collective-permute-start.24) | collective-permute-done | bytes 294944 | tf_op jit(solution)/shard_map/ppermute | solution.py:759
  205.5 1.2 collective-permute-start.26
  206.7 1.2 copy-done.4
  207.9 1.2 copy-done.5
  209.1 1.9 adam.2
  211.8 3.7 %reduce-scatter.5.cloned.1.call-done = bf16[1,4,5,48,384]{4,3,2,1,0:T(8,128)(2,1)} async-done(((bf16[4,4,5,48,384]{4,3,2,1,0:T(8,128)(2,1)}), bf16[1,4,5,48,384]{4,3,2,1,0:T(8,128)(2,1)}) %reduce-scatter.5.cloned.1.call-update) | async-done | bytes 737296 | tf_op jit(solution)/shard_map/reduce_scatter | solution.py:845
  215.5 1.3 dynamic-slice_bitcast_fusion.4
  216.8 3.1 %collective-permute-start.27 = (bf16[5,48,384]{2,1,0:T(8,128)(2,1)S(1)}, bf16[5,48,384]{2,1,0:T(8,128)(2,1)S(1)}, u32[]{:S(2)}, u32[]{:S(2)}) collective-permute-start(bf16[5,48,384]{2,1,0:T(8,128)(2,1)S(1)} %get-tuple-element.145), channel_id=1, source_target_pairs={{0,8},{2,10},{4,12},{6,14},{8,16},{10,18},{12,20},{14,22},{16,24},... | collective-permute-start | bytes 552968 | tf_op jit(solution)/shard_map/ppermute | solution.py:759
  219.9 1.1 collective-permute-start.28
  221.0 1.3 collective-permute-start.29
  223.0 3.2 %collective-permute-done.27.refs_1_ = bf16[5,48,384]{2,1,0:T(8,128)(2,1)S(1)} collective-permute-done((bf16[5,48,384]{2,1,0:T(8,128)(2,1)S(1)}, bf16[5,48,384]{2,1,0:T(8,128)(2,1)S(1)}, u32[]{:S(2)}, u32[]{:S(2)}) %collective-permute-start.27) | collective-permute-done | bytes 184352 | tf_op jit(solution)/shard_map/ppermute | solution.py:759
  226.2 6.8 %collective-permute-done.28.refs_2_ = bf16[5,48,384]{2,1,0:T(8,128)(2,1)S(1)} collective-permute-done((bf16[5,48,384]{2,1,0:T(8,128)(2,1)S(1)}, bf16[5,48,384]{2,1,0:T(8,128)(2,1)S(1)}, u32[]{:S(2)}, u32[]{:S(2)}) %collective-permute-start.28) | collective-permute-done | bytes 184352 | tf_op jit(solution)/shard_map/ppermute | solution.py:759
  233.1 1.2 adam.3
  (117 shorter events, 10.8 us)
Async XLA Ops:
  7.2 94.7 %all-gather.3.cloned.1.call-start = ((), (), s32[]{:S(2)}) async-start(), calls=%async_computation.4 | async-start | bytes 10948608 | tf_op jit(solution)/shard_map/all_gather | solution.py:766
  9.3 170.1 %reduce-scatter.3.cloned.1.call-start = ((), (), s32[]{:S(2)}) async-start(), calls=%async_computation.2 | async-start | bytes 10616832 | tf_op jit(solution)/shard_map/reduce_scatter | solution.py:831
  9.4 20.0 %collective-permute-start = (bf16[4,48,384]{2,1,0:T(8,128)(2,1)S(1)}, bf16[4,48,384]{2,1,0:T(8,128)(2,1)S(1)}, u32[]{:S(2)}, u32[]{:S(2)}) collective-permute-start(bf16[4,48,384]{2,1,0:T(8,128)(2,1)S(1)} %get-tuple-element.76), channel_id=1, source_target_pairs={{0,8},{2,10},{4,12},{6,14},{8,16},{10,18},{12,20},{14,22},{16,24},... | collective-permute-start | bytes 442376 | tf_op jit(solution)/shard_map/ppermute | solution.py:759
  12.5 16.9 %collective-permute-start.1 = (bf16[4,48,384]{2,1,0:T(8,128)(2,1)S(1)}, bf16[4,48,384]{2,1,0:T(8,128)(2,1)S(1)}, u32[]{:S(2)}, u32[]{:S(2)}) collective-permute-start(bf16[4,48,384]{2,1,0:T(8,128)(2,1)S(1)} %get-tuple-element.76), channel_id=1, source_target_pairs={{0,16},{2,18},{4,20},{6,22},{8,24},{10,26},{12,28},{14,30},{16,0},... | collective-permute-start | bytes 442376 | tf_op jit(solution)/shard_map/ppermute | solution.py:759
  15.1 14.3 %collective-permute-start.2 = (bf16[4,48,384]{2,1,0:T(8,128)(2,1)S(1)}, bf16[4,48,384]{2,1,0:T(8,128)(2,1)S(1)}, u32[]{:S(2)}, u32[]{:S(2)}) collective-permute-start(bf16[4,48,384]{2,1,0:T(8,128)(2,1)S(1)} %get-tuple-element.76), channel_id=1, source_target_pairs={{0,24},{2,26},{4,28},{6,30},{8,0},{10,2},{12,4},{14,6},{16,8},{18,... | collective-permute-start | bytes 442376 | tf_op jit(solution)/shard_map/ppermute | solution.py:759
  28.1 44.7 %copy-start.27 = (s32[2]{0:T(128)S(1)}, s32[2]{0:T(128)}, u32[]{:S(2)}) copy-start(s32[2]{0:T(128)} %param.13) | copy-start | bytes 28
  29.6 45.6 %copy-start.7 = (bf16[4,2,48,384]{3,2,1,0:T(8,128)(2,1)}, bf16[4,2,48,384]{3,2,1,0:T(8,128)(2,1)S(1)}, u32[]{:S(2)}) copy-start(bf16[4,2,48,384]{3,2,1,0:T(8,128)(2,1)S(1)} %get-tuple-element.147.refs_1_) | copy-start | bytes 884740
  29.6 45.6 %copy-start.8 = (bf16[4,2,48,384]{3,2,1,0:T(8,128)(2,1)}, bf16[4,2,48,384]{3,2,1,0:T(8,128)(2,1)S(1)}, u32[]{:S(2)}) copy-start(bf16[4,2,48,384]{3,2,1,0:T(8,128)(2,1)S(1)} %get-tuple-element.148.refs_0_) | copy-start | bytes 884740
  29.6 15.7 %collective-permute-start.3 = (bf16[4,2,48,384]{3,2,1,0:T(8,128)(2,1)S(1)}, bf16[4,2,48,384]{3,2,1,0:T(8,128)(2,1)S(1)}, u32[]{:S(2)}, u32[]{:S(2)}) collective-permute-start(bf16[4,2,48,384]{3,2,1,0:T(8,128)(2,1)S(1)} %get-tuple-element.148.refs_0_), channel_id=1, source_target_pairs={{0,1},{1,0},{2,3},{3,2},{4,5},{5,4},{6,7},{7,6},{8,9},{9,8},{10,11... | collective-permute-start | bytes 884744 | tf_op jit(solution)/shard_map/ppermute | solution.py:750
  31.2 14.2 %collective-permute-start.4 = (bf16[4,2,48,384]{3,2,1,0:T(8,128)(2,1)S(1)}, bf16[4,2,48,384]{3,2,1,0:T(8,128)(2,1)S(1)}, u32[]{:S(2)}, u32[]{:S(2)}) collective-permute-start(bf16[4,2,48,384]{3,2,1,0:T(8,128)(2,1)S(1)} %get-tuple-element.147.refs_1_), channel_id=1, source_target_pairs={{0,4},{2,6},{4,0},{6,2},{8,12},{10,14},{12,8},{14,10},{16,20},{18,... | collective-permute-start | bytes 884744 | tf_op jit(solution)/shard_map/ppermute | solution.py:754
  32.7 14.3 %collective-permute-start.5 = (bf16[4,2,48,384]{3,2,1,0:T(8,128)(2,1)S(1)}, bf16[4,2,48,384]{3,2,1,0:T(8,128)(2,1)S(1)}, u32[]{:S(2)}, u32[]{:S(2)}) collective-permute-start(bf16[4,2,48,384]{3,2,1,0:T(8,128)(2,1)S(1)} %get-tuple-element.148.refs_0_), channel_id=1, source_target_pairs={{0,4},{2,6},{4,0},{6,2},{8,12},{10,14},{12,8},{14,10},{16,20},{18,... | collective-permute-start | bytes 884744 | tf_op jit(solution)/shard_map/ppermute | solution.py:754
  33.2 27.2 %collective-permute-start.6 = (bf16[4,2,48,384]{3,2,1,0:T(8,128)(2,1)S(1)}, bf16[4,2,48,384]{3,2,1,0:T(8,128)(2,1)S(1)}, u32[]{:S(2)}, u32[]{:S(2)}) collective-permute-start(bf16[4,2,48,384]{3,2,1,0:T(8,128)(2,1)S(1)} %get-tuple-element.147.refs_1_), channel_id=1, source_target_pairs={{0,1},{1,0},{2,3},{3,2},{4,5},{5,4},{6,7},{7,6},{8,9},{9,8},{10,11... | collective-permute-start | bytes 884744 | tf_op jit(solution)/shard_map/ppermute | solution.py:750
  33.7 26.7 %collective-permute-start.9 = (bf16[4,2,48,384]{3,2,1,0:T(8,128)(2,1)S(1)}, bf16[4,2,48,384]{3,2,1,0:T(8,128)(2,1)S(1)}, u32[]{:S(2)}, u32[]{:S(2)}) collective-permute-start(bf16[4,2,48,384]{3,2,1,0:T(8,128)(2,1)S(1)} %get-tuple-element.148.refs_0_), channel_id=1, source_target_pairs={{0,2},{2,0},{4,6},{6,4},{8,10},{10,8},{12,14},{14,12},{16,18},{18,... | collective-permute-start | bytes 884744 | tf_op jit(solution)/shard_map/ppermute | solution.py:754
  45.3 29.9 %copy-start.18 = (bf16[4,2,48,384]{3,2,1,0:T(8,128)(2,1)}, bf16[4,2,48,384]{3,2,1,0:T(8,128)(2,1)S(1)}, u32[]{:S(2)}) copy-start(bf16[4,2,48,384]{3,2,1,0:T(8,128)(2,1)S(1)} %collective-permute-done.3.refs_2_) | copy-start | bytes 884740
  45.3 15.6 %collective-permute-start.10 = (bf16[4,2,48,384]{3,2,1,0:T(8,128)(2,1)S(1)}, bf16[4,2,48,384]{3,2,1,0:T(8,128)(2,1)S(1)}, u32[]{:S(2)}, u32[]{:S(2)}) collective-permute-start(bf16[4,2,48,384]{3,2,1,0:T(8,128)(2,1)S(1)} %get-tuple-element.147.refs_1_), channel_id=1, source_target_pairs={{0,2},{2,0},{4,6},{6,4},{8,10},{10,8},{12,14},{14,12},{16,18},{18,... | collective-permute-start | bytes 884744 | tf_op jit(solution)/shard_map/ppermute | solution.py:754
  45.3 29.9 %copy-start.19 = (bf16[4,2,48,384]{3,2,1,0:T(8,128)(2,1)}, bf16[4,2,48,384]{3,2,1,0:T(8,128)(2,1)S(1)}, u32[]{:S(2)}) copy-start(bf16[4,2,48,384]{3,2,1,0:T(8,128)(2,1)S(1)} %collective-permute-done.4.refs_3_) | copy-start | bytes 884740
  45.4 15.6 %collective-permute-start.7 = (bf16[4,2,48,384]{3,2,1,0:T(8,128)(2,1)S(1)}, bf16[4,2,48,384]{3,2,1,0:T(8,128)(2,1)S(1)}, u32[]{:S(2)}, u32[]{:S(2)}) collective-permute-start(bf16[4,2,48,384]{3,2,1,0:T(8,128)(2,1)S(1)} %collective-permute-done.3.refs_2_), channel_id=1, source_target_pairs={{0,4},{2,6},{4,0},{6,2},{8,12},{10,14},{12,8},{14,10},{16,20},{18,... | collective-permute-start | bytes 884744 | tf_op jit(solution)/shard_map/ppermute | solution.py:754
  47.0 28.3 %copy-start.20 = (bf16[4,2,48,384]{3,2,1,0:T(8,128)(2,1)}, bf16[4,2,48,384]{3,2,1,0:T(8,128)(2,1)S(1)}, u32[]{:S(2)}) copy-start(bf16[4,2,48,384]{3,2,1,0:T(8,128)(2,1)S(1)} %collective-permute-done.5.refs_4_) | copy-start | bytes 884740
  47.0 25.3 %collective-permute-start.8 = (bf16[4,2,48,384]{3,2,1,0:T(8,128)(2,1)S(1)}, bf16[4,2,48,384]{3,2,1,0:T(8,128)(2,1)S(1)}, u32[]{:S(2)}, u32[]{:S(2)}) collective-permute-start(bf16[4,2,48,384]{3,2,1,0:T(8,128)(2,1)S(1)} %collective-permute-done.4.refs_3_), channel_id=1, source_target_pairs={{0,1},{1,0},{2,3},{3,2},{4,5},{5,4},{6,7},{7,6},{8,9},{9,8},{10,11... | collective-permute-start | bytes 884744 | tf_op jit(solution)/shard_map/ppermute | solution.py:750
  60.4 14.9 %copy-start.21 = (bf16[4,2,48,384]{3,2,1,0:T(8,128)(2,1)}, bf16[4,2,48,384]{3,2,1,0:T(8,128)(2,1)S(1)}, u32[]{:S(2)}) copy-start(bf16[4,2,48,384]{3,2,1,0:T(8,128)(2,1)S(1)} %collective-permute-done.6.refs_5_) | copy-start | bytes 884740
  60.4 11.9 %collective-permute-start.11 = (bf16[4,2,48,384]{3,2,1,0:T(8,128)(2,1)S(1)}, bf16[4,2,48,384]{3,2,1,0:T(8,128)(2,1)S(1)}, u32[]{:S(2)}, u32[]{:S(2)}) collective-permute-start(bf16[4,2,48,384]{3,2,1,0:T(8,128)(2,1)S(1)} %collective-permute-done.3.refs_2_), channel_id=1, source_target_pairs={{0,2},{2,0},{4,6},{6,4},{8,10},{10,8},{12,14},{14,12},{16,18},{18,... | collective-permute-start | bytes 884744 | tf_op jit(solution)/shard_map/ppermute | solution.py:754
  60.4 14.9 %copy-start.22 = (bf16[4,2,48,384]{3,2,1,0:T(8,128)(2,1)}, bf16[4,2,48,384]{3,2,1,0:T(8,128)(2,1)S(1)}, u32[]{:S(2)}) copy-start(bf16[4,2,48,384]{3,2,1,0:T(8,128)(2,1)S(1)} %collective-permute-done.9.refs_8_) | copy-start | bytes 884740
  60.4 14.8 %collective-permute-start.12 = (bf16[4,2,48,384]{3,2,1,0:T(8,128)(2,1)S(1)}, bf16[4,2,48,384]{3,2,1,0:T(8,128)(2,1)}, u32[]{:S(2)}, u32[]{:S(2)}) collective-permute-start(bf16[4,2,48,384]{3,2,1,0:T(8,128)(2,1)S(1)} %collective-permute-done.4.refs_3_), channel_id=1, source_target_pairs={{0,2},{2,0},{4,6},{6,4},{8,10},{10,8},{12,14},{14,12},{16,18},{18,... | collective-permute-start | bytes 884744 | tf_op jit(solution)/shard_map/ppermute | solution.py:754
  60.9 14.4 %copy-start.23 = (bf16[4,2,48,384]{3,2,1,0:T(8,128)(2,1)}, bf16[4,2,48,384]{3,2,1,0:T(8,128)(2,1)S(1)}, u32[]{:S(2)}) copy-start(bf16[4,2,48,384]{3,2,1,0:T(8,128)(2,1)S(1)} %collective-permute-done.10.refs_9_) | copy-start | bytes 884740
  60.9 14.3 %collective-permute-start.13 = (bf16[4,2,48,384]{3,2,1,0:T(8,128)(2,1)S(1)}, bf16[4,2,48,384]{3,2,1,0:T(8,128)(2,1)}, u32[]{:S(2)}, u32[]{:S(2)}) collective-permute-start(bf16[4,2,48,384]{3,2,1,0:T(8,128)(2,1)S(1)} %collective-permute-done.5.refs_4_), channel_id=1, source_target_pairs={{0,2},{2,0},{4,6},{6,4},{8,10},{10,8},{12,14},{14,12},{16,18},{18,... | collective-permute-start | bytes 884744 | tf_op jit(solution)/shard_map/ppermute | solution.py:754
  61.0 14.3 %copy-start.24 = (bf16[4,2,48,384]{3,2,1,0:T(8,128)(2,1)}, bf16[4,2,48,384]{3,2,1,0:T(8,128)(2,1)S(1)}, u32[]{:S(2)}) copy-start(bf16[4,2,48,384]{3,2,1,0:T(8,128)(2,1)S(1)} %collective-permute-done.7.refs_6_) | copy-start | bytes 884740
  61.0 14.2 %collective-permute-start.14 = (bf16[4,2,48,384]{3,2,1,0:T(8,128)(2,1)S(1)}, bf16[4,2,48,384]{3,2,1,0:T(8,128)(2,1)}, u32[]{:S(2)}, u32[]{:S(2)}) collective-permute-start(bf16[4,2,48,384]{3,2,1,0:T(8,128)(2,1)S(1)} %collective-permute-done.6.refs_5_), channel_id=1, source_target_pairs={{0,2},{2,0},{4,6},{6,4},{8,10},{10,8},{12,14},{14,12},{16,18},{18,... | collective-permute-start | bytes 884744 | tf_op jit(solution)/shard_map/ppermute | solution.py:754
  72.3 2.9 %collective-permute-start.15 = (bf16[4,2,48,384]{3,2,1,0:T(8,128)(2,1)S(1)}, bf16[4,2,48,384]{3,2,1,0:T(8,128)(2,1)}, u32[]{:S(2)}, u32[]{:S(2)}) collective-permute-start(bf16[4,2,48,384]{3,2,1,0:T(8,128)(2,1)S(1)} %collective-permute-done.7.refs_6_), channel_id=1, source_target_pairs={{0,2},{2,0},{4,6},{6,4},{8,10},{10,8},{12,14},{14,12},{16,18},{18,... | collective-permute-start | bytes 884744 | tf_op jit(solution)/shard_map/ppermute | solution.py:754
  72.3 2.9 %collective-permute-start.16 = (bf16[4,2,48,384]{3,2,1,0:T(8,128)(2,1)S(1)}, bf16[4,2,48,384]{3,2,1,0:T(8,128)(2,1)}, u32[]{:S(2)}, u32[]{:S(2)}) collective-permute-start(bf16[4,2,48,384]{3,2,1,0:T(8,128)(2,1)S(1)} %collective-permute-done.8.refs_7_), channel_id=1, source_target_pairs={{0,2},{2,0},{4,6},{6,4},{8,10},{10,8},{12,14},{14,12},{16,18},{18,... | collective-permute-start | bytes 884744 | tf_op jit(solution)/shard_map/ppermute | solution.py:754
  126.7 88.8 %reduce-scatter.5.cloned.1.call-start = ((), (), s32[]{:S(2)}) async-start(), calls=%async_computation.3 | async-start | bytes 3686400 | tf_op jit(solution)/shard_map/reduce_scatter | solution.py:845
  135.6 20.1 %copy-start.9 = (f32[7,768]{1,0:T(8,128)S(1)}, f32[7,768]{1,0:T(8,128)}, u32[]{:S(2)}) copy-start(f32[7,768]{1,0:T(8,128)} %get-tuple-element.99) | copy-start | bytes 64516
  135.6 20.1 %copy-start.11 = (f32[3,768]{1,0:T(4,128)S(1)}, f32[3,768]{1,0:T(4,128)}, u32[]{:S(2)}) copy-start(f32[3,768]{1,0:T(4,128)} %get-tuple-element.100) | copy-start | bytes 27652
  156.5 12.9 %collective-permute-start.19 = (f32[12,768]{1,0:T(8,128)S(1)}, f32[12,768]{1,0:T(8,128)S(1)}, u32[]{:S(2)}, u32[]{:S(2)}) collective-permute-start(f32[12,768]{1,0:T(8,128)S(1)} %pad_maximum_fusion.2), channel_id=1, source_target_pairs={{0,24},{2,26},{4,28},{6,30},{8,0},{10,2},{12,4},{14,6},{16,8},{18,... | collective-permute-start | bytes 110600 | tf_op jit(solution)/shard_map/ppermute | solution.py:759
  158.3 11.1 %collective-permute-start.18 = (f32[12,768]{1,0:T(8,128)S(1)}, f32[12,768]{1,0:T(8,128)S(1)}, u32[]{:S(2)}, u32[]{:S(2)}) collective-permute-start(f32[12,768]{1,0:T(8,128)S(1)} %pad_maximum_fusion.2), channel_id=1, source_target_pairs={{0,16},{2,18},{4,20},{6,22},{8,24},{10,26},{12,28},{14,30},{16,0},... | collective-permute-start | bytes 110600 | tf_op jit(solution)/shard_map/ppermute | solution.py:759
  159.1 10.3 %collective-permute-start.17 = (f32[12,768]{1,0:T(8,128)S(1)}, f32[12,768]{1,0:T(8,128)S(1)}, u32[]{:S(2)}, u32[]{:S(2)}) collective-permute-start(f32[12,768]{1,0:T(8,128)S(1)} %pad_maximum_fusion.2), channel_id=1, source_target_pairs={{0,8},{2,10},{4,12},{6,14},{8,16},{10,18},{12,20},{14,22},{16,24},... | collective-permute-start | bytes 110600 | tf_op jit(solution)/shard_map/ppermute | solution.py:759
  169.5 5.7 %collective-permute-start.20 = (bf16[4,4,5,48,384]{4,3,2,1,0:T(8,128)(2,1)}, bf16[4,4,5,48,384]{4,3,2,1,0:T(8,128)(2,1)S(1)}, u32[]{:S(2)}, u32[]{:S(2)}) collective-permute-start(bf16[4,4,5,48,384]{4,3,2,1,0:T(8,128)(2,1)} %get-tuple-element.104), channel_id=1, source_target_pairs={{0,2},{2,0},{4,6},{6,4},{8,10},{10,8},{12,14},{14,12},{16,18},{18,... | collective-permute-start | bytes 8847368 | tf_op jit(solution)/shard_map/ppermute | solution.py:754
  181.7 18.5 %collective-permute-start.23 = (bf16[8,48,384]{2,1,0:T(8,128)(2,1)}, bf16[8,48,384]{2,1,0:T(8,128)(2,1)S(1)}, u32[]{:S(2)}, u32[]{:S(2)}) collective-permute-start(bf16[8,48,384]{2,1,0:T(8,128)(2,1)} %get-tuple-element.113), channel_id=1, source_target_pairs={{0,8},{2,10},{4,12},{6,14},{8,16},{10,18},{12,20},{14,22},{16,24},... | collective-permute-start | bytes 884744 | tf_op jit(solution)/shard_map/ppermute | solution.py:759
  183.4 22.1 %collective-permute-start.24 = (bf16[8,48,384]{2,1,0:T(8,128)(2,1)}, bf16[8,48,384]{2,1,0:T(8,128)(2,1)S(1)}, u32[]{:S(2)}, u32[]{:S(2)}) collective-permute-start(bf16[8,48,384]{2,1,0:T(8,128)(2,1)} %get-tuple-element.114), channel_id=1, source_target_pairs={{0,16},{2,18},{4,20},{6,22},{8,24},{10,26},{12,28},{14,30},{16,0},... | collective-permute-start | bytes 884744 | tf_op jit(solution)/shard_map/ppermute | solution.py:759
  185.3 20.2 %collective-permute-start.25 = (bf16[8,48,384]{2,1,0:T(8,128)(2,1)}, bf16[8,48,384]{2,1,0:T(8,128)(2,1)S(1)}, u32[]{:S(2)}, u32[]{:S(2)}) collective-permute-start(bf16[8,48,384]{2,1,0:T(8,128)(2,1)} %get-tuple-element.115), channel_id=1, source_target_pairs={{0,24},{2,26},{4,28},{6,30},{8,0},{10,2},{12,4},{14,6},{16,8},{18,... | collective-permute-start | bytes 884744 | tf_op jit(solution)/shard_map/ppermute | solution.py:759
  193.5 1.2 collective-permute-start.21
  194.7 5.4 %collective-permute-start.22 = (f32[12,768]{1,0:T(8,128)S(1)}, f32[12,768]{1,0:T(8,128)S(1)}, u32[]{:S(2)}, u32[]{:S(2)}) collective-permute-start(f32[12,768]{1,0:T(8,128)S(1)} %add.139), channel_id=1, source_target_pairs={{0,1},{1,0},{2,3},{3,2},{4,5},{5,4},{6,7},{7,6},{8,9},{9,8},{10,11... | collective-permute-start | bytes 110600 | tf_op jit(solution)/shard_map/ppermute | solution.py:750
  200.1 22.2 %copy-start.12 = (f32[6,768]{1,0:T(8,128)S(1)}, f32[6,768]{1,0:T(8,128)}, u32[]{:S(2)}) copy-start(f32[6,768]{1,0:T(8,128)} %nv_ref.3) | copy-start | bytes 55300
  200.1 22.2 %copy-start.13 = (f32[6,768]{1,0:T(8,128)S(1)}, f32[6,768]{1,0:T(8,128)}, u32[]{:S(2)}) copy-start(f32[6,768]{1,0:T(8,128)} %param.21) | copy-start | bytes 55300
  200.2 22.2 %copy-start.14 = (f32[6,768]{1,0:T(8,128)S(1)}, f32[6,768]{1,0:T(8,128)}, u32[]{:S(2)}) copy-start(f32[6,768]{1,0:T(8,128)} %param.22) | copy-start | bytes 55300
  205.5 5.5 %collective-permute-start.26 = (f32[12,768]{1,0:T(8,128)S(1)}, f32[12,768]{1,0:T(8,128)S(1)}, u32[]{:S(2)}, u32[]{:S(2)}) collective-permute-start(f32[12,768]{1,0:T(8,128)S(1)} %add.140), channel_id=1, source_target_pairs={{0,4},{2,6},{4,0},{6,2},{8,12},{10,14},{12,8},{14,10},{16,20},{18,... | collective-permute-start | bytes 110600 | tf_op jit(solution)/shard_map/ppermute | solution.py:754
  216.8 9.5 %collective-permute-start.27 = (bf16[5,48,384]{2,1,0:T(8,128)(2,1)S(1)}, bf16[5,48,384]{2,1,0:T(8,128)(2,1)S(1)}, u32[]{:S(2)}, u32[]{:S(2)}) collective-permute-start(bf16[5,48,384]{2,1,0:T(8,128)(2,1)S(1)} %get-tuple-element.145), channel_id=1, source_target_pairs={{0,8},{2,10},{4,12},{6,14},{8,16},{10,18},{12,20},{14,22},{16,24},... | collective-permute-start | bytes 552968 | tf_op jit(solution)/shard_map/ppermute | solution.py:759
  219.9 13.2 %collective-permute-start.28 = (bf16[5,48,384]{2,1,0:T(8,128)(2,1)S(1)}, bf16[5,48,384]{2,1,0:T(8,128)(2,1)S(1)}, u32[]{:S(2)}, u32[]{:S(2)}) collective-permute-start(bf16[5,48,384]{2,1,0:T(8,128)(2,1)S(1)} %get-tuple-element.144), channel_id=1, source_target_pairs={{0,16},{2,18},{4,20},{6,22},{8,24},{10,26},{12,28},{14,30},{16,0},... | collective-permute-start | bytes 552968 | tf_op jit(solution)/shard_map/ppermute | solution.py:759
  221.0 12.1 %collective-permute-start.29 = (bf16[5,48,384]{2,1,0:T(8,128)(2,1)S(1)}, bf16[5,48,384]{2,1,0:T(8,128)(2,1)S(1)}, u32[]{:S(2)}, u32[]{:S(2)}) collective-permute-start(bf16[5,48,384]{2,1,0:T(8,128)(2,1)S(1)} %get-tuple-element.143), channel_id=1, source_target_pairs={{0,24},{2,26},{4,28},{6,30},{8,0},{10,2},{12,4},{14,6},{16,8},{18,... | collective-permute-start | bytes 552968 | tf_op jit(solution)/shard_map/ppermute | solution.py:759
  (13 other events, 75.5 us)
Sparse Core Ops, SparseCore 0:
  10.2 91.6 all-gather.2
  126.8 52.2 reduce-scatter.2
  181.4 34.0 reduce-scatter.4

commit v3 on v2

--- a/solution.py
+++ b/solution.py
@@ -451,7 +451,7 @@
         copy_g(2 * i).start()
         return carry
 
-    lax.fori_loop(0, blocks, backward, 0, unroll=UNROLL)
+    lax.fori_loop(0, blocks, backward, 0, unroll=2)
     for i in range(blocks):
         sums_ref[3 + i : 4 + i] = hsum_ref[i]
     copy_unit.wait()

time: 244 us -> 243 us (level)
  no operation moved by 1% of the time
where the time goes in v3:
time: 243 us; the launch traced here: 241 us
  Pallas kernels  97.8 us (40%)
  waiting for transfers between devices  52.4 us (22%)
  starting transfers between devices  44.8 us (18%)
  other arithmetic  14.8 us (6%)
  between operations  14.3 us (6%)
  local copies, waits for them, and re-layouts  12.7 us (5%)
  blocking collectives  4.39 us (2%)
    pallas_call x1, Pallas kernels, mlp(): pl.pallas_call(functools.partial(mlp_kernel, blocks), grid=(1,), in_specs...  24.3 us
    ppermute x4, waiting for transfers between devices, swap_x(): return lax.ppermute(value, 'mp', [(0, 1), (1, 0)])  24.1 us
    ppermute x12, starting transfers between devices, shift_line(): lax.ppermute(value, 'dp', [(d, (d + 4 * step) % dp) for d in range(dp)])  21.1 us
    pallas_call x1, Pallas kernels, attend_back(): pl.pallas_call(attend_back_kernel, grid=(heads // 2,), in_specs=[pl.Block...  20.1 us
    ppermute x4, starting transfers between devices, swap_x(): return lax.ppermute(value, 'mp', [(0, 1), (1, 0)])  17.2 us
    pallas_call x1, Pallas kernels, attend(): pl.pallas_call(attend_kernel, grid=(heads // 2,), in_specs=[pl.BlockSpec(...  15.8 us
    ppermute x12, waiting for transfers between devices, shift_line(): lax.ppermute(value, 'dp', [(d, (d + 4 * step) % dp) for d in range(dp)])  15.4 us
    pallas_call x1, Pallas kernels, project_back(): pl.pallas_call(project_back_kernel, grid=(5,), in_specs=[pl.BlockSpec(mem...  9.4 us
  transfers between devices with their start and end apart: 33, of which 10 were waited for; matrix products, arithmetic and copies ran while one was open for 9% of the time, Pallas kernels for 30%

profile of v3, /device:TPU:0, one launch (start us, length us, event | category | flops | bytes accessed | tf_op | source)
XLA Modules:
  0.0 241.0 jit_solution(8861147185957389627)
XLA Ops:
  7.3 1.3 copy-done.2
  9.4 3.1 %collective-permute-start = (bf16[4,48,384]{2,1,0:T(8,128)(2,1)S(1)}, bf16[4,48,384]{2,1,0:T(8,128)(2,1)S(1)}, u32[]{:S(2)}, u32[]{:S(2)}) collective-permute-start(bf16[4,48,384]{2,1,0:T(8,128)(2,1)S(1)} %get-tuple-element.76), channel_id=1, source_target_pairs={{0,8},{2,10},{4,12},{6,14},{8,16},{10,18},{12,20},{14,22},{16,24},... | collective-permute-start | bytes 442376 | tf_op jit(solution)/shard_map/ppermute | solution.py:759
  12.5 2.6 %collective-permute-start.1 = (bf16[4,48,384]{2,1,0:T(8,128)(2,1)S(1)}, bf16[4,48,384]{2,1,0:T(8,128)(2,1)S(1)}, u32[]{:S(2)}, u32[]{:S(2)}) collective-permute-start(bf16[4,48,384]{2,1,0:T(8,128)(2,1)S(1)} %get-tuple-element.76), channel_id=1, source_target_pairs={{0,16},{2,18},{4,20},{6,22},{8,24},{10,26},{12,28},{14,30},{16,0},... | collective-permute-start | bytes 442376 | tf_op jit(solution)/shard_map/ppermute | solution.py:759
  15.1 1.4 collective-permute-start.2
  16.4 4.4 %all_gather.9 = f32[6,768]{1,0:T(8,128)S(1)} all-gather(f32[6,384]{1,0:T(8,128)S(1)} %copy-done.10), channel_id=1, replica_groups=mesh['dp'=16,'mp'=2] {'mp'}, dimensions={1}, use_global_device_ids=true | all-gather | bytes 27648 | tf_op jit(solution)/shard_map/all_gather | solution.py:956
  20.8 0.9 constant_dynamic-slice_fusion.x_ref.x_hbm
  21.8 6.3 %fusion = (bf16[1024,384]{1,0:T(8,128)(2,1)S(1)}, bf16[1024,384]{1,0:T(8,128)(2,1)S(1)}) fusion(f32[384]{0:T(512)S(1)} %negate_power_fusion, f32[1024]{0:T(1024)S(1)} %subtract_convert_fusion), kind=kLoop, calls=%fused_computation.3 | loop fusion | flops 1179648 | bytes 1578496 | tf_op jit(solution)/shard_map/convert
  28.1 1.3 pad_maximum_fusion.sine_ref.sine_hbm
  29.6 1.6 collective-permute-start.3
  31.2 1.5 collective-permute-start.4
  33.7 11.6 %collective-permute-done.3.refs_2_ = bf16[4,2,48,384]{3,2,1,0:T(8,128)(2,1)S(1)} collective-permute-done((bf16[4,2,48,384]{3,2,1,0:T(8,128)(2,1)S(1)}, bf16[4,2,48,384]{3,2,1,0:T(8,128)(2,1)S(1)}, u32[]{:S(2)}, u32[]{:S(2)}) %collective-permute-start.3) | collective-permute-done | bytes 294944 | tf_op jit(solution)/shard_map/ppermute | solution.py:750
  45.4 1.6 collective-permute-start.7
  47.0 13.4 %collective-permute-start.8 = (bf16[4,2,48,384]{3,2,1,0:T(8,128)(2,1)S(1)}, bf16[4,2,48,384]{3,2,1,0:T(8,128)(2,1)S(1)}, u32[]{:S(2)}, u32[]{:S(2)}) collective-permute-start(bf16[4,2,48,384]{3,2,1,0:T(8,128)(2,1)S(1)} %collective-permute-done.4.refs_3_), channel_id=1, source_target_pairs={{0,1},{1,0},{2,3},{3,2},{4,5},{5,4},{6,7},{7,6},{8,9},{9,8},{10,11... | collective-permute-start | bytes 884744 | tf_op jit(solution)/shard_map/ppermute | solution.py:750
  61.4 10.8 %collective-permute-done.8.refs_7_ = bf16[4,2,48,384]{3,2,1,0:T(8,128)(2,1)S(1)} collective-permute-done((bf16[4,2,48,384]{3,2,1,0:T(8,128)(2,1)S(1)}, bf16[4,2,48,384]{3,2,1,0:T(8,128)(2,1)S(1)}, u32[]{:S(2)}, u32[]{:S(2)}) %collective-permute-start.8) | collective-permute-done | bytes 294944 | tf_op jit(solution)/shard_map/ppermute | solution.py:750
  75.3 8.6 %project.1 = (bf16[512,768]{1,0:T(8,128)(2,1)}, bf16[512,768]{1,0:T(8,128)(2,1)}, bf16[512,768]{1,0:T(8,128)(2,1)}, bf16[512,768]{1,0:T(8,128)(2,1)}, bf16[1024,...) custom-call(s32[4]{0:T(128)} %pad_add_fusion.place_ref, bf16[512,768]{1,0:T(8,128)(2,1)} %constant_dynamic-slice_fusion.x_ref.x_hbm, ...), custom_call_target="tpu_custom_call" | custom-call | flops 8999999488 | tf_op jit(solution)/shard_map/project/pallas_call | solution.py:285
  83.9 15.8 %attend.1 = (bf16[12,512,512]{2,1,0:T(8,128)(2,1)}, bf16[512,768]{1,0:T(8,128)(2,1)}) custom-call(s32[1]{0:T(128)} %dynamic_slice.36.len_ref, bf16[512,768]{1,0:T(8,128)(2,1)} %get-tuple-element.80.qc_ref, bf16[512,768]{1,0:T(8,128)(2,1)} %get-tuple-element.81.qp_ref, bf16[512,768]{1,0:T(8,128)(2,1)} %get-tuple-element.82.k_ref, ...), custom_call_target="tpu_custom_call" | custom-call | flops 19000000512 | tf_op jit(solution)/shard_map/attend/pallas_call | solution.py:343
  99.8 2.2 all-gather.3.cloned.1.call-done
  101.9 24.3 %mlp.1 = (bf16[512,768]{1,0:T(8,128)(2,1)}, f32[512,768]{1,0:T(8,128)}, f32[512,128]{1,0:T(8,128)}, f32[512,768]{1,0:T(8,128)}, bf16[8,4,8,48,384]{4,3,2,1,0:T(8...) custom-call(f32[6,768]{1,0:T(8,128)} %nv_ref.3, f32[4,1,768]{2,1,0:T(1,128)} %reshape.37.hb_ref, ...), custom_call_target="tpu_custom_call" | custom-call | flops 23000000512 | tf_op jit(solution)/shard_map/mlp/pallas_call | solution.py:483
  126.3 8.9 %norm_down.1 = (f32[512,768]{1,0:T(8,128)}, bf16[512,768]{1,0:T(8,128)(2,1)}, bf16[512,768]{1,0:T(8,128)(2,1)}, f32[3,768]{1,0:T(4,128)}) custom-call(f32[6,768]{1,0:T(8,128)} %nv_ref.3, f32[512,128]{1,0:T(8,128)} %get-tuple-element.89.inv_ref, f32[512,768]{1,0:T(8,128)} %get-tuple-element.90.unit_hbm, f32[512,768]{1,0:T(8,128)} %get-tuple-element.91.gh2_hbm, ...), custom_call_target="tpu_custom_call" | custom-call | flops 8000000000 | tf_op jit(solution)/shard_map/norm_down/pallas_call | solution.py:554
  135.2 20.1 %attend_back.1 = (bf16[3,512,768]{2,1,0:T(8,128)(2,1)}, bf16[1024,768]{1,0:T(8,128)(2,1)}, f32[2,768]{1,0:T(2,128)}) custom-call(bf16[12,512,512]{2,1,0:T(8,128)(2,1)} %get-tuple-element.88.probs_ref, bf16[512,768]{1,0:T(8,128)(2,1)} %get-tuple-element.93.gm_ref, bf16[512,768]{1,0:T(8,128)(2,1)} %get-tuple-element.80.qc_ref, ...), custom_call_target="tpu_custom_call" | custom-call | flops 28000000000 | tf_op jit(solution)/shard_map/attend_back/pallas_call | solution.py:646
  156.0 1.9 collective-permute-start.19
  159.5 9.4 %project_back.1 = (bf16[4,4,5,48,384]{4,3,2,1,0:T(8,128)(2,1)}, bf16[4,4,5,48,384]{4,3,2,1,0:T(8,128)(2,1)}) custom-call(s32[1]{0:T(128)} %bitcast.4.core_ref, bf16[512,768]{1,0:T(8,128)(2,1)} %constant_dynamic-slice_fusion.x_ref.x_hbm, bf16[3,512,768]{2,1,0:T(8,128)(2,1)} %get-tuple-element.107.gqkv_ref, bf16[1024,768]{1,0:T(8,128)(2,1)} %get-tuple-element.95.grel_hbm, ...), custom_call_target="tpu_custom_call" | custom-call | flops 8999999488 | tf_op jit(solution)/shard_map/project_back/pallas_call | solution.py:708
  169.1 5.6 %collective-permute-done.20 = bf16[4,4,5,48,384]{4,3,2,1,0:T(8,128)(2,1)S(1)} collective-permute-done((bf16[4,4,5,48,384]{4,3,2,1,0:T(8,128)(2,1)}, bf16[4,4,5,48,384]{4,3,2,1,0:T(8,128)(2,1)S(1)}, u32[]{:S(2)}, u32[]{:S(2)}) %collective-permute-start.20) | collective-permute-done | bytes 2949152 | tf_op jit(solution)/shard_map/ppermute | solution.py:754
  174.7 4.3 %add_convert_fusion = bf16[4,4,5,48,384]{4,3,2,1,0:T(8,128)(2,1)} fusion(bf16[4,4,5,48,384]{4,3,2,1,0:T(8,128)(2,1)S(1)} %collective-permute-done.20, bf16[4,4,5,48,384]{4,3,2,1,0:T(8,128)(2,1)} %get-tuple-element.103), kind=kLoop, calls=%fused_computation | loop fusion | flops 5898240 | bytes 8847360 | tf_op jit(solution)/shard_map/convert_element_type | solution.py:838
  179.1 1.2 copy-done.6
  180.3 0.9 dynamic-slice_bitcast_fusion
  181.2 2.0 collective-permute-start.23
  183.2 1.6 collective-permute-start.24
  184.8 1.3 collective-permute-start.25
  186.2 6.9 %token_grad.1 = f32[512,768]{1,0:T(8,128)} custom-call(bf16[3,512,768]{2,1,0:T(8,128)(2,1)} %get-tuple-element.107.gqkv_ref, bf16[3,2,768,384]{3,2,1,0:T(8,128)(2,1)} %get-tuple-element.108.w_ref, f32[512,768]{1,0:T(8,128)} %get-tuple-element.109.gh1_ref), custom_call_target="tpu_custom_call" | custom-call | flops 6000000000 | tf_op jit(solution)/shard_map/token_grad/pallas_call | solution.py:737
  193.0 1.2 collective-permute-done.21
  194.3 1.7 collective-permute-start.22
  196.0 1.0 slice.59.refs_5_
  197.0 1.0 slice.60.refs_6_
  198.0 1.7 collective-permute-done.22
  199.8 5.3 %collective-permute-done.24.refs_2_ = bf16[8,48,384]{2,1,0:T(8,128)(2,1)S(1)} collective-permute-done((bf16[8,48,384]{2,1,0:T(8,128)(2,1)}, bf16[8,48,384]{2,1,0:T(8,128)(2,1)S(1)}, u32[]{:S(2)}, u32[]{:S(2)}) %collective-permute-start.24) | collective-permute-done | bytes 294944 | tf_op jit(solution)/shard_map/ppermute | solution.py:759
  205.1 1.2 collective-permute-start.26
  206.3 1.2 copy-done.4
  207.5 1.2 copy-done.5
  208.7 1.9 adam.2
  211.3 3.8 %reduce-scatter.5.cloned.1.call-done = bf16[1,4,5,48,384]{4,3,2,1,0:T(8,128)(2,1)} async-done(((bf16[4,4,5,48,384]{4,3,2,1,0:T(8,128)(2,1)}), bf16[1,4,5,48,384]{4,3,2,1,0:T(8,128)(2,1)}) %reduce-scatter.5.cloned.1.call-update) | async-done | bytes 737296 | tf_op jit(solution)/shard_map/reduce_scatter | solution.py:845
  215.1 1.3 dynamic-slice_bitcast_fusion.4
  216.4 3.1 %collective-permute-start.27 = (bf16[5,48,384]{2,1,0:T(8,128)(2,1)S(1)}, bf16[5,48,384]{2,1,0:T(8,128)(2,1)S(1)}, u32[]{:S(2)}, u32[]{:S(2)}) collective-permute-start(bf16[5,48,384]{2,1,0:T(8,128)(2,1)S(1)} %get-tuple-element.145), channel_id=1, source_target_pairs={{0,8},{2,10},{4,12},{6,14},{8,16},{10,18},{12,20},{14,22},{16,24},... | collective-permute-start | bytes 552968 | tf_op jit(solution)/shard_map/ppermute | solution.py:759
  219.5 1.1 collective-permute-start.28
  220.6 1.3 collective-permute-start.29
  222.6 3.3 %collective-permute-done.27.refs_1_ = bf16[5,48,384]{2,1,0:T(8,128)(2,1)S(1)} collective-permute-done((bf16[5,48,384]{2,1,0:T(8,128)(2,1)S(1)}, bf16[5,48,384]{2,1,0:T(8,128)(2,1)S(1)}, u32[]{:S(2)}, u32[]{:S(2)}) %collective-permute-start.27) | collective-permute-done | bytes 184352 | tf_op jit(solution)/shard_map/ppermute | solution.py:759
  225.8 6.8 %collective-permute-done.28.refs_2_ = bf16[5,48,384]{2,1,0:T(8,128)(2,1)S(1)} collective-permute-done((bf16[5,48,384]{2,1,0:T(8,128)(2,1)S(1)}, bf16[5,48,384]{2,1,0:T(8,128)(2,1)S(1)}, u32[]{:S(2)}, u32[]{:S(2)}) %collective-permute-start.28) | collective-permute-done | bytes 184352 | tf_op jit(solution)/shard_map/ppermute | solution.py:759
  232.7 1.2 adam.3
  (117 shorter events, 10.8 us)
Async XLA Ops:
  7.2 94.7 %all-gather.3.cloned.1.call-start = ((), (), s32[]{:S(2)}) async-start(), calls=%async_computation.4 | async-start | bytes 10948608 | tf_op jit(solution)/shard_map/all_gather | solution.py:766
  9.3 169.7 %reduce-scatter.3.cloned.1.call-start = ((), (), s32[]{:S(2)}) async-start(), calls=%async_computation.2 | async-start | bytes 10616832 | tf_op jit(solution)/shard_map/reduce_scatter | solution.py:831
  9.4 20.0 %collective-permute-start = (bf16[4,48,384]{2,1,0:T(8,128)(2,1)S(1)}, bf16[4,48,384]{2,1,0:T(8,128)(2,1)S(1)}, u32[]{:S(2)}, u32[]{:S(2)}) collective-permute-start(bf16[4,48,384]{2,1,0:T(8,128)(2,1)S(1)} %get-tuple-element.76), channel_id=1, source_target_pairs={{0,8},{2,10},{4,12},{6,14},{8,16},{10,18},{12,20},{14,22},{16,24},... | collective-permute-start | bytes 442376 | tf_op jit(solution)/shard_map/ppermute | solution.py:759
  12.5 16.9 %collective-permute-start.1 = (bf16[4,48,384]{2,1,0:T(8,128)(2,1)S(1)}, bf16[4,48,384]{2,1,0:T(8,128)(2,1)S(1)}, u32[]{:S(2)}, u32[]{:S(2)}) collective-permute-start(bf16[4,48,384]{2,1,0:T(8,128)(2,1)S(1)} %get-tuple-element.76), channel_id=1, source_target_pairs={{0,16},{2,18},{4,20},{6,22},{8,24},{10,26},{12,28},{14,30},{16,0},... | collective-permute-start | bytes 442376 | tf_op jit(solution)/shard_map/ppermute | solution.py:759
  15.1 14.3 %collective-permute-start.2 = (bf16[4,48,384]{2,1,0:T(8,128)(2,1)S(1)}, bf16[4,48,384]{2,1,0:T(8,128)(2,1)S(1)}, u32[]{:S(2)}, u32[]{:S(2)}) collective-permute-start(bf16[4,48,384]{2,1,0:T(8,128)(2,1)S(1)} %get-tuple-element.76), channel_id=1, source_target_pairs={{0,24},{2,26},{4,28},{6,30},{8,0},{10,2},{12,4},{14,6},{16,8},{18,... | collective-permute-start | bytes 442376 | tf_op jit(solution)/shard_map/ppermute | solution.py:759
  28.1 44.7 %copy-start.27 = (s32[2]{0:T(128)S(1)}, s32[2]{0:T(128)}, u32[]{:S(2)}) copy-start(s32[2]{0:T(128)} %param.13) | copy-start | bytes 28
  29.6 45.6 %copy-start.7 = (bf16[4,2,48,384]{3,2,1,0:T(8,128)(2,1)}, bf16[4,2,48,384]{3,2,1,0:T(8,128)(2,1)S(1)}, u32[]{:S(2)}) copy-start(bf16[4,2,48,384]{3,2,1,0:T(8,128)(2,1)S(1)} %get-tuple-element.147.refs_1_) | copy-start | bytes 884740
  29.6 45.6 %copy-start.8 = (bf16[4,2,48,384]{3,2,1,0:T(8,128)(2,1)}, bf16[4,2,48,384]{3,2,1,0:T(8,128)(2,1)S(1)}, u32[]{:S(2)}) copy-start(bf16[4,2,48,384]{3,2,1,0:T(8,128)(2,1)S(1)} %get-tuple-element.148.refs_0_) | copy-start | bytes 884740
  29.6 15.7 %collective-permute-start.3 = (bf16[4,2,48,384]{3,2,1,0:T(8,128)(2,1)S(1)}, bf16[4,2,48,384]{3,2,1,0:T(8,128)(2,1)S(1)}, u32[]{:S(2)}, u32[]{:S(2)}) collective-permute-start(bf16[4,2,48,384]{3,2,1,0:T(8,128)(2,1)S(1)} %get-tuple-element.148.refs_0_), channel_id=1, source_target_pairs={{0,1},{1,0},{2,3},{3,2},{4,5},{5,4},{6,7},{7,6},{8,9},{9,8},{10,11... | collective-permute-start | bytes 884744 | tf_op jit(solution)/shard_map/ppermute | solution.py:750
  31.2 14.2 %collective-permute-start.4 = (bf16[4,2,48,384]{3,2,1,0:T(8,128)(2,1)S(1)}, bf16[4,2,48,384]{3,2,1,0:T(8,128)(2,1)S(1)}, u32[]{:S(2)}, u32[]{:S(2)}) collective-permute-start(bf16[4,2,48,384]{3,2,1,0:T(8,128)(2,1)S(1)} %get-tuple-element.147.refs_1_), channel_id=1, source_target_pairs={{0,4},{2,6},{4,0},{6,2},{8,12},{10,14},{12,8},{14,10},{16,20},{18,... | collective-permute-start | bytes 884744 | tf_op jit(solution)/shard_map/ppermute | solution.py:754
  32.7 14.3 %collective-permute-start.5 = (bf16[4,2,48,384]{3,2,1,0:T(8,128)(2,1)S(1)}, bf16[4,2,48,384]{3,2,1,0:T(8,128)(2,1)S(1)}, u32[]{:S(2)}, u32[]{:S(2)}) collective-permute-start(bf16[4,2,48,384]{3,2,1,0:T(8,128)(2,1)S(1)} %get-tuple-element.148.refs_0_), channel_id=1, source_target_pairs={{0,4},{2,6},{4,0},{6,2},{8,12},{10,14},{12,8},{14,10},{16,20},{18,... | collective-permute-start | bytes 884744 | tf_op jit(solution)/shard_map/ppermute | solution.py:754
  33.2 27.2 %collective-permute-start.6 = (bf16[4,2,48,384]{3,2,1,0:T(8,128)(2,1)S(1)}, bf16[4,2,48,384]{3,2,1,0:T(8,128)(2,1)S(1)}, u32[]{:S(2)}, u32[]{:S(2)}) collective-permute-start(bf16[4,2,48,384]{3,2,1,0:T(8,128)(2,1)S(1)} %get-tuple-element.147.refs_1_), channel_id=1, source_target_pairs={{0,1},{1,0},{2,3},{3,2},{4,5},{5,4},{6,7},{7,6},{8,9},{9,8},{10,11... | collective-permute-start | bytes 884744 | tf_op jit(solution)/shard_map/ppermute | solution.py:750
  33.7 26.7 %collective-permute-start.9 = (bf16[4,2,48,384]{3,2,1,0:T(8,128)(2,1)S(1)}, bf16[4,2,48,384]{3,2,1,0:T(8,128)(2,1)S(1)}, u32[]{:S(2)}, u32[]{:S(2)}) collective-permute-start(bf16[4,2,48,384]{3,2,1,0:T(8,128)(2,1)S(1)} %get-tuple-element.148.refs_0_), channel_id=1, source_target_pairs={{0,2},{2,0},{4,6},{6,4},{8,10},{10,8},{12,14},{14,12},{16,18},{18,... | collective-permute-start | bytes 884744 | tf_op jit(solution)/shard_map/ppermute | solution.py:754
  45.3 29.9 %copy-start.18 = (bf16[4,2,48,384]{3,2,1,0:T(8,128)(2,1)}, bf16[4,2,48,384]{3,2,1,0:T(8,128)(2,1)S(1)}, u32[]{:S(2)}) copy-start(bf16[4,2,48,384]{3,2,1,0:T(8,128)(2,1)S(1)} %collective-permute-done.3.refs_2_) | copy-start | bytes 884740
  45.3 15.6 %collective-permute-start.10 = (bf16[4,2,48,384]{3,2,1,0:T(8,128)(2,1)S(1)}, bf16[4,2,48,384]{3,2,1,0:T(8,128)(2,1)S(1)}, u32[]{:S(2)}, u32[]{:S(2)}) collective-permute-start(bf16[4,2,48,384]{3,2,1,0:T(8,128)(2,1)S(1)} %get-tuple-element.147.refs_1_), channel_id=1, source_target_pairs={{0,2},{2,0},{4,6},{6,4},{8,10},{10,8},{12,14},{14,12},{16,18},{18,... | collective-permute-start | bytes 884744 | tf_op jit(solution)/shard_map/ppermute | solution.py:754
  45.3 29.9 %copy-start.19 = (bf16[4,2,48,384]{3,2,1,0:T(8,128)(2,1)}, bf16[4,2,48,384]{3,2,1,0:T(8,128)(2,1)S(1)}, u32[]{:S(2)}) copy-start(bf16[4,2,48,384]{3,2,1,0:T(8,128)(2,1)S(1)} %collective-permute-done.4.refs_3_) | copy-start | bytes 884740
  45.4 15.6 %collective-permute-start.7 = (bf16[4,2,48,384]{3,2,1,0:T(8,128)(2,1)S(1)}, bf16[4,2,48,384]{3,2,1,0:T(8,128)(2,1)S(1)}, u32[]{:S(2)}, u32[]{:S(2)}) collective-permute-start(bf16[4,2,48,384]{3,2,1,0:T(8,128)(2,1)S(1)} %collective-permute-done.3.refs_2_), channel_id=1, source_target_pairs={{0,4},{2,6},{4,0},{6,2},{8,12},{10,14},{12,8},{14,10},{16,20},{18,... | collective-permute-start | bytes 884744 | tf_op jit(solution)/shard_map/ppermute | solution.py:754
  47.0 28.3 %copy-start.20 = (bf16[4,2,48,384]{3,2,1,0:T(8,128)(2,1)}, bf16[4,2,48,384]{3,2,1,0:T(8,128)(2,1)S(1)}, u32[]{:S(2)}) copy-start(bf16[4,2,48,384]{3,2,1,0:T(8,128)(2,1)S(1)} %collective-permute-done.5.refs_4_) | copy-start | bytes 884740
  47.0 25.3 %collective-permute-start.8 = (bf16[4,2,48,384]{3,2,1,0:T(8,128)(2,1)S(1)}, bf16[4,2,48,384]{3,2,1,0:T(8,128)(2,1)S(1)}, u32[]{:S(2)}, u32[]{:S(2)}) collective-permute-start(bf16[4,2,48,384]{3,2,1,0:T(8,128)(2,1)S(1)} %collective-permute-done.4.refs_3_), channel_id=1, source_target_pairs={{0,1},{1,0},{2,3},{3,2},{4,5},{5,4},{6,7},{7,6},{8,9},{9,8},{10,11... | collective-permute-start | bytes 884744 | tf_op jit(solution)/shard_map/ppermute | solution.py:750
  60.4 14.9 %copy-start.21 = (bf16[4,2,48,384]{3,2,1,0:T(8,128)(2,1)}, bf16[4,2,48,384]{3,2,1,0:T(8,128)(2,1)S(1)}, u32[]{:S(2)}) copy-start(bf16[4,2,48,384]{3,2,1,0:T(8,128)(2,1)S(1)} %collective-permute-done.6.refs_5_) | copy-start | bytes 884740
  60.4 11.9 %collective-permute-start.11 = (bf16[4,2,48,384]{3,2,1,0:T(8,128)(2,1)S(1)}, bf16[4,2,48,384]{3,2,1,0:T(8,128)(2,1)S(1)}, u32[]{:S(2)}, u32[]{:S(2)}) collective-permute-start(bf16[4,2,48,384]{3,2,1,0:T(8,128)(2,1)S(1)} %collective-permute-done.3.refs_2_), channel_id=1, source_target_pairs={{0,2},{2,0},{4,6},{6,4},{8,10},{10,8},{12,14},{14,12},{16,18},{18,... | collective-permute-start | bytes 884744 | tf_op jit(solution)/shard_map/ppermute | solution.py:754
  60.4 14.9 %copy-start.22 = (bf16[4,2,48,384]{3,2,1,0:T(8,128)(2,1)}, bf16[4,2,48,384]{3,2,1,0:T(8,128)(2,1)S(1)}, u32[]{:S(2)}) copy-start(bf16[4,2,48,384]{3,2,1,0:T(8,128)(2,1)S(1)} %collective-permute-done.9.refs_8_) | copy-start | bytes 884740
  60.4 14.8 %collective-permute-start.12 = (bf16[4,2,48,384]{3,2,1,0:T(8,128)(2,1)S(1)}, bf16[4,2,48,384]{3,2,1,0:T(8,128)(2,1)}, u32[]{:S(2)}, u32[]{:S(2)}) collective-permute-start(bf16[4,2,48,384]{3,2,1,0:T(8,128)(2,1)S(1)} %collective-permute-done.4.refs_3_), channel_id=1, source_target_pairs={{0,2},{2,0},{4,6},{6,4},{8,10},{10,8},{12,14},{14,12},{16,18},{18,... | collective-permute-start | bytes 884744 | tf_op jit(solution)/shard_map/ppermute | solution.py:754
  60.9 14.4 %copy-start.23 = (bf16[4,2,48,384]{3,2,1,0:T(8,128)(2,1)}, bf16[4,2,48,384]{3,2,1,0:T(8,128)(2,1)S(1)}, u32[]{:S(2)}) copy-start(bf16[4,2,48,384]{3,2,1,0:T(8,128)(2,1)S(1)} %collective-permute-done.10.refs_9_) | copy-start | bytes 884740
  60.9 14.3 %collective-permute-start.13 = (bf16[4,2,48,384]{3,2,1,0:T(8,128)(2,1)S(1)}, bf16[4,2,48,384]{3,2,1,0:T(8,128)(2,1)}, u32[]{:S(2)}, u32[]{:S(2)}) collective-permute-start(bf16[4,2,48,384]{3,2,1,0:T(8,128)(2,1)S(1)} %collective-permute-done.5.refs_4_), channel_id=1, source_target_pairs={{0,2},{2,0},{4,6},{6,4},{8,10},{10,8},{12,14},{14,12},{16,18},{18,... | collective-permute-start | bytes 884744 | tf_op jit(solution)/shard_map/ppermute | solution.py:754
  61.0 14.3 %copy-start.24 = (bf16[4,2,48,384]{3,2,1,0:T(8,128)(2,1)}, bf16[4,2,48,384]{3,2,1,0:T(8,128)(2,1)S(1)}, u32[]{:S(2)}) copy-start(bf16[4,2,48,384]{3,2,1,0:T(8,128)(2,1)S(1)} %collective-permute-done.7.refs_6_) | copy-start | bytes 884740
  61.0 14.2 %collective-permute-start.14 = (bf16[4,2,48,384]{3,2,1,0:T(8,128)(2,1)S(1)}, bf16[4,2,48,384]{3,2,1,0:T(8,128)(2,1)}, u32[]{:S(2)}, u32[]{:S(2)}) collective-permute-start(bf16[4,2,48,384]{3,2,1,0:T(8,128)(2,1)S(1)} %collective-permute-done.6.refs_5_), channel_id=1, source_target_pairs={{0,2},{2,0},{4,6},{6,4},{8,10},{10,8},{12,14},{14,12},{16,18},{18,... | collective-permute-start | bytes 884744 | tf_op jit(solution)/shard_map/ppermute | solution.py:754
  72.3 2.9 %collective-permute-start.15 = (bf16[4,2,48,384]{3,2,1,0:T(8,128)(2,1)S(1)}, bf16[4,2,48,384]{3,2,1,0:T(8,128)(2,1)}, u32[]{:S(2)}, u32[]{:S(2)}) collective-permute-start(bf16[4,2,48,384]{3,2,1,0:T(8,128)(2,1)S(1)} %collective-permute-done.7.refs_6_), channel_id=1, source_target_pairs={{0,2},{2,0},{4,6},{6,4},{8,10},{10,8},{12,14},{14,12},{16,18},{18,... | collective-permute-start | bytes 884744 | tf_op jit(solution)/shard_map/ppermute | solution.py:754
  72.3 2.9 %collective-permute-start.16 = (bf16[4,2,48,384]{3,2,1,0:T(8,128)(2,1)S(1)}, bf16[4,2,48,384]{3,2,1,0:T(8,128)(2,1)}, u32[]{:S(2)}, u32[]{:S(2)}) collective-permute-start(bf16[4,2,48,384]{3,2,1,0:T(8,128)(2,1)S(1)} %collective-permute-done.8.refs_7_), channel_id=1, source_target_pairs={{0,2},{2,0},{4,6},{6,4},{8,10},{10,8},{12,14},{14,12},{16,18},{18,... | collective-permute-start | bytes 884744 | tf_op jit(solution)/shard_map/ppermute | solution.py:754
  126.3 88.8 %reduce-scatter.5.cloned.1.call-start = ((), (), s32[]{:S(2)}) async-start(), calls=%async_computation.3 | async-start | bytes 3686400 | tf_op jit(solution)/shard_map/reduce_scatter | solution.py:845
  135.2 20.1 %copy-start.9 = (f32[7,768]{1,0:T(8,128)S(1)}, f32[7,768]{1,0:T(8,128)}, u32[]{:S(2)}) copy-start(f32[7,768]{1,0:T(8,128)} %get-tuple-element.99) | copy-start | bytes 64516
  135.2 20.1 %copy-start.11 = (f32[3,768]{1,0:T(4,128)S(1)}, f32[3,768]{1,0:T(4,128)}, u32[]{:S(2)}) copy-start(f32[3,768]{1,0:T(4,128)} %get-tuple-element.100) | copy-start | bytes 27652
  156.0 12.9 %collective-permute-start.19 = (f32[12,768]{1,0:T(8,128)S(1)}, f32[12,768]{1,0:T(8,128)S(1)}, u32[]{:S(2)}, u32[]{:S(2)}) collective-permute-start(f32[12,768]{1,0:T(8,128)S(1)} %pad_maximum_fusion.2), channel_id=1, source_target_pairs={{0,24},{2,26},{4,28},{6,30},{8,0},{10,2},{12,4},{14,6},{16,8},{18,... | collective-permute-start | bytes 110600 | tf_op jit(solution)/shard_map/ppermute | solution.py:759
  157.9 11.0 %collective-permute-start.18 = (f32[12,768]{1,0:T(8,128)S(1)}, f32[12,768]{1,0:T(8,128)S(1)}, u32[]{:S(2)}, u32[]{:S(2)}) collective-permute-start(f32[12,768]{1,0:T(8,128)S(1)} %pad_maximum_fusion.2), channel_id=1, source_target_pairs={{0,16},{2,18},{4,20},{6,22},{8,24},{10,26},{12,28},{14,30},{16,0},... | collective-permute-start | bytes 110600 | tf_op jit(solution)/shard_map/ppermute | solution.py:759
  158.7 10.3 %collective-permute-start.17 = (f32[12,768]{1,0:T(8,128)S(1)}, f32[12,768]{1,0:T(8,128)S(1)}, u32[]{:S(2)}, u32[]{:S(2)}) collective-permute-start(f32[12,768]{1,0:T(8,128)S(1)} %pad_maximum_fusion.2), channel_id=1, source_target_pairs={{0,8},{2,10},{4,12},{6,14},{8,16},{10,18},{12,20},{14,22},{16,24},... | collective-permute-start | bytes 110600 | tf_op jit(solution)/shard_map/ppermute | solution.py:759
  169.0 5.7 %collective-permute-start.20 = (bf16[4,4,5,48,384]{4,3,2,1,0:T(8,128)(2,1)}, bf16[4,4,5,48,384]{4,3,2,1,0:T(8,128)(2,1)S(1)}, u32[]{:S(2)}, u32[]{:S(2)}) collective-permute-start(bf16[4,4,5,48,384]{4,3,2,1,0:T(8,128)(2,1)} %get-tuple-element.104), channel_id=1, source_target_pairs={{0,2},{2,0},{4,6},{6,4},{8,10},{10,8},{12,14},{14,12},{16,18},{18,... | collective-permute-start | bytes 8847368 | tf_op jit(solution)/shard_map/ppermute | solution.py:754
  181.2 18.5 %collective-permute-start.23 = (bf16[8,48,384]{2,1,0:T(8,128)(2,1)}, bf16[8,48,384]{2,1,0:T(8,128)(2,1)S(1)}, u32[]{:S(2)}, u32[]{:S(2)}) collective-permute-start(bf16[8,48,384]{2,1,0:T(8,128)(2,1)} %get-tuple-element.113), channel_id=1, source_target_pairs={{0,8},{2,10},{4,12},{6,14},{8,16},{10,18},{12,20},{14,22},{16,24},... | collective-permute-start | bytes 884744 | tf_op jit(solution)/shard_map/ppermute | solution.py:759
  183.2 21.9 %collective-permute-start.24 = (bf16[8,48,384]{2,1,0:T(8,128)(2,1)}, bf16[8,48,384]{2,1,0:T(8,128)(2,1)S(1)}, u32[]{:S(2)}, u32[]{:S(2)}) collective-permute-start(bf16[8,48,384]{2,1,0:T(8,128)(2,1)} %get-tuple-element.114), channel_id=1, source_target_pairs={{0,16},{2,18},{4,20},{6,22},{8,24},{10,26},{12,28},{14,30},{16,0},... | collective-permute-start | bytes 884744 | tf_op jit(solution)/shard_map/ppermute | solution.py:759
  184.8 20.2 %collective-permute-start.25 = (bf16[8,48,384]{2,1,0:T(8,128)(2,1)}, bf16[8,48,384]{2,1,0:T(8,128)(2,1)S(1)}, u32[]{:S(2)}, u32[]{:S(2)}) collective-permute-start(bf16[8,48,384]{2,1,0:T(8,128)(2,1)} %get-tuple-element.115), channel_id=1, source_target_pairs={{0,24},{2,26},{4,28},{6,30},{8,0},{10,2},{12,4},{14,6},{16,8},{18,... | collective-permute-start | bytes 884744 | tf_op jit(solution)/shard_map/ppermute | solution.py:759
  193.0 1.2 collective-permute-start.21
  194.3 5.4 %collective-permute-start.22 = (f32[12,768]{1,0:T(8,128)S(1)}, f32[12,768]{1,0:T(8,128)S(1)}, u32[]{:S(2)}, u32[]{:S(2)}) collective-permute-start(f32[12,768]{1,0:T(8,128)S(1)} %add.139), channel_id=1, source_target_pairs={{0,1},{1,0},{2,3},{3,2},{4,5},{5,4},{6,7},{7,6},{8,9},{9,8},{10,11... | collective-permute-start | bytes 110600 | tf_op jit(solution)/shard_map/ppermute | solution.py:750
  199.7 22.2 %copy-start.12 = (f32[6,768]{1,0:T(8,128)S(1)}, f32[6,768]{1,0:T(8,128)}, u32[]{:S(2)}) copy-start(f32[6,768]{1,0:T(8,128)} %nv_ref.3) | copy-start | bytes 55300
  199.7 22.2 %copy-start.13 = (f32[6,768]{1,0:T(8,128)S(1)}, f32[6,768]{1,0:T(8,128)}, u32[]{:S(2)}) copy-start(f32[6,768]{1,0:T(8,128)} %param.21) | copy-start | bytes 55300
  199.7 22.2 %copy-start.14 = (f32[6,768]{1,0:T(8,128)S(1)}, f32[6,768]{1,0:T(8,128)}, u32[]{:S(2)}) copy-start(f32[6,768]{1,0:T(8,128)} %param.22) | copy-start | bytes 55300
  205.1 5.4 %collective-permute-start.26 = (f32[12,768]{1,0:T(8,128)S(1)}, f32[12,768]{1,0:T(8,128)S(1)}, u32[]{:S(2)}, u32[]{:S(2)}) collective-permute-start(f32[12,768]{1,0:T(8,128)S(1)} %add.140), channel_id=1, source_target_pairs={{0,4},{2,6},{4,0},{6,2},{8,12},{10,14},{12,8},{14,10},{16,20},{18,... | collective-permute-start | bytes 110600 | tf_op jit(solution)/shard_map/ppermute | solution.py:754
  216.4 9.5 %collective-permute-start.27 = (bf16[5,48,384]{2,1,0:T(8,128)(2,1)S(1)}, bf16[5,48,384]{2,1,0:T(8,128)(2,1)S(1)}, u32[]{:S(2)}, u32[]{:S(2)}) collective-permute-start(bf16[5,48,384]{2,1,0:T(8,128)(2,1)S(1)} %get-tuple-element.145), channel_id=1, source_target_pairs={{0,8},{2,10},{4,12},{6,14},{8,16},{10,18},{12,20},{14,22},{16,24},... | collective-permute-start | bytes 552968 | tf_op jit(solution)/shard_map/ppermute | solution.py:759
  219.5 13.2 %collective-permute-start.28 = (bf16[5,48,384]{2,1,0:T(8,128)(2,1)S(1)}, bf16[5,48,384]{2,1,0:T(8,128)(2,1)S(1)}, u32[]{:S(2)}, u32[]{:S(2)}) collective-permute-start(bf16[5,48,384]{2,1,0:T(8,128)(2,1)S(1)} %get-tuple-element.144), channel_id=1, source_target_pairs={{0,16},{2,18},{4,20},{6,22},{8,24},{10,26},{12,28},{14,30},{16,0},... | collective-permute-start | bytes 552968 | tf_op jit(solution)/shard_map/ppermute | solution.py:759
  220.6 12.1 %collective-permute-start.29 = (bf16[5,48,384]{2,1,0:T(8,128)(2,1)S(1)}, bf16[5,48,384]{2,1,0:T(8,128)(2,1)S(1)}, u32[]{:S(2)}, u32[]{:S(2)}) collective-permute-start(bf16[5,48,384]{2,1,0:T(8,128)(2,1)S(1)} %get-tuple-element.143), channel_id=1, source_target_pairs={{0,24},{2,26},{4,28},{6,30},{8,0},{10,2},{12,4},{14,6},{16,8},{18,... | collective-permute-start | bytes 552968 | tf_op jit(solution)/shard_map/ppermute | solution.py:759
  (13 other events, 75.4 us)
Sparse Core Ops, SparseCore 0:
  10.2 91.6 all-gather.2
  126.4 52.2 reduce-scatter.2
  181.0 34.0 reduce-scatter.4
